TPU v7x, 128 devices: a whole 4x4x4 slice. The times are simulated.
128 devices in a mesh: space: 8 (over y_lo, z), vel: 16 (over y_hi, x, core).
Axes of the slice: x: 4, y: 4 (y_hi: 2, y_lo: 2; y = y_hi * 2 + y_lo), z: 4, core: 2. Of those that a mesh axis runs over, the one named last changes fastest.
Arguments:
- dist: float32 [128, 16, 16, 2048], P('space', None, None, 'vel'), may hold values from 0.05 to 2
- relax_rate: float32 [128, 16, 16], P('space'), may hold values from 0.2 to 0.9
- kinetic_cells: int32 [2, 32768], P(None, 'space'), may hold values from 0 to 4095, as said below
- kinetic_count: int32 [2, 8], replicated, may hold values from 1 to 4096, 16384 in all within a row
- map_a: bfloat16 [2048, 768], replicated, may hold values from -0.125 to 0.125
- map_b: bfloat16 [2048, 768], replicated, may hold values from -0.125 to 0.125
- map_c: bfloat16 [768, 2048], replicated, may hold values from -0.21875 to 0.21875
Outputs:
- dist_out: float32 [128, 16, 16, 2048], P('space', None, None, 'vel')
Inputs may be any that keep to these rules, and one draw needn't show every extreme that they name: `kinetic_cells`: for each step, the 4096 entries of a slab's block are a permutation of that slab's local cell numbers. `kinetic_count`: each step's counts sum to 16384, and one slab is kinetic in all its cells.
All inputs are finite; a program needn't handle non-finite values.
Results may differ from a plain program's by a relative error of at most 0.0034.
Values may be sent and summed in bfloat16 or wider, within the bound.
No kernel may reach another device: no remote copies, remote signals or barrier semaphores. Data moves between devices by JAX's collectives and lax.ppermute only.
A program may use at most 128 MiB of HBM per device.

v0:
```python
import jax
import jax.numpy as jnp
from jax import lax
from jax.sharding import PartitionSpec as P

GX = 16
GY = 16
GZ = 8
STEPS = 2


COURANT = 0.1
SPACING = 0.5
COLLIDE = 0.5


def padded_2(block, sides, width):
    for axis, dim in sides:
        count = lax.axis_size(axis)
        forward = [(i, i + 1) for i in range(count - 1)]
        forward.append((count - 1, 0))
        backward = [(target, source) for source, target in forward]
        low = lax.ppermute(
            lax.slice_in_dim(block, block.shape[dim] - width, None, axis=dim), axis, forward
        )
        high = lax.ppermute(lax.slice_in_dim(block, 0, width, axis=dim), axis, backward)
        block = jnp.concatenate([low, block, high], axis=dim)
    return block


def velocity_tables():
    grid_index = jnp.arange(GX * GY * GZ, dtype=jnp.int32)
    along_x = ((grid_index // (GY * GZ)).astype(jnp.float32) - 0.5 * (GX - 1)) * SPACING
    along_y = ((grid_index // GZ % GY).astype(jnp.float32) - 0.5 * (GY - 1)) * SPACING
    along_z = ((grid_index % GZ).astype(jnp.float32) - 0.5 * (GZ - 1)) * SPACING
    speed_sq = along_x * along_x + along_y * along_y + along_z * along_z
    weights = jnp.exp(-0.5 * speed_sq)
    weights = weights / jnp.sum(weights)
    moment_basis = jnp.stack([jnp.ones_like(along_x), along_x, along_y, along_z, speed_sq])
    consts = (
        jnp.sum(weights * along_x * along_x),
        jnp.sum(weights * along_y * along_y),
        jnp.sum(weights * along_z * along_z),
        jnp.sum(weights * speed_sq),
        jnp.sum(weights * speed_sq * speed_sq),
    )
    return (moment_basis, moment_basis * weights[None, :], consts)


def coefficients(moments, consts):
    thermal = (moments[4] - consts[3] * moments[0]) / (consts[4] - consts[3] * consts[3])
    return jnp.stack(
        [
            moments[0] - consts[3] * thermal,
            moments[1] / consts[0],
            moments[2] / consts[1],
            moments[3] / consts[2],
            thermal,
        ]
    )


def limited_slope(first_diff, second_diff):
    return (
        0.5
        * (jnp.sign(first_diff) + jnp.sign(second_diff))
        * jnp.minimum(jnp.abs(first_diff), jnp.abs(second_diff))
    )


def face_flux(padded, velocity, direction):
    extent = padded.shape[direction] - 4

    def window(array, offset, amount):
        return lax.slice_in_dim(array, offset, offset + amount, axis=direction)

    diffs = window(padded, 1, extent + 3) - window(padded, 0, extent + 3)
    left_state = window(padded, 1, extent + 1) + 0.5 * limited_slope(
        window(diffs, 0, extent + 1), window(diffs, 1, extent + 1)
    )
    right_state = window(padded, 2, extent + 1) - 0.5 * limited_slope(
        window(diffs, 1, extent + 1), window(diffs, 2, extent + 1)
    )
    fluxes = jnp.maximum(velocity, 0.0) * left_state + jnp.minimum(velocity, 0.0) * right_state
    return window(fluxes, 1, extent) - window(fluxes, 0, extent)


def periodic_pad(current, direction):
    extent = current.shape[direction]
    return jnp.concatenate(
        [
            lax.slice_in_dim(current, extent - 2, extent, axis=direction),
            current,
            lax.slice_in_dim(current, 0, 2, axis=direction),
        ],
        axis=direction,
    )


def transport(padded, current, speed_x, speed_y, speed_z):
    change = face_flux(padded, speed_x, 0) + face_flux(periodic_pad(current, 1), speed_y, 1)
    change = change + face_flux(periodic_pad(current, 2), speed_z, 2)
    return current - COURANT * change


def body(dist, relax_rate, kinetic_cells, kinetic_count, map_a, map_b, map_c):
    vel_width = dist.shape[3]
    groups = lax.axis_size("vel")
    rank_vel = lax.axis_index("vel")
    rank_space = lax.axis_index("space")
    moment_basis, weighted, consts = velocity_tables()
    local_basis = lax.dynamic_slice_in_dim(moment_basis, rank_vel * vel_width, vel_width, 1)
    local_weighted = lax.dynamic_slice_in_dim(weighted, rank_vel * vel_width, vel_width, 1)
    cell_count = dist.shape[0] * dist.shape[1] * dist.shape[2]
    relax_rows = relax_rate.reshape(cell_count, 1)
    current = dist
    for step_index in range(STEPS):
        padded = padded_2(current, (("space", 0),), 2)
        advected = transport(padded, current, local_basis[1], local_basis[2], local_basis[3])
        flat_rows = advected.reshape(cell_count, vel_width)
        partial_value = jnp.einsum(
            "mv,cv->mc", local_basis, flat_rows, precision=lax.Precision.HIGHEST
        )
        totals = lax.psum(partial_value, "vel")
        coeffs = coefficients(totals, consts)
        equilibrium = jnp.einsum(
            "mc,mv->cv", coeffs, local_weighted, precision=lax.Precision.HIGHEST
        )
        relaxed = flat_rows + relax_rows * (equilibrium - flat_rows)
        kin_order = kinetic_cells[step_index]
        slab_counts = kinetic_count[step_index]
        own_count = lax.dynamic_index_in_dim(slab_counts, rank_space, 0, False)
        position = jnp.arange(cell_count, dtype=jnp.int32)
        is_live = position < own_count
        kin_rows = flat_rows[kin_order]
        outgoing = kin_rows.astype(jnp.bfloat16)
        buffer = outgoing.reshape(groups, cell_count // groups, vel_width)
        row_block = lax.all_to_all(buffer, "vel", split_axis=0, concat_axis=2, tiled=True)[0]
        first_map = jnp.dot(row_block, map_a, preferred_element_type=jnp.float32)
        second_map = jnp.dot(row_block, map_b, preferred_element_type=jnp.float32)
        hidden = (first_map * second_map).astype(jnp.bfloat16)
        product = jnp.dot(hidden, map_c, preferred_element_type=jnp.float32).astype(jnp.bfloat16)
        returned = lax.all_to_all(product[None], "vel", split_axis=2, concat_axis=0, tiled=True)
        collided = returned.reshape(cell_count, vel_width)
        kinetic = kin_rows + COLLIDE * collided.astype(jnp.float32)
        new_rows = jnp.where(is_live[:, None], kinetic, relaxed[kin_order])
        result = relaxed.at[kin_order].set(new_rows)
        current = result.reshape(dist.shape)
    return current


def solution(mesh):
    return jax.shard_map(
        body,
        mesh=mesh,
        in_specs=(
            P("space", None, None, "vel"),
            P("space", None, None),
            P(None, "space"),
            P(),
            P(),
            P(),
            P(),
        ),
        out_specs=P("space", None, None, "vel"),
        check_vma=False,
    )
```

profile of v0, /device:TPU:1, one launch (start us, length us, event | category | flops | bytes accessed | tf_op | source)
XLA Modules:
  0.0 545.8 jit_solution(13775078447263442646)
XLA Ops:
  8.6 5.6 %collective-permute-start.1 = (f32[2,16,16,128]{3,2,1,0:T(8,128)}, f32[2,16,16,128]{3,2,1,0:T(8,128)}, u32[]{:S(2)}, u32[]{:S(2)}) collective-permute-start(f32[2,16,16,128]{3,2,1,0:T(8,128)} %get-tuple-element.16), channel_id=1, source_target_pairs={{16,0},{32,16},{48,32},{64,48},{80,64},{96,80},{112,96},{0,112},{1... | collective-permute-start | bytes 786440 | tf_op jit(solution)/shard_map/ppermute | solution.py:26
  40.0 15.8 %gather_fusion = f32[4096,128]{1,0:T(8,128)} fusion(f32[4096,128]{1,0:T(8,128)} %bitcast.87, s32[4096]{0:T(1024)S(1)} %broadcast_clamp_fusion.1), kind=kCustom, calls=%fused_computation | custom fusion | bytes 4210688 | tf_op jit(solution)/shard_map/gather | solution.py:135
  60.7 7.6 %all-to-all-start = ((bf16[16,256,128]{1,2,0:T(8,128)(2,1)}), bf16[16,256,128]{1,2,0:T(8,128)(2,1)}, u32[]{:S(2)}, u32[]{:S(2)}) async-start(bf16[16,256,128]{1,2,0:T(8,128)(2,1)} %copy.14), calls=%async_computation | async-start | bytes 2097152 | tf_op jit(solution)/shard_map/all_to_all | solution.py:138
  89.9 5.6 %fusion.14 = bf16[1,256,2048]{2,1,0:T(8,128)(2,1)} fusion(bf16[768,2048]{1,0:T(8,128)(2,1)S(1)} %copy-done, f32[256,768]{1,0:T(8,128)} %fusion.102, bf16[256,2048]{0,1:T(8,128)(2,1)} %bitcast.13, bf16[2048,768]{1,0:T(8,128)(2,1)} %param.12), kind=kOutput, calls=%fused_computation.39 | convolution fusion | flops 1611530240 | bytes 9175040 | tf_op jit(solution)/shard_map/dot_general | solution.py:142
  95.5 5.9 %copy.15 = bf16[1,256,2048]{1,0,2:T(2,128)(2,1)} copy(bf16[1,256,2048]{2,1,0:T(8,128)(2,1)} %fusion.14) | data formatting | bytes 2097152 | tf_op jit(solution)/shard_map/broadcast_in_dim | solution.py:143
  101.9 12.6 %reduce = bf16[2048,256]{1,0:T(8,128)(2,1)} reduce(bf16[2048,1,256]{2,1,0:T(2,128)(2,1)} %bitcast.93, bf16[]{:T(256)} %broadcast.660), dimensions={1}, to_apply=%bitcast.56.reduce_sub_computation | reduce | bytes 2097154
  122.0 99.7 %all-reduce.3.cloned.1.call-done = f32[5,4096]{1,0:T(8,128)} async-done(((f32[5,4096]{1,0:T(8,128)}), f32[5,4096]{1,0:T(8,128)}) %all-reduce.3.cloned.1.call-update) | async-done | bytes 81936 | tf_op jit(solution)/shard_map/psum | solution.py:124
  225.7 6.2 %fusion.3 = f32[4096,128]{1,0:T(8,128)} fusion(f32[4096,128]{1,0:T(8,128)} %bitcast.89, f32[5,4096]{1,0:T(8,128)S(1)} %stack.7, f32[4096]{0:T(1024)S(1)} %mul.515, f32[5,128]{1,0:T(8,128)S(1)} %constant_dynamic-slice_fusion.2, f32[128]{0:T(128)S(1)} %dynamic-slice.2), kind=kOutput, calls=%fused_computation.11 | convolution fusion | flops 33030784 | bytes 4295680 | tf_op jit(solution)/shard_map/mc,mv->cv/dot_general | solution.py:126
  231.9 15.7 %gather_fusion.1 = f32[4096,128]{1,0:T(8,128)} fusion(f32[4096,128]{1,0:T(8,128)} %fusion.3, s32[4096]{0:T(1024)S(1)} %broadcast_clamp_fusion.1), kind=kCustom, calls=%fused_computation.1 | custom fusion | bytes 4210688 | tf_op jit(solution)/shard_map/gather | solution.py:146
  247.6 5.8 %reshape.361 = bf16[2048,1,256]{2,1,0:T(2,128)(2,1)} reshape(bf16[16,2,16384]{2,1,0:T(2,128)(2,1)} %all-to-all-done.1) | data formatting | bytes 2097152
  258.3 6.0 %copy.16 = f32[1,256,16,128]{3,1,2,0:T(8,128)} copy(f32[1,256,16,128]{1,0,3,2:T(1,128)} %bitcast.95) | data formatting | bytes 4194304 | tf_op jit(solution)/shard_map/mul | solution.py:145
  268.5 13.8 %scatter_fusion = f32[4096,128]{1,0:T(8,128)} fusion(f32[4096,128]{1,0:T(8,128)} %fusion.3, s32[4096]{0:T(1024)S(1)} %bitcast.104, f32[4096,128]{1,0:T(8,128)} %fusion.45), kind=kCustom, calls=%fused_computation.4 | custom fusion | bytes 6307840 | tf_op jit(solution)/shard_map/scatter | solution.py:147
  308.2 15.8 %gather_fusion.2 = f32[4096,128]{1,0:T(8,128)} fusion(f32[4096,128]{1,0:T(8,128)} %bitcast.90, s32[4096]{0:T(1024)S(1)} %broadcast_clamp_fusion), kind=kCustom, calls=%fused_computation.2 | custom fusion | bytes 4210688 | tf_op jit(solution)/shard_map/gather | solution.py:135
  328.9 6.6 %all-to-all-start.2 = ((bf16[16,256,128]{1,2,0:T(8,128)(2,1)}), bf16[16,256,128]{1,2,0:T(8,128)(2,1)}, u32[]{:S(2)}, u32[]{:S(2)}) async-start(bf16[16,256,128]{1,2,0:T(8,128)(2,1)} %copy.17), calls=%async_computation.2 | async-start | bytes 2097152 | tf_op jit(solution)/shard_map/all_to_all | solution.py:138
  340.2 12.8 %all-to-all-done.2 = bf16[16,256,128]{1,2,0:T(8,128)(2,1)} async-done(((bf16[16,256,128]{1,2,0:T(8,128)(2,1)}), bf16[16,256,128]{1,2,0:T(8,128)(2,1)}, u32[]{:S(2)}, u32[]{:S(2)}) %all-to-all-start.2) | async-done | bytes 1048608 | tf_op jit(solution)/shard_map/all_to_all | solution.py:138
  357.1 5.6 %fusion.15 = bf16[1,256,2048]{2,1,0:T(8,128)(2,1)} fusion(bf16[768,2048]{1,0:T(8,128)(2,1)S(1)} %copy-done, f32[256,768]{1,0:T(8,128)} %fusion.104, bf16[256,2048]{0,1:T(8,128)(2,1)} %bitcast.30, bf16[2048,768]{1,0:T(8,128)(2,1)} %param.12), kind=kOutput, calls=%fused_computation.40 | convolution fusion | flops 1611530240 | bytes 9175040 | tf_op jit(solution)/shard_map/dot_general | solution.py:142
  362.7 5.9 %copy.18 = bf16[1,256,2048]{1,0,2:T(2,128)(2,1)} copy(bf16[1,256,2048]{2,1,0:T(8,128)(2,1)} %fusion.15) | data formatting | bytes 2097152 | tf_op jit(solution)/shard_map/broadcast_in_dim | solution.py:143
  368.6 12.6 %reduce.1 = bf16[2048,256]{1,0:T(8,128)(2,1)} reduce(bf16[2048,1,256]{2,1,0:T(2,128)(2,1)} %bitcast.94, bf16[]{:T(256)} %broadcast.660), dimensions={1}, to_apply=%bitcast.58.reduce_sub_computation | reduce | bytes 2097154
  388.3 89.9 %all-reduce.5.cloned.1.call-done = f32[5,4096]{1,0:T(8,128)} async-done(((f32[5,4096]{1,0:T(8,128)}), f32[5,4096]{1,0:T(8,128)}) %all-reduce.5.cloned.1.call-update) | async-done | bytes 81936 | tf_op jit(solution)/shard_map/psum | solution.py:124
  482.3 6.2 %fusion.1 = f32[4096,128]{1,0:T(8,128)} fusion(f32[4096,128]{1,0:T(8,128)} %bitcast.92, f32[5,4096]{1,0:T(8,128)S(1)} %stack.8, f32[4096]{0:T(1024)S(1)} %mul.515, f32[5,128]{1,0:T(8,128)S(1)} %constant_dynamic-slice_fusion.2, f32[128]{0:T(128)S(1)} %dynamic-slice.2), kind=kOutput, calls=%fused_computation.8 | convolution fusion | flops 33030784 | bytes 4295680 | tf_op jit(solution)/shard_map/mc,mv->cv/dot_general | solution.py:126
  488.4 15.7 %gather_fusion.3 = f32[4096,128]{1,0:T(8,128)} fusion(f32[4096,128]{1,0:T(8,128)} %fusion.1, s32[4096]{0:T(1024)S(1)} %broadcast_clamp_fusion), kind=kCustom, calls=%fused_computation.3 | custom fusion | bytes 4210688 | tf_op jit(solution)/shard_map/gather | solution.py:146
  504.2 5.8 %reshape.363 = bf16[2048,1,256]{2,1,0:T(2,128)(2,1)} reshape(bf16[16,2,16384]{2,1,0:T(2,128)(2,1)} %all-to-all-done.3) | data formatting | bytes 2097152
  514.8 6.0 %copy.19 = f32[1,256,16,128]{3,1,2,0:T(8,128)} copy(f32[1,256,16,128]{1,0,3,2:T(1,128)} %bitcast.96) | data formatting | bytes 4194304 | tf_op jit(solution)/shard_map/mul | solution.py:145
  525.0 13.8 %scatter_fusion.1 = f32[4096,128]{1,0:T(8,128)} fusion(f32[4096,128]{1,0:T(8,128)} %fusion.1, s32[4096]{0:T(1024)S(1)} %bitcast.102, f32[4096,128]{1,0:T(8,128)} %fusion.44), kind=kCustom, calls=%fused_computation.5 | custom fusion | bytes 6307840 | tf_op jit(solution)/shard_map/scatter | solution.py:147
  (107 shorter events, 132.9 us)
Async XLA Ops:
  6.5 83.3 %copy-start = (bf16[768,2048]{1,0:T(8,128)(2,1)S(1)}, bf16[768,2048]{1,0:T(8,128)(2,1)}, u32[]{:S(2)}) copy-start(bf16[768,2048]{1,0:T(8,128)(2,1)} %param.13) | copy-start | bytes 9437188
  6.5 9.5 %copy-start.2 = (f32[16,16,16,128]{3,2,1,0:T(8,128)S(1)}, f32[16,16,16,128]{3,2,1,0:T(8,128)}, u32[]{:S(2)}) copy-start(f32[16,16,16,128]{3,2,1,0:T(8,128)} %param.7) | copy-start | bytes 6291460
  8.6 24.4 %collective-permute-start.1 = (f32[2,16,16,128]{3,2,1,0:T(8,128)}, f32[2,16,16,128]{3,2,1,0:T(8,128)}, u32[]{:S(2)}, u32[]{:S(2)}) collective-permute-start(f32[2,16,16,128]{3,2,1,0:T(8,128)} %get-tuple-element.16), channel_id=1, source_target_pairs={{16,0},{32,16},{48,32},{64,48},{80,64},{96,80},{112,96},{0,112},{1... | collective-permute-start | bytes 786440 | tf_op jit(solution)/shard_map/ppermute | solution.py:26
  14.2 17.6 %collective-permute-start = (f32[2,16,16,128]{3,2,1,0:T(8,128)}, f32[2,16,16,128]{3,2,1,0:T(8,128)}, u32[]{:S(2)}, u32[]{:S(2)}) collective-permute-start(f32[2,16,16,128]{3,2,1,0:T(8,128)} %get-tuple-element.15), channel_id=1, source_target_pairs={{0,16},{16,32},{32,48},{48,64},{64,80},{80,96},{96,112},{112,0},{1... | collective-permute-start | bytes 786440 | tf_op jit(solution)/shard_map/ppermute | solution.py:23
  15.9 1.0 copy-start.5
  21.5 0.8 copy-start.10
  21.5 1.6 copy-start.3
  21.5 2.5 copy-start.4
  21.5 2.5 copy-start.6
  24.0 4.8 copy-start.7
  24.0 4.8 copy-start.8
  58.4 13.6 %copy-start.9 = (f32[16,16,16]{2,1,0:T(8,128)S(1)}, f32[16,16,16]{2,1,0:T(8,128)}, u32[]{:S(2)}) copy-start(f32[16,16,16]{2,1,0:T(8,128)} %param.8) | copy-start | bytes 49156
  58.4 16.6 %copy-start.11 = (s32[2,8]{1,0:T(2,128)S(1)}, s32[2,8]{1,0:T(2,128)}, u32[]{:S(2)}) copy-start(s32[2,8]{1,0:T(2,128)} %param.10) | copy-start | bytes 196
  60.7 25.1 %all-to-all-start = ((bf16[16,256,128]{1,2,0:T(8,128)(2,1)}), bf16[16,256,128]{1,2,0:T(8,128)(2,1)}, u32[]{:S(2)}, u32[]{:S(2)}) async-start(bf16[16,256,128]{1,2,0:T(8,128)(2,1)} %copy.14), calls=%async_computation | async-start | bytes 2097152 | tf_op jit(solution)/shard_map/all_to_all | solution.py:138
  68.3 153.4 %all-reduce.3.cloned.1.call-start = ((), (), s32[]{:S(2)}) async-start(), calls=%async_computation.4 | async-start | bytes 262144 | tf_op jit(solution)/shard_map/psum | solution.py:124
  116.6 131.0 %all-to-all-start.1 = ((bf16[16,2,16384]{2,1,0:T(2,128)(2,1)}), bf16[16,2,16384]{2,1,0:T(2,128)(2,1)}, u32[]{:S(2)}, u32[]{:S(2)}) async-start(bf16[16,2,16384]{2,1,0:T(2,128)(2,1)} %reshape.360), calls=%async_computation.1 | async-start | bytes 2097152 | tf_op jit(solution)/shard_map/all_to_all | solution.py:143
  282.2 3.0 copy-start.1
  291.5 7.4 %collective-permute-start.3 = (f32[2,16,16,128]{3,2,1,0:T(8,128)S(1)}, f32[2,16,16,128]{3,2,1,0:T(8,128)S(1)}, u32[]{:S(2)}, u32[]{:S(2)}) collective-permute-start(f32[2,16,16,128]{3,2,1,0:T(8,128)S(1)} %bitcast.100), channel_id=1, source_target_pairs={{16,0},{32,16},{48,32},{64,48},{80,64},{96,80},{112,96},{0,112},{1... | collective-permute-start | bytes 786440 | tf_op jit(solution)/shard_map/ppermute | solution.py:26
  294.2 8.6 %collective-permute-start.2 = (f32[2,16,16,128]{3,2,1,0:T(8,128)S(1)}, f32[2,16,16,128]{3,2,1,0:T(8,128)S(1)}, u32[]{:S(2)}, u32[]{:S(2)}) collective-permute-start(f32[2,16,16,128]{3,2,1,0:T(8,128)S(1)} %bitcast.99), channel_id=1, source_target_pairs={{0,16},{16,32},{32,48},{48,64},{64,80},{80,96},{96,112},{112,0},{1... | collective-permute-start | bytes 786440 | tf_op jit(solution)/shard_map/ppermute | solution.py:23
  328.9 24.1 %all-to-all-start.2 = ((bf16[16,256,128]{1,2,0:T(8,128)(2,1)}), bf16[16,256,128]{1,2,0:T(8,128)(2,1)}, u32[]{:S(2)}, u32[]{:S(2)}) async-start(bf16[16,256,128]{1,2,0:T(8,128)(2,1)} %copy.17), calls=%async_computation.2 | async-start | bytes 2097152 | tf_op jit(solution)/shard_map/all_to_all | solution.py:138
  335.5 142.7 %all-reduce.5.cloned.1.call-start = ((), (), s32[]{:S(2)}) async-start(), calls=%async_computation.5 | async-start | bytes 262144 | tf_op jit(solution)/shard_map/psum | solution.py:124
  383.3 120.9 %all-to-all-start.3 = ((bf16[16,2,16384]{2,1,0:T(2,128)(2,1)}), bf16[16,2,16384]{2,1,0:T(2,128)(2,1)}, u32[]{:S(2)}, u32[]{:S(2)}) async-start(bf16[16,2,16384]{2,1,0:T(2,128)(2,1)} %reshape.362), calls=%async_computation.3 | async-start | bytes 2097152 | tf_op jit(solution)/shard_map/all_to_all | solution.py:143
Sparse Core Ops, SparseCore 0:
  81.9 139.7 all-reduce.2
  340.3 137.8 all-reduce.4
where the time goes:
time: 556 us; the launch traced here: 546 us
  waiting for transfers between devices  212 us (38%)
  local copies, waits for them, and re-layouts  149 us (27%)
  other arithmetic  96.1 us (17%)
  matrix products  39.9 us (7%)
  starting transfers between devices  33.4 us (6%)
  between operations  16.1 us (3%)
    psum x2, waiting for transfers between devices, body(): totals = lax.psum(partial_value, 'vel')  190 us
    gather x2, local copies, waits for them, and re-layouts, body(): kin_rows = flat_rows[kin_order]  31.5 us
    gather x2, local copies, waits for them, and re-layouts, body(): new_rows = jnp.where(is_live[:, None], kinetic, relaxed[kin_order])  31.5 us
    scatter x2, local copies, waits for them, and re-layouts, body(): result = relaxed.at[kin_order].set(new_rows)  27.5 us
    unnamed x2, other arithmetic  25.2 us
    add x6, other arithmetic, face_flux(): jnp.maximum(velocity, 0.0) * left_state  22 us
    unnamed x31, local copies, waits for them, and re-layouts  19.8 us
    all_to_all x2, waiting for transfers between devices, body(): lax.all_to_all(buffer, 'vel', split_axis=0, concat_axis=2, tiled=True)[0]  16.8 us
  transfers between devices with their start and end apart: 10, of which 6 were waited for; matrix products, arithmetic and copies ran while one was open for 27% of the time, Pallas kernels for 0%

commit v1 on v0

v1 whole, which is shorter than its diff:
```python
import jax
import jax.numpy as jnp
import numpy as np
from jax import lax
from jax.experimental import pallas as pl
from jax.experimental.pallas import tpu as pltpu
from jax.sharding import PartitionSpec as P

GX = 16
GY = 16
GZ = 8
NV = GX * GY * GZ
RANK = 768
COURANT = 0.1
SPACING = 0.5
COLLIDE = 0.5

CX = 16
NY = 16
NZ = 16
LAYER = NY * NZ
WIDTH = 128
GROUPS = NV // WIDTH
OFFSET = 3.0 / 16.0
BX = 4
BY = 4
LINE = BX * NZ
LIMIT = 12 << 20


def tables():
    k = np.arange(NV)
    vx = ((k // (GY * GZ)) - 0.5 * (GX - 1)) * SPACING
    vy = ((k // GZ % GY) - 0.5 * (GY - 1)) * SPACING
    vz = ((k % GZ) - 0.5 * (GZ - 1)) * SPACING
    s = vx * vx + vy * vy + vz * vz
    w = np.exp(-0.5 * s)
    w = w / w.sum()
    sx, sy, sz = (w * vx * vx).sum(), (w * vy * vy).sum(), (w * vz * vz).sum()
    m2, m4 = (w * s).sum(), (w * s * s).sum()
    basis = np.stack([np.ones(NV), vx, vy, vz, s - OFFSET])
    q = np.zeros((5, 5))
    scale = 1.0 / (m4 - m2 * m2)
    thermal = np.zeros(5)
    thermal[0] = (OFFSET - m2) * scale
    thermal[4] = scale
    q[:, 4] = thermal
    q[:, 0] = (OFFSET - m2) * thermal
    q[0, 0] += 1.0
    q[1, 1], q[2, 2], q[3, 3] = 1.0 / sx, 1.0 / sy, 1.0 / sz
    project = np.zeros((NV, 128))
    project[:, :5] = basis.T
    mix = np.zeros((128, 128))
    expand = np.zeros((128, NV))
    for part in range(3):
        mix[:5, 8 * part : 8 * part + 5] = q
        expand[8 * part : 8 * part + 5] = basis
    return (
        project.astype(jnp.bfloat16),
        mix.astype(np.float32),
        expand.astype(jnp.bfloat16),
        w.reshape(1, NV).astype(np.float32),
        (COURANT * np.stack([vy[:WIDTH], vz[:WIDTH]])).astype(np.float32),
    )


def minmod_half(a, b):
    return 0.5 * (jnp.maximum(jnp.minimum(a, b), 0.0) + jnp.minimum(jnp.maximum(a, b), 0.0))


def call(kernel, name, operands, outs, spaces=None, scratch=(), flops=0, limit=8 << 20):
    vmem = pl.BlockSpec(memory_space=pltpu.VMEM)
    smem = pl.BlockSpec(memory_space=pltpu.SMEM)
    scalars = spaces or 0
    moved = sum(o.size * o.dtype.itemsize for o in operands) + sum(
        o.size * o.dtype.itemsize for o in outs
    )
    return pl.pallas_call(
        kernel,
        out_shape=tuple(outs),
        in_specs=[smem] * scalars + [vmem] * (len(operands) - scalars),
        out_specs=tuple(vmem for _ in outs),
        scratch_shapes=list(scratch),
        compiler_params=pltpu.CompilerParams(vmem_limit_bytes=limit),
        cost_estimate=pl.CostEstimate(flops=flops, bytes_accessed=moved, transcendentals=0),
        name=name,
    )(*operands)


def flux_change_z(f, uz, z_up):
    dz = pltpu.roll(f, NZ - 1, 0) - f
    slope = minmod_half(pltpu.roll(dz, 1, 0), dz)
    down = pltpu.roll(f - slope, NZ - 1, 0)
    flux = jnp.where(z_up, f + slope, down)
    return uz * (flux - pltpu.roll(flux, 1, 0))


def edges(before, here, after):
    slope = minmod_half(here - before, after - here)
    return here + slope, here - slope


def upwind_face(before, here, after):
    return here + minmod_half(here - before, after - here)


def first_yz_kernel(f_ref, u_ref, part_ref):
    uy = jnp.broadcast_to(u_ref[0:1], (NZ, WIDTH))
    uz = jnp.broadcast_to(u_ref[1:2], (NZ, WIDTH))
    y_up = uy > 0.0
    z_up = uz > 0.0

    def layer(x, carry):
        def at(y):
            return f_ref[x, y % NY]

        up, _ = edges(at(-2), at(-1), at(0))
        next_up, next_down = edges(at(-1), at(0), at(1))
        flux_before = jnp.where(y_up, up, next_down)
        for y in range(NY):
            up = next_up
            next_up, next_down = edges(at(y), at(y + 1), at(y + 2))
            flux = jnp.where(y_up, up, next_down)
            here = at(y)
            part_ref[x, y] = here - uy * (flux - flux_before) - flux_change_z(here, uz, z_up)
            flux_before = flux
        return carry

    lax.fori_loop(0, CX, layer, 0)


def first_x_kernel(sign_ref, speed_ref, f_ref, part_ref, behind_ref, ahead_ref, rows_ref):
    s = sign_ref[0]
    ux = speed_ref[0]
    forward = s > 0

    def line(y, carry):
        quarter = y // BY
        high = quarter // 2
        core = (quarter + high) % 2
        target = high * (GROUPS // 2) + core
        inner = (y % BY) * NZ

        def at(k):
            if k == -2:
                return behind_ref[jnp.where(forward, 0, 1), y].astype(jnp.float32)
            if k == -1:
                return behind_ref[jnp.where(forward, 1, 0), y].astype(jnp.float32)
            if k == CX:
                return ahead_ref[0, y].astype(jnp.float32)
            return f_ref[jnp.where(forward, k, CX - 1 - k), y]

        face_before = upwind_face(at(-2), at(-1), at(0))
        for k in range(CX):
            x = jnp.where(forward, k, CX - 1 - k)
            face = upwind_face(at(k - 1), at(k), at(k + 1))
            result = part_ref[x, y] - ux * (face - face_before)
            face_before = face
            start = pl.multiple_of((x % BX) * LINE + inner, NZ)
            rows_ref[target + (x // BX) * 2, pl.ds(start, NZ), :] = result.astype(jnp.bfloat16)
        return carry

    lax.fori_loop(0, NY, line, 0)


def collision_terms(
    rows, a_ref, b_ref, c_ref, project_ref, mix_ref, expand_ref, w_ref, hidden_ref
):
    moments = jnp.dot(rows, project_ref[...], preferred_element_type=jnp.float32)
    coeffs = jnp.dot(
        moments, mix_ref[...], precision=lax.Precision.HIGHEST, preferred_element_type=jnp.float32
    )
    lane = lax.broadcasted_iota(jnp.int32, coeffs.shape, 1)
    high = coeffs.astype(jnp.bfloat16).astype(jnp.float32)
    rest = coeffs - high
    middle = rest.astype(jnp.bfloat16).astype(jnp.float32)
    split = jnp.where(lane < 8, high, jnp.where(lane < 16, middle, rest - middle))
    split = split.astype(jnp.bfloat16)
    for n in range(RANK // 256):
        cols = slice(256 * n, 256 * (n + 1))
        first = jnp.dot(rows, a_ref[:, cols], preferred_element_type=jnp.float32)
        second = jnp.dot(rows, b_ref[:, cols], preferred_element_type=jnp.float32)
        hidden_ref[:, cols] = (first * second).astype(jnp.bfloat16)
    hidden = hidden_ref[...]
    for n in range(NV // 256):
        cols = slice(256 * n, 256 * (n + 1))
        collision = jnp.dot(hidden, c_ref[:, cols], preferred_element_type=jnp.float32)
        collision = collision.astype(jnp.bfloat16).astype(jnp.float32)
        poly = jnp.dot(split, expand_ref[:, cols], preferred_element_type=jnp.float32)
        equilibrium = poly * w_ref[:, cols]
        for half in range(2):
            part = slice(WIDTH * half, WIDTH * (half + 1))
            yield 2 * n + half, collision[:, part], equilibrium[:, part]


def first_collide_kernel(
    rows_ref, a_ref, b_ref, c_ref, project_ref, mix_ref, expand_ref, w_ref, rate_ref, mask_ref,
    f_ref, x_up_ref, x_down_ref, y_up_ref, y_down_ref, hidden_ref,
):
    rows = jnp.concatenate([rows_ref[g] for g in range(GROUPS)], axis=1)
    rate = jnp.broadcast_to(rate_ref[...], (LAYER, WIDTH))
    kinetic = jnp.broadcast_to(mask_ref[...], (LAYER, WIDTH)) > 0.0
    half = GROUPS // 2
    for g, collision, equilibrium in collision_terms(
        rows, a_ref, b_ref, c_ref, project_ref, mix_ref, expand_ref, w_ref, hidden_ref
    ):
        moved = rows_ref[g].astype(jnp.float32)
        change = jnp.where(kinetic, COLLIDE * collision, rate * (equilibrium - moved))
        result = moved + change
        f_ref[g] = result
        sent = result.astype(jnp.bfloat16)
        x_up_ref[g] = sent[3 * LINE : 4 * LINE]
        x_down_ref[g] = sent[0:LINE]
        if g >= half:
            x_up_ref[g + half] = sent[2 * LINE : 3 * LINE]
        else:
            x_down_ref[g + GROUPS] = sent[LINE : 2 * LINE]
        for x in range(BX):
            here = slice(NZ * x, NZ * (x + 1))
            y_down_ref[g, here] = sent[LINE * x : LINE * x + NZ]
            y_up_ref[g, here] = sent[LINE * x + 3 * NZ : LINE * x + 4 * NZ]
    low_lane = lax.broadcasted_iota(jnp.int32, (NZ, WIDTH), 1) < WIDTH // 2
    for g in range(half):
        for x in range(BX):
            here = slice(NZ * x, NZ * (x + 1))
            second = slice(LINE * x + NZ, LINE * x + 2 * NZ)
            third = slice(LINE * x + 2 * NZ, LINE * x + 3 * NZ)
            y_up_ref[GROUPS + g, here] = jnp.where(
                low_lane,
                pltpu.roll(f_ref[g, third], WIDTH // 2, 1),
                f_ref[g + half, third],
            ).astype(jnp.bfloat16)
            y_down_ref[GROUPS + g, here] = jnp.where(
                low_lane,
                f_ref[g, second],
                pltpu.roll(f_ref[g + half, second], WIDTH // 2, 1),
            ).astype(jnp.bfloat16)


def second_z_kernel(f_ref, u_ref, part_ref):
    uz = jnp.broadcast_to(u_ref[1:2], (NZ, WIDTH))
    z_up = uz > 0.0

    def group(g, carry):
        for c in range(BX * BY):
            here = slice(NZ * c, NZ * (c + 1))
            f = f_ref[g, here]
            part_ref[g, here] = f - flux_change_z(f, uz, z_up)
        return carry

    lax.fori_loop(0, GROUPS, group, 0)


def second_xy_kernel(
    f_ref, part_ref, x_below_ref, x_above_ref, y_below_ref, y_above_ref, u_ref,
    moved_ref,
):
    uy = jnp.broadcast_to(u_ref[0:1], (NZ, WIDTH))
    y_up = uy > 0.0
    half = GROUPS // 2

    def wide(ref, g, i):
        return ref[g, NZ * i : NZ * (i + 1)].astype(jnp.float32)

    def group(pair, upward):
        g = pair + half if upward else pair
        extra = pair + GROUPS
        ux = (g.astype(jnp.float32) - 0.5 * (GX - 1)) * (SPACING * COURANT)
        ux = ux if upward else -ux
        for y in range(BY):
            behind, ahead = (x_below_ref, x_above_ref) if upward else (x_above_ref, x_below_ref)

            def at_x(k):
                if k == -2:
                    return wide(behind, extra, y)
                if k == -1:
                    return wide(behind, g, y)
                if k == BX:
                    return wide(ahead, g, y)
                x = k if upward else BX - 1 - k
                return f_ref[g, LINE * x + NZ * y : LINE * x + NZ * (y + 1)]

            face_before = upwind_face(at_x(-2), at_x(-1), at_x(0))
            for k in range(BX):
                x = k if upward else BX - 1 - k
                face = upwind_face(at_x(k - 1), at_x(k), at_x(k + 1))
                here = slice(LINE * x + NZ * y, LINE * x + NZ * (y + 1))
                moved_ref[g, here] = part_ref[g, here] - ux * (face - face_before)
                face_before = face
        for x in range(BX):

            def at_y(y):
                if y == -2:
                    below = wide(y_below_ref, extra, x)
                    return below if upward else pltpu.roll(below, WIDTH // 2, 1)
                if y == -1:
                    return wide(y_below_ref, g, x)
                if y == BY:
                    return wide(y_above_ref, g, x)
                if y == BY + 1:
                    above = wide(y_above_ref, extra, x)
                    return pltpu.roll(above, WIDTH // 2, 1) if upward else above
                return f_ref[g, LINE * x + NZ * y : LINE * x + NZ * (y + 1)]

            up, _ = edges(at_y(-2), at_y(-1), at_y(0))
            next_up, next_down = edges(at_y(-1), at_y(0), at_y(1))
            flux_before = jnp.where(y_up, up, next_down)
            for y in range(BY):
                up = next_up
                next_up, next_down = edges(at_y(y), at_y(y + 1), at_y(y + 2))
                flux = jnp.where(y_up, up, next_down)
                here = slice(LINE * x + NZ * y, LINE * x + NZ * (y + 1))
                moved_ref[g, here] = moved_ref[g, here] - uy * (flux - flux_before)
                flux_before = flux

    def downwards(pair, carry):
        group(pair, False)
        return carry

    def upwards(pair, carry):
        group(pair, True)
        return carry

    lax.fori_loop(0, half, downwards, 0)
    lax.fori_loop(0, half, upwards, 0)


def second_collide_kernel(
    moved_ref, a_ref, b_ref, c_ref, project_ref, mix_ref, expand_ref, w_ref, rate_ref, mask_ref,
    out_ref, hidden_ref,
):
    rows = jnp.concatenate([moved_ref[g].astype(jnp.bfloat16) for g in range(GROUPS)], axis=1)
    rate = jnp.broadcast_to(rate_ref[...], (LAYER, WIDTH))
    kinetic = jnp.broadcast_to(mask_ref[...], (LAYER, WIDTH)) > 0.0
    for g, collision, equilibrium in collision_terms(
        rows, a_ref, b_ref, c_ref, project_ref, mix_ref, expand_ref, w_ref, hidden_ref
    ):
        moved = moved_ref[g]
        change = jnp.where(kinetic, COLLIDE * collision, rate * (equilibrium - moved))
        out_ref[g] = (moved + change).astype(jnp.bfloat16)


def place_kernel(in_ref, out_ref):
    for high in range(2):
        for core in range(2):
            quarter = 2 * high + (core ^ high)
            for x in range(BX):
                for y in range(BY):
                    c = LINE * x + NZ * y
                    out_ref[x, BY * quarter + y] = in_ref[high, 0, core, c : c + NZ].astype(
                        jnp.float32
                    )


def place(pieces):
    pieces = pieces.reshape(2, GROUPS // 4, 2, LAYER, WIDTH)
    return pl.pallas_call(
        place_kernel,
        grid=(GROUPS // 4,),
        out_shape=jax.ShapeDtypeStruct((CX, NY, NZ, WIDTH), jnp.float32),
        in_specs=[pl.BlockSpec((2, 1, 2, LAYER, WIDTH), lambda i: (0, i, 0, 0, 0))],
        out_specs=pl.BlockSpec((BX, NY, NZ, WIDTH), lambda i: (i, 0, 0, 0)),
        compiler_params=pltpu.CompilerParams(vmem_limit_bytes=8 << 20),
        cost_estimate=pl.CostEstimate(flops=0, bytes_accessed=3 << 20, transcendentals=0),
        name="place",
    )(pieces)


def device_of(space, high, x, core):
    return (space * 2 + high) * 8 + x * 2 + core


def steps_of(slabs):
    upwind, downwind, x_up, y_up = [], [], [], []
    for space in range(slabs):
        for high in range(2):
            for x in range(4):
                for core in range(2):
                    me = device_of(space, high, x, core)
                    after = device_of((space + 1) % slabs, high, x, core)
                    before = device_of((space - 1) % slabs, high, x, core)
                    upwind.append((me, after if high else before))
                    downwind.append((me, before if high else after))
                    next_slab = (space + (x == 3)) % slabs
                    x_up.append((me, device_of(next_slab, high, (x + 1) % 4, core)))
                    quarter = (2 * high + (core ^ high) + 1) % 4
                    y_up.append(
                        (me, device_of(space, quarter // 2, x, (quarter % 2) ^ (quarter // 2)))
                    )
    back = lambda pairs: [(target, source) for source, target in pairs]
    return upwind, downwind, x_up, back(x_up), y_up, back(y_up)


def body(dist, relax_rate, kinetic_cells, kinetic_count, map_a, map_b, map_c):
    rank_vel = lax.axis_index("vel")
    rank_space = lax.axis_index("space")
    both = ("space", "vel")
    upwind, downwind, x_up, x_down, y_up, y_down = steps_of(lax.axis_size("space"))
    project, mix, expand, w, u = tables()
    consts = (jnp.asarray(project), jnp.asarray(mix), jnp.asarray(expand), jnp.asarray(w))
    maps = (map_a, map_b, map_c)
    u = jnp.asarray(u)
    vx = (rank_vel.astype(jnp.float32) - 0.5 * (GX - 1)) * SPACING
    speed = (COURANT * jnp.abs(vx)).reshape(1)
    forward = rank_vel >= GROUPS // 2
    sign = jnp.where(forward, 1, -1).astype(jnp.int32).reshape(1)

    behind = lax.dynamic_slice_in_dim(dist, jnp.where(forward, CX - 2, 0), 2, 0)
    ahead = lax.dynamic_slice_in_dim(dist, jnp.where(forward, 0, CX - 1), 1, 0)
    behind = lax.ppermute(behind, both, upwind)
    ahead = lax.ppermute(ahead, both, downwind)

    high, x_quarter, core = rank_vel // 8, rank_vel // 2 % 4, rank_vel % 2
    y_quarter = 2 * high + (core + high) % 2
    rate = lax.dynamic_slice(relax_rate, (BX * x_quarter, BY * y_quarter, 0), (BX, BY, NZ))
    rate = rate.reshape(LAYER, 1)
    own = lax.dynamic_index_in_dim(kinetic_count, rank_space, 1, False)
    live = jnp.arange(CX * LAYER, dtype=jnp.int32)[None, :] < own[:, None]
    listed = jnp.where(live, kinetic_cells, -1)
    slot = jnp.arange(LAYER, dtype=jnp.int32)
    cell = (BX * x_quarter + slot // LINE) * LAYER + (BY * y_quarter * NZ + slot % LINE)
    masks = jnp.any(listed[:, None, :] == cell[None, :, None], axis=2, keepdims=True)
    masks = masks.astype(jnp.float32)

    state = jax.ShapeDtypeStruct((CX, NY, NZ, WIDTH), jnp.float32)
    wide = jax.ShapeDtypeStruct((GROUPS, LAYER, WIDTH), jnp.float32)
    narrow = jax.ShapeDtypeStruct((GROUPS, LAYER, WIDTH), jnp.bfloat16)
    halo = jax.ShapeDtypeStruct((GROUPS + GROUPS // 2, LINE, WIDTH), jnp.bfloat16)
    hidden = (pltpu.VMEM((LAYER, RANK), jnp.bfloat16),)

    (part,) = call(first_yz_kernel, "first_yz", (dist, u), (state,), flops=12_000_000)
    (rows,) = call(
        first_x_kernel, "first_x", (sign, speed, dist, part, behind, ahead), (narrow,), 2,
        flops=6_000_000,
    )
    gathered = lax.all_to_all(rows, "vel", split_axis=0, concat_axis=0, tiled=True)
    f, up_x, down_x, up_y, down_y = call(
        first_collide_kernel, "first_collide", (gathered,) + maps + consts + (rate, masks[0]),
        (wide, halo, halo, halo, halo), scratch=hidden, flops=2_500_000_000, limit=LIMIT,
    )
    x_below = lax.ppermute(up_x, both, x_up)
    x_above = lax.ppermute(down_x, both, x_down)
    y_below = lax.ppermute(up_y, both, y_up)
    y_above = lax.ppermute(down_y, both, y_down)
    (part,) = call(second_z_kernel, "second_z", (f, u), (wide,), flops=6_000_000)
    (moved,) = call(
        second_xy_kernel, "second_xy", (f, part, x_below, x_above, y_below, y_above, u), (wide,),
        flops=12_000_000,
    )
    (result,) = call(
        second_collide_kernel, "second_collide", (moved,) + maps + consts + (rate, masks[1]),
        (narrow,), scratch=hidden, flops=2_500_000_000, limit=LIMIT,
    )
    return place(lax.all_to_all(result, "vel", split_axis=0, concat_axis=0, tiled=True))


def solution(mesh):
    return jax.shard_map(
        body,
        mesh=mesh,
        in_specs=(
            P("space", None, None, "vel"),
            P("space", None, None),
            P(None, "space"),
            P(),
            P(),
            P(),
            P(),
        ),
        out_specs=P("space", None, None, "vel"),
        check_vma=False,
    )
```

time: 556 us -> 110 us (0.20); the launches traced: 546 us -> 109 us
  waiting for transfers between devices: 212 us -> 22.5 us
  local copies, waits for them, and re-layouts: 149 us -> 18.2 us
  other arithmetic: 96.1 us -> 1.29 us
  matrix products: 39.9 us -> 0 us
  blocking collectives: 0 us -> 25.1 us
  Pallas kernels: 0 us -> 21.2 us
  between operations: 16.1 us -> 0.32 us
  starting transfers between devices: 33.4 us -> 20.2 us
    psum x2 -> x0, waiting for transfers between devices: 190 us -> none  [body(): totals = lax.psum(partial_value, 'vel')]
    gather x4 -> x0, local copies, waits for them, and re-layouts: 63 us -> none  [the longest x2 31.5 us: body(): kin_rows = flat_rows[kin_order]]
    dot_general x8 -> x0, matrix products: 39.9 us -> none  [the longest x2 12.4 us: body(): jnp.einsum('mc,mv->cv', coeffs, local_weighted, precision=lax.Precision.H...]
    scatter x2 -> x0, local copies, waits for them, and re-layouts: 27.5 us -> none  [body(): result = relaxed.at[kin_order].set(new_rows)]
    unnamed x2 -> x0, other arithmetic: 25.2 us -> none
    all_to_all x0 -> x1, blocking collectives: none -> 25.1 us  [body(): lax.all_to_all(result, 'vel', split_axis=0, concat_axis=0, tiled=True)]
    add x6 -> x1, other arithmetic: 22 us -> 0.01 us  [body(): (BX * x_quarter + slot // LINE) * LAYER]
    pallas_call x0 -> x7, Pallas kernels: none -> 21.2 us  [the longest x6 19.3 us: call(): pl.pallas_call(kernel, out_shape=tuple(outs), in_specs=[smem] * scalars +...]
  transfers between devices with their start and end apart: 10 -> 7, of which waited for: 6 -> 4; matrix products, arithmetic and copies ran while one was open for 27% -> 4% of each run, Pallas kernels for 0% -> 4%
where the time goes in v1:
time: 110 us; the launch traced here: 109 us
  blocking collectives  25.1 us (23%)
  waiting for transfers between devices  22.5 us (20%)
  Pallas kernels  21.2 us (19%)
  starting transfers between devices  20.2 us (18%)
  local copies, waits for them, and re-layouts  18.2 us (17%)
  other arithmetic  1.29 us (1%)
    all_to_all x1, blocking collectives, body(): lax.all_to_all(result, 'vel', split_axis=0, concat_axis=0, tiled=True)  25.1 us
    pallas_call x6, Pallas kernels, call(): pl.pallas_call(kernel, out_shape=tuple(outs), in_specs=[smem] * scalars +...  19.3 us
    all_to_all x1, waiting for transfers between devices, body(): lax.all_to_all(rows, 'vel', split_axis=0, concat_axis=0, tiled=True)  15.2 us
    unnamed x46, local copies, waits for them, and re-layouts  14.4 us
    all_to_all x1, starting transfers between devices, body(): lax.all_to_all(rows, 'vel', split_axis=0, concat_axis=0, tiled=True)  7.47 us
    ppermute x1, starting transfers between devices, body(): x_above = lax.ppermute(down_x, both, x_down)  5.68 us
    ppermute x1, starting transfers between devices, body(): behind = lax.ppermute(behind, both, upwind)  5.67 us
    ppermute x1, waiting for transfers between devices, body(): x_below = lax.ppermute(up_x, both, x_up)  4.16 us
  transfers between devices with their start and end apart: 7, of which 4 were waited for; matrix products, arithmetic and copies ran while one was open for 4% of the time, Pallas kernels for 4%

profile of v1, /device:TPU:1, one launch (start us, length us, event | category | flops | bytes accessed | tf_op | source)
XLA Modules:
  0.0 108.8 jit_solution(1013876076256476562)
XLA Ops:
  0.0 1.0 constant_dynamic-slice_fusion.2
  1.0 5.7 %collective-permute-start = (f32[2,16,16,128]{3,2,1,0:T(8,128)S(1)}, f32[2,16,16,128]{3,2,1,0:T(8,128)S(1)}, u32[]{:S(2)}, u32[]{:S(2)}) collective-permute-start(f32[2,16,16,128]{3,2,1,0:T(8,128)S(1)} %constant_dynamic-slice_fusion.2), channel_id=1, source_target_pairs={{0,112},{1,113},{2,114},{3,115},{4,116},{5,117},{6,118},{7,119},{8... | collective-permute-start | bytes 786440 | tf_op jit(solution)/shard_map/ppermute | solution.py:410
  8.6 1.6 %copy-done.6 = f32[16,16,16,128]{3,2,1,0:T(8,128)S(1)} copy-done((f32[16,16,16,128]{3,2,1,0:T(8,128)S(1)}, f32[16,16,16,128]{3,2,1,0:T(8,128)}, u32[]{:S(2)}) %copy-start.6) | copy-done | bytes 2097176
  10.8 2.5 %first_yz.1.part_ref = f32[16,16,16,128]{3,2,1,0:T(8,128)S(1)} custom-call(f32[16,16,16,128]{3,2,1,0:T(8,128)S(1)} %copy-done.6, f32[2,128]{1,0:T(2,128)S(1)} %copy-done.19), custom_call_target="tpu_custom_call" | custom-call | flops 12000000 | bytes 4195328 | tf_op jit(solution)/shard_map/first_yz/pallas_call | solution.py:78
  15.2 2.0 %first_x.1 = bf16[16,256,128]{2,1,0:T(8,128)(2,1)S(1)} custom-call(s32[1]{0:T(128)} %bitcast.sign_ref, f32[1]{0:T(128)} %bitcast.1.speed_ref, f32[16,16,16,128]{3,2,1,0:T(8,128)S(1)} %copy-done.6, f32[16,16,16,128]{3,2,1,0:T(8,128)S(1)} %first_yz.1.part_ref, f32[2,16,16,128]{3,2,1,0:T(8,128)S(1)} %collective-permute-done.behind_ref, ...), custom_call_target="tpu_custom_call" | custom-call | flops 6000000 | bytes 5636104 | tf_op jit(solution)/shard_map/first_x/pallas_call | solution.py:78
  18.1 7.5 %all-to-all-start = ((bf16[16,256,128]{2,1,0:T(8,128)(2,1)}), bf16[16,256,128]{2,1,0:T(8,128)(2,1)}, u32[]{:S(2)}, u32[]{:S(2)}) async-start(bf16[16,256,128]{2,1,0:T(8,128)(2,1)} %copy-done.9), calls=%async_computation | async-start | bytes 2097152 | tf_op jit(solution)/shard_map/all_to_all | solution.py:436
  25.8 1.2 %compare_reduce_fusion = pred[2,256]{1,0:T(4,128)(4,1)S(1)} fusion(s32[2,4096]{1,0:T(2,128)S(1)} %compare_select_fusion, s32[256]{0:T(256)S(1)} %fusion.3), kind=kLoop, calls=%fused_computation | loop fusion | flops 4193792 | bytes 34304 | tf_op jit(solution)/shard_map/reduce_or | solution.py:422
  27.8 15.2 %all-to-all-done.rows_ref = bf16[16,256,128]{2,1,0:T(8,128)(2,1)} async-done(((bf16[16,256,128]{2,1,0:T(8,128)(2,1)}), bf16[16,256,128]{2,1,0:T(8,128)(2,1)}, u32[]{:S(2)}, u32[]{:S(2)}) %all-to-all-start) | async-done | bytes 1048608 | tf_op jit(solution)/shard_map/all_to_all | solution.py:436
  43.1 1.9 %copy-done.2 = bf16[2048,768]{1,0:T(8,128)(2,1)S(1)} copy-done((bf16[2048,768]{1,0:T(8,128)(2,1)S(1)}, bf16[2048,768]{1,0:T(8,128)(2,1)}, u32[]{:S(2)}) %copy-start.2) | copy-done | bytes 3145752
  45.0 1.9 %copy-done.4 = bf16[768,2048]{1,0:T(8,128)(2,1)S(1)} copy-done((bf16[768,2048]{1,0:T(8,128)(2,1)S(1)}, bf16[768,2048]{1,0:T(8,128)(2,1)}, u32[]{:S(2)}) %copy-start.4) | copy-done | bytes 3145752
  46.8 1.0 copy-done.10
  47.9 1.0 copy-done.12
  49.8 6.0 %first_collide.1 = (f32[16,256,128]{2,1,0:T(8,128)S(1)}, bf16[24,64,128]{2,1,0:T(8,128)(2,1)}, bf16[24,64,128]{2,1,0:T(8,128)(2,1)}, bf16[24,64,128]{2,1,0:T(8,128)(2,1)}, bf16[24,64,128]{2,1,0:T(8,128)(2,1)}) custom-call(bf16[16,256,128]{2,1,0:T(8,128)(2,1)} %all-to-all-done.rows_ref, bf16[2048,768]{1,0:T(8,128)(2,1)S(1)} %copy-done.1, ...), custom_call_target="tpu_custom_call" | custom-call | flops 2500000000 | bytes 15280128 | tf_op jit(solution)/shard_map/first_collide/pallas_call | solution.py:78
  55.8 1.3 %copy-done.7 = f32[16,256,128]{2,1,0:T(8,128)} copy-done((f32[16,256,128]{2,1,0:T(8,128)}, f32[16,256,128]{2,1,0:T(8,128)S(1)}, u32[]{:S(2)}) %copy-start.7) | copy-done | bytes 2097176
  57.1 5.7 %collective-permute-start.3 = (bf16[24,64,128]{2,1,0:T(8,128)(2,1)}, bf16[24,64,128]{2,1,0:T(8,128)(2,1)}, u32[]{:S(2)}, u32[]{:S(2)}) collective-permute-start(bf16[24,64,128]{2,1,0:T(8,128)(2,1)} %get-tuple-element.12), channel_id=1, source_target_pairs={{2,0},{3,1},{4,2},{5,3},{6,4},{7,5},{16,6},{17,7},{10,8},{11,9},{1... | collective-permute-start | bytes 1179656 | tf_op jit(solution)/shard_map/ppermute | solution.py:442
  63.1 1.0 collective-permute-start.5
  64.2 1.6 %copy-done.8 = f32[16,256,128]{2,1,0:T(8,128)S(1)} copy-done((f32[16,256,128]{2,1,0:T(8,128)S(1)}, f32[16,256,128]{2,1,0:T(8,128)}, u32[]{:S(2)}) %copy-start.8) | copy-done | bytes 2097176
  65.8 1.6 %second_z.1.part_ref = f32[16,256,128]{2,1,0:T(8,128)S(1)} custom-call(f32[16,256,128]{2,1,0:T(8,128)S(1)} %copy-done.8, f32[2,128]{1,0:T(2,128)S(1)} %copy-done.20), custom_call_target="tpu_custom_call" | custom-call | flops 6000000 | bytes 4195328 | tf_op jit(solution)/shard_map/second_z/pallas_call | solution.py:78
  67.4 4.2 %collective-permute-done.2.x_below_ref = bf16[24,64,128]{2,1,0:T(8,128)(2,1)} collective-permute-done((bf16[24,64,128]{2,1,0:T(8,128)(2,1)}, bf16[24,64,128]{2,1,0:T(8,128)(2,1)}, u32[]{:S(2)}, u32[]{:S(2)}) %collective-permute-start.2) | collective-permute-done | bytes 393248 | tf_op jit(solution)/shard_map/ppermute | solution.py:441
  71.6 2.9 %collective-permute-done.5.y_above_ref = bf16[24,64,128]{2,1,0:T(8,128)(2,1)} collective-permute-done((bf16[24,64,128]{2,1,0:T(8,128)(2,1)}, bf16[24,64,128]{2,1,0:T(8,128)(2,1)}, u32[]{:S(2)}, u32[]{:S(2)}) %collective-permute-start.5) | collective-permute-done | bytes 393248 | tf_op jit(solution)/shard_map/ppermute | solution.py:444
  74.5 3.7 %second_xy.1.moved_ref = f32[16,256,128]{2,1,0:T(8,128)S(1)} custom-call(f32[16,256,128]{2,1,0:T(8,128)S(1)} %copy-done.8, f32[16,256,128]{2,1,0:T(8,128)S(1)} %second_z.1.part_ref, bf16[24,64,128]{2,1,0:T(8,128)(2,1)} %collective-permute-done.2.x_below_ref, bf16[24,64,128]{2,1,0:T(8,128)(2,1)} %collective-permute-done.3.x_above_ref, ...), custom_call_target="tpu_custom_call" | custom-call | flops 12000000 | bytes 7865344 | tf_op jit(solution)/shard_map/second_xy/pallas_call | solution.py:78
  78.2 3.6 %second_collide.1 = bf16[16,256,128]{2,1,0:T(8,128)(2,1)S(1)} custom-call(f32[16,256,128]{2,1,0:T(8,128)S(1)} %second_xy.1.moved_ref, bf16[2048,768]{1,0:T(8,128)(2,1)S(1)} %copy-done.1, bf16[2048,768]{1,0:T(8,128)(2,1)S(1)} %copy-done.3, bf16[768,2048]{1,0:T(8,128)(2,1)S(1)} %copy-done.5, bf16[2048,128]{1,0:T(8,128)(2,1)S(1)} %copy-done.11, ...), custom_call_target="tpu_custom_call" | custom-call | flops 2500000000 | bytes 13707264 | tf_op jit(solution)/shard_map/second_collide/pallas_call | solution.py:78
  81.8 25.1 %all_to_all.10 = bf16[16,256,128]{2,1,0:T(8,128)(2,1)S(1)} all-to-all(bf16[16,256,128]{2,1,0:T(8,128)(2,1)S(1)} %second_collide.1), channel_id=1, replica_groups=mesh['space'=8,'vel'=16] {'vel'}, dimensions={0} | all-to-all | bytes 2097152 | tf_op jit(solution)/shard_map/all_to_all | solution.py:454
  107.0 1.9 %place.1 = f32[16,16,16,128]{3,2,1,0:T(8,128)} custom-call(bf16[2,4,2,256,128]{4,3,2,1,0:T(8,128)(2,1)S(1)} %bitcast.7), custom_call_target="tpu_custom_call" | custom-call | bytes 3145728 | tf_op jit(solution)/shard_map/place/pallas_call | solution.py:357
  (56 shorter events, 7.6 us)
Async XLA Ops:
  0.0 27.7 %copy-start = (f32[16,16,16]{2,1,0:T(8,128)S(1)}, f32[16,16,16]{2,1,0:T(8,128)}, u32[]{:S(2)}) copy-start(f32[16,16,16]{2,1,0:T(8,128)} %param.13) | copy-start | bytes 49156
  1.0 13.2 %collective-permute-start = (f32[2,16,16,128]{3,2,1,0:T(8,128)S(1)}, f32[2,16,16,128]{3,2,1,0:T(8,128)S(1)}, u32[]{:S(2)}, u32[]{:S(2)}) collective-permute-start(f32[2,16,16,128]{3,2,1,0:T(8,128)S(1)} %constant_dynamic-slice_fusion.2), channel_id=1, source_target_pairs={{0,112},{1,113},{2,114},{3,115},{4,116},{5,117},{6,118},{7,119},{8... | collective-permute-start | bytes 786440 | tf_op jit(solution)/shard_map/ppermute | solution.py:410
  7.6 6.0 %collective-permute-start.1 = (f32[1,16,16,128]{3,2,1,0:T(8,128)S(1)}, f32[1,16,16,128]{3,2,1,0:T(8,128)S(1)}, u32[]{:S(2)}, u32[]{:S(2)}) collective-permute-start(f32[1,16,16,128]{3,2,1,0:T(8,128)S(1)} %constant_dynamic-slice_fusion.1), channel_id=1, source_target_pairs={{0,16},{1,17},{2,18},{3,19},{4,20},{5,21},{6,22},{7,23},{8,120},{9... | collective-permute-start | bytes 393224 | tf_op jit(solution)/shard_map/ppermute | solution.py:411
  8.6 1.6 %copy-start.6 = (f32[16,16,16,128]{3,2,1,0:T(8,128)S(1)}, f32[16,16,16,128]{3,2,1,0:T(8,128)}, u32[]{:S(2)}) copy-start(f32[16,16,16,128]{3,2,1,0:T(8,128)} %f_ref.3) | copy-start | bytes 6291460
  15.2 27.9 %copy-start.1 = (bf16[2048,768]{1,0:T(8,128)(2,1)S(1)}, bf16[2048,768]{1,0:T(8,128)(2,1)}, u32[]{:S(2)}) copy-start(bf16[2048,768]{1,0:T(8,128)(2,1)} %a_ref.3) | copy-start | bytes 9437188
  18.1 7.5 %copy-start.21 = (s32[2,4096]{1,0:T(2,128)S(1)}, s32[2,4096]{1,0:T(2,128)}, u32[]{:S(2)}) copy-start(s32[2,4096]{1,0:T(2,128)} %param.14) | copy-start | bytes 98308
  18.1 24.9 %copy-start.18 = (f32[1,2048]{1,0:T(1,128)S(1)}, f32[1,2048]{1,0:T(1,128)}, u32[]{:S(2)}) copy-start(f32[1,2048]{1,0:T(1,128)} %constant.126.clone.w_ref) | copy-start | bytes 24580
  18.1 24.9 %all-to-all-start = ((bf16[16,256,128]{2,1,0:T(8,128)(2,1)}), bf16[16,256,128]{2,1,0:T(8,128)(2,1)}, u32[]{:S(2)}, u32[]{:S(2)}) async-start(bf16[16,256,128]{2,1,0:T(8,128)(2,1)} %copy-done.9), calls=%async_computation | async-start | bytes 2097152 | tf_op jit(solution)/shard_map/all_to_all | solution.py:436
  43.1 1.9 %copy-start.2 = (bf16[2048,768]{1,0:T(8,128)(2,1)S(1)}, bf16[2048,768]{1,0:T(8,128)(2,1)}, u32[]{:S(2)}) copy-start(bf16[2048,768]{1,0:T(8,128)(2,1)} %b_ref.3) | copy-start | bytes 9437188
  45.0 1.9 %copy-start.4 = (bf16[768,2048]{1,0:T(8,128)(2,1)S(1)}, bf16[768,2048]{1,0:T(8,128)(2,1)}, u32[]{:S(2)}) copy-start(bf16[768,2048]{1,0:T(8,128)(2,1)} %c_ref.3) | copy-start | bytes 9437188
  46.8 1.0 copy-start.10
  49.8 14.3 %copy-start.22 = (f32[256,1]{0,1:T(1,128)S(1)}, f32[256,1]{0,1:T(1,128)}, u32[]{:S(2)}) copy-start(f32[256,1]{0,1:T(1,128)} %get-tuple-element.15) | copy-start | bytes 3076
  49.8 14.5 %copy-start.20 = (f32[2,128]{1,0:T(2,128)S(1)}, f32[2,128]{1,0:T(2,128)}, u32[]{:S(2)}) copy-start(f32[2,128]{1,0:T(2,128)} %constant.127.clone.u_ref) | copy-start | bytes 3076
  55.8 1.3 %copy-start.7 = (f32[16,256,128]{2,1,0:T(8,128)}, f32[16,256,128]{2,1,0:T(8,128)S(1)}, u32[]{:S(2)}) copy-start(f32[16,256,128]{2,1,0:T(8,128)S(1)} %get-tuple-element.10.f_ref) | copy-start | bytes 6291460
  57.1 14.5 %collective-permute-start.2 = (bf16[24,64,128]{2,1,0:T(8,128)(2,1)}, bf16[24,64,128]{2,1,0:T(8,128)(2,1)}, u32[]{:S(2)}, u32[]{:S(2)}) collective-permute-start(bf16[24,64,128]{2,1,0:T(8,128)(2,1)} %get-tuple-element.11), channel_id=1, source_target_pairs={{0,2},{1,3},{2,4},{3,5},{4,6},{5,7},{6,16},{7,17},{8,10},{9,11},{1... | collective-permute-start | bytes 1179656 | tf_op jit(solution)/shard_map/ppermute | solution.py:441
  57.1 14.5 %collective-permute-start.3 = (bf16[24,64,128]{2,1,0:T(8,128)(2,1)}, bf16[24,64,128]{2,1,0:T(8,128)(2,1)}, u32[]{:S(2)}, u32[]{:S(2)}) collective-permute-start(bf16[24,64,128]{2,1,0:T(8,128)(2,1)} %get-tuple-element.12), channel_id=1, source_target_pairs={{2,0},{3,1},{4,2},{5,3},{6,4},{7,5},{16,6},{17,7},{10,8},{11,9},{1... | collective-permute-start | bytes 1179656 | tf_op jit(solution)/shard_map/ppermute | solution.py:442
  62.8 8.8 %collective-permute-start.4 = (bf16[24,64,128]{2,1,0:T(8,128)(2,1)}, bf16[24,64,128]{2,1,0:T(8,128)(2,1)}, u32[]{:S(2)}, u32[]{:S(2)}) collective-permute-start(bf16[24,64,128]{2,1,0:T(8,128)(2,1)} %get-tuple-element.13), channel_id=1, source_target_pairs={{0,1},{1,9},{2,3},{3,11},{4,5},{5,13},{6,7},{7,15},{8,0},{9,8},{10... | collective-permute-start | bytes 1179656 | tf_op jit(solution)/shard_map/ppermute | solution.py:443
  63.1 11.4 %collective-permute-start.5 = (bf16[24,64,128]{2,1,0:T(8,128)(2,1)}, bf16[24,64,128]{2,1,0:T(8,128)(2,1)}, u32[]{:S(2)}, u32[]{:S(2)}) collective-permute-start(bf16[24,64,128]{2,1,0:T(8,128)(2,1)} %get-tuple-element.14), channel_id=1, source_target_pairs={{1,0},{9,1},{3,2},{11,3},{5,4},{13,5},{7,6},{15,7},{0,8},{8,9},{2,... | collective-permute-start | bytes 1179656 | tf_op jit(solution)/shard_map/ppermute | solution.py:444
  64.2 1.6 %copy-start.8 = (f32[16,256,128]{2,1,0:T(8,128)S(1)}, f32[16,256,128]{2,1,0:T(8,128)}, u32[]{:S(2)}) copy-start(f32[16,256,128]{2,1,0:T(8,128)} %copy-done.7) | copy-start | bytes 6291460
  67.4 10.8 %copy-start.3 = (bf16[2048,768]{1,0:T(8,128)(2,1)S(1)}, bf16[2048,768]{1,0:T(8,128)(2,1)}, u32[]{:S(2)}) copy-start(bf16[2048,768]{1,0:T(8,128)(2,1)} %b_ref.3) | copy-start | bytes 9437188
  67.4 10.8 %copy-start.5 = (bf16[768,2048]{1,0:T(8,128)(2,1)S(1)}, bf16[768,2048]{1,0:T(8,128)(2,1)}, u32[]{:S(2)}) copy-start(bf16[768,2048]{1,0:T(8,128)(2,1)} %c_ref.3) | copy-start | bytes 9437188
  67.4 10.8 %copy-start.11 = (bf16[2048,128]{1,0:T(8,128)(2,1)S(1)}, bf16[2048,128]{1,0:T(8,128)(2,1)}, u32[]{:S(2)}) copy-start(bf16[2048,128]{1,0:T(8,128)(2,1)} %constant.123.clone.project_ref) | copy-start | bytes 1572868
  67.4 10.8 %copy-start.13 = (bf16[128,2048]{1,0:T(8,128)(2,1)S(1)}, bf16[128,2048]{1,0:T(8,128)(2,1)}, u32[]{:S(2)}) copy-start(bf16[128,2048]{1,0:T(8,128)(2,1)} %constant.125.clone.expand_ref) | copy-start | bytes 1572868
  67.4 10.8 %copy-start.15 = (f32[128,128]{1,0:T(8,128)S(1)}, f32[128,128]{1,0:T(8,128)}, u32[]{:S(2)}) copy-start(f32[128,128]{1,0:T(8,128)} %constant.124.clone.mix_ref) | copy-start | bytes 196612
  (6 other events, 5.1 us)

commit v2 on v1

--- a/solution.py
+++ b/solution.py
@@ -25,7 +25,6 @@
 BX = 4
 BY = 4
 LINE = BX * NZ
-LIMIT = 12 << 20
 
 
 def tables():
@@ -60,7 +59,6 @@
         mix.astype(np.float32),
         expand.astype(jnp.bfloat16),
         w.reshape(1, NV).astype(np.float32),
-        (COURANT * np.stack([vy[:WIDTH], vz[:WIDTH]])).astype(np.float32),
     )
 
 
@@ -68,23 +66,35 @@
     return 0.5 * (jnp.maximum(jnp.minimum(a, b), 0.0) + jnp.minimum(jnp.maximum(a, b), 0.0))
 
 
-def call(kernel, name, operands, outs, spaces=None, scratch=(), flops=0, limit=8 << 20):
-    vmem = pl.BlockSpec(memory_space=pltpu.VMEM)
-    smem = pl.BlockSpec(memory_space=pltpu.SMEM)
-    scalars = spaces or 0
-    moved = sum(o.size * o.dtype.itemsize for o in operands) + sum(
-        o.size * o.dtype.itemsize for o in outs
-    )
+ALL_VMEM = 62 << 20
+X_VMEM = 8 << 20
+HBM = pltpu.HBM
+VMEM = pltpu.VMEM
+SMEM = pltpu.SMEM
+DMA = pltpu.SemaphoreType.DMA
+
+
+def call(kernel, name, operands, outs, scratch=(), flops=0, limit=8 << 20):
+    shapes = [jax.ShapeDtypeStruct(shape, dtype) for shape, dtype, _ in outs]
+    arrays = [o for o, _ in operands]
+    moved = sum(o.size * o.dtype.itemsize for o in arrays + shapes)
     return pl.pallas_call(
         kernel,
-        out_shape=tuple(outs),
-        in_specs=[smem] * scalars + [vmem] * (len(operands) - scalars),
-        out_specs=tuple(vmem for _ in outs),
+        out_shape=tuple(shapes),
+        in_specs=[pl.BlockSpec(memory_space=space) for _, space in operands],
+        out_specs=tuple(pl.BlockSpec(memory_space=space) for _, _, space in outs),
         scratch_shapes=list(scratch),
         compiler_params=pltpu.CompilerParams(vmem_limit_bytes=limit),
         cost_estimate=pl.CostEstimate(flops=flops, bytes_accessed=moved, transcendentals=0),
         name=name,
-    )(*operands)
+    )(*arrays)
+
+
+def speeds_yz():
+    lane = lax.broadcasted_iota(jnp.int32, (NZ, WIDTH), 1)
+    along_y = (lane >> 3).astype(jnp.float32) - 0.5 * (GY - 1)
+    along_z = (lane & (GZ - 1)).astype(jnp.float32) - 0.5 * (GZ - 1)
+    return along_y * (SPACING * COURANT), along_z * (SPACING * COURANT)
 
 
 def flux_change_z(f, uz, z_up):
@@ -104,13 +114,38 @@
     return here + minmod_half(here - before, after - here)
 
 
-def first_yz_kernel(f_ref, u_ref, part_ref):
-    uy = jnp.broadcast_to(u_ref[0:1], (NZ, WIDTH))
-    uz = jnp.broadcast_to(u_ref[1:2], (NZ, WIDTH))
+def first_halo_kernel(sign_ref, dist_ref, behind_ref, ahead_ref, layers_ref, sems):
+    forward = sign_ref[0] > 0
+    copies = [
+        pltpu.make_async_copy(
+            dist_ref.at[pl.ds(jnp.where(forward, CX - 2, 0), 2)], layers_ref.at[0:2], sems.at[0]
+        ),
+        pltpu.make_async_copy(
+            dist_ref.at[pl.ds(jnp.where(forward, 0, CX - 1), 1)], layers_ref.at[2:3], sems.at[1]
+        ),
+    ]
+    for copy in copies:
+        copy.start()
+    copies[0].wait()
+    behind_ref[...] = layers_ref[0:2].astype(jnp.bfloat16)
+    copies[1].wait()
+    ahead_ref[...] = layers_ref[2:3].astype(jnp.bfloat16)
+
+
+def first_yz_kernel(dist_ref, f_ref, part_ref, sems):
+    uy, uz = speeds_yz()
     y_up = uy > 0.0
     z_up = uz > 0.0
 
-    def layer(x, carry):
+    def fetch(i):
+        return pltpu.make_async_copy(
+            dist_ref.at[pl.ds(2 * i, 2)], f_ref.at[pl.ds(2 * i, 2)], sems.at[i]
+        )
+
+    for i in range(CX // 2):
+        fetch(i).start()
+
+    def layer(x):
         def at(y):
             return f_ref[x, y % NY]
 
@@ -124,22 +159,29 @@
             here = at(y)
             part_ref[x, y] = here - uy * (flux - flux_before) - flux_change_z(here, uz, z_up)
             flux_before = flux
+
+    def two_layers(i, carry):
+        fetch(i).wait()
+        layer(2 * i)
+        layer(2 * i + 1)
         return carry
 
-    lax.fori_loop(0, CX, layer, 0)
-
-
-def first_x_kernel(sign_ref, speed_ref, f_ref, part_ref, behind_ref, ahead_ref, rows_ref):
+    lax.fori_loop(0, CX // 2, two_layers, 0)
+
+
+def first_x_kernel(
+    sign_ref, speed_ref, f_ref, part_ref, behind_ref, ahead_ref, out_ref, rows_ref, sems
+):
     s = sign_ref[0]
     ux = speed_ref[0]
     forward = s > 0
 
-    def line(y, carry):
-        quarter = y // BY
-        high = quarter // 2
-        core = (quarter + high) % 2
-        target = high * (GROUPS // 2) + core
-        inner = (y % BY) * NZ
+    def put(target):
+        return pltpu.make_async_copy(rows_ref.at[target], out_ref.at[target], sems.at[target])
+
+    def line(quarter, y):
+        inner = y * NZ
+        y = quarter * BY + y
 
         def at(k):
             if k == -2:
@@ -157,15 +199,31 @@
             result = part_ref[x, y] - ux * (face - face_before)
             face_before = face
             start = pl.multiple_of((x % BX) * LINE + inner, NZ)
-            rows_ref[target + (x // BX) * 2, pl.ds(start, NZ), :] = result.astype(jnp.bfloat16)
+            high = x // (2 * BX)
+            core = (x // BX + high) % 2
+            target = high * (GROUPS // 2) + quarter * 2 + core
+            rows_ref[target, pl.ds(start, NZ), :] = result.astype(jnp.bfloat16)
+
+    def lines(quarter, carry):
+        def one(y, inside):
+            line(quarter, y)
+            return inside
+
+        lax.fori_loop(0, BY, one, 0)
+        for high in range(2):
+            for core in range(2):
+                put(high * (GROUPS // 2) + quarter * 2 + core).start()
         return carry
 
-    lax.fori_loop(0, NY, line, 0)
+    lax.fori_loop(0, NY // BY, lines, 0)
+    for target in range(GROUPS):
+        put(target).wait()
 
 
 def collision_terms(
-    rows, a_ref, b_ref, c_ref, project_ref, mix_ref, expand_ref, w_ref, hidden_ref
+    rows, a_ref, b_ref, c_ref, project_ref, mix_ref, expand_ref, w_ref, hidden_ref, arrive
 ):
+    arrive(0)
     moments = jnp.dot(rows, project_ref[...], preferred_element_type=jnp.float32)
     coeffs = jnp.dot(
         moments, mix_ref[...], precision=lax.Precision.HIGHEST, preferred_element_type=jnp.float32
@@ -178,12 +236,15 @@
     split = split.astype(jnp.bfloat16)
     for n in range(RANK // 256):
         cols = slice(256 * n, 256 * (n + 1))
+        arrive(1 + n)
         first = jnp.dot(rows, a_ref[:, cols], preferred_element_type=jnp.float32)
         second = jnp.dot(rows, b_ref[:, cols], preferred_element_type=jnp.float32)
         hidden_ref[:, cols] = (first * second).astype(jnp.bfloat16)
     hidden = hidden_ref[...]
     for n in range(NV // 256):
         cols = slice(256 * n, 256 * (n + 1))
+        if n % 2 == 0:
+            arrive(4 + n // 2)
         collision = jnp.dot(hidden, c_ref[:, cols], preferred_element_type=jnp.float32)
         collision = collision.astype(jnp.bfloat16).astype(jnp.float32)
         poly = jnp.dot(split, expand_ref[:, cols], preferred_element_type=jnp.float32)
@@ -194,15 +255,53 @@
 
 
 def first_collide_kernel(
-    rows_ref, a_ref, b_ref, c_ref, project_ref, mix_ref, expand_ref, w_ref, rate_ref, mask_ref,
-    f_ref, x_up_ref, x_down_ref, y_up_ref, y_down_ref, hidden_ref,
+    rows_hbm, a_hbm, b_hbm, c_hbm, project_hbm, mix_hbm, expand_hbm, w_ref, rate_ref, mask_ref,
+    f_out, x_up_out, x_down_out, y_up_out, y_down_out,
+    rows_ref, a_ref, b_ref, c_ref, project_ref, mix_ref, expand_ref, hidden_ref,
+    f_ref, x_up_ref, x_down_ref, y_up_ref, y_down_ref, in_sems, out_sems,
 ):
+    pieces = [[(rows_hbm, rows_ref), (project_hbm, project_ref), (mix_hbm, mix_ref)]]
+    for n in range(RANK // 256):
+        cols = slice(256 * n, 256 * (n + 1))
+        pieces.append([(a_hbm.at[:, cols], a_ref.at[:, cols]), (b_hbm.at[:, cols], b_ref.at[:, cols])])
+    pieces.append([(expand_hbm, expand_ref)])
+    for n in range(4):
+        cols = slice(512 * n, 512 * (n + 1))
+        if n:
+            pieces.append([])
+        pieces[-1].append((c_hbm.at[:, cols], c_ref.at[:, cols]))
+    fetches, count = [], 0
+    for piece in pieces:
+        fetches.append([])
+        for source, target in piece:
+            fetches[-1].append(pltpu.make_async_copy(source, target, in_sems.at[count]))
+            fetches[-1][-1].start()
+            count += 1
+
+    def arrive(i):
+        for fetch in fetches[i]:
+            fetch.wait()
+
+    stores = []
+
+    def send(source, target, first, last):
+        stores.append(
+            pltpu.make_async_copy(
+                source.at[first:last], target.at[first:last], out_sems.at[len(stores)]
+            )
+        )
+        stores[-1].start()
+
+    for fetch in fetches[0]:
+        fetch.wait()
     rows = jnp.concatenate([rows_ref[g] for g in range(GROUPS)], axis=1)
     rate = jnp.broadcast_to(rate_ref[...], (LAYER, WIDTH))
     kinetic = jnp.broadcast_to(mask_ref[...], (LAYER, WIDTH)) > 0.0
     half = GROUPS // 2
+    low_lane = lax.broadcasted_iota(jnp.int32, (NZ, WIDTH), 1) < WIDTH // 2
     for g, collision, equilibrium in collision_terms(
-        rows, a_ref, b_ref, c_ref, project_ref, mix_ref, expand_ref, w_ref, hidden_ref
+        rows, a_ref, b_ref, c_ref, project_ref, mix_ref, expand_ref, w_ref, hidden_ref,
+        lambda i: arrive(i) if i else None,
     ):
         moved = rows_ref[g].astype(jnp.float32)
         change = jnp.where(kinetic, COLLIDE * collision, rate * (equilibrium - moved))
@@ -219,43 +318,62 @@
             here = slice(NZ * x, NZ * (x + 1))
             y_down_ref[g, here] = sent[LINE * x : LINE * x + NZ]
             y_up_ref[g, here] = sent[LINE * x + 3 * NZ : LINE * x + 4 * NZ]
-    low_lane = lax.broadcasted_iota(jnp.int32, (NZ, WIDTH), 1) < WIDTH // 2
-    for g in range(half):
-        for x in range(BX):
-            here = slice(NZ * x, NZ * (x + 1))
-            second = slice(LINE * x + NZ, LINE * x + 2 * NZ)
-            third = slice(LINE * x + 2 * NZ, LINE * x + 3 * NZ)
-            y_up_ref[GROUPS + g, here] = jnp.where(
-                low_lane,
-                pltpu.roll(f_ref[g, third], WIDTH // 2, 1),
-                f_ref[g + half, third],
-            ).astype(jnp.bfloat16)
-            y_down_ref[GROUPS + g, here] = jnp.where(
-                low_lane,
-                f_ref[g, second],
-                pltpu.roll(f_ref[g + half, second], WIDTH // 2, 1),
-            ).astype(jnp.bfloat16)
-
-
-def second_z_kernel(f_ref, u_ref, part_ref):
-    uz = jnp.broadcast_to(u_ref[1:2], (NZ, WIDTH))
+            if g >= half:
+                low = g - half
+                second = slice(LINE * x + NZ, LINE * x + 2 * NZ)
+                third = slice(LINE * x + 2 * NZ, LINE * x + 3 * NZ)
+                y_up_ref[GROUPS + low, here] = jnp.where(
+                    low_lane, pltpu.roll(f_ref[low, third], WIDTH // 2, 1), result[third]
+                ).astype(jnp.bfloat16)
+                y_down_ref[GROUPS + low, here] = jnp.where(
+                    low_lane, f_ref[low, second], pltpu.roll(result[second], WIDTH // 2, 1)
+                ).astype(jnp.bfloat16)
+        if g % 4 == 3:
+            first = g - 3
+            send(f_ref, f_out, first, g + 1)
+            for source, target in (
+                (y_up_ref, y_up_out), (y_down_ref, y_down_out),
+                (x_up_ref, x_up_out), (x_down_ref, x_down_out),
+            ):
+                send(source, target, first, g + 1)
+            if g >= half:
+                send(y_up_ref, y_up_out, first + half, g + 1 + half)
+                send(y_down_ref, y_down_out, first + half, g + 1 + half)
+                send(x_up_ref, x_up_out, first + half, g + 1 + half)
+            else:
+                send(x_down_ref, x_down_out, first + GROUPS, g + 1 + GROUPS)
+    for store in stores:
+        store.wait()
+
+
+def second_z_kernel(f_hbm, f_ref, part_ref, sems):
+    _, uz = speeds_yz()
     z_up = uz > 0.0
 
-    def group(g, carry):
-        for c in range(BX * BY):
-            here = slice(NZ * c, NZ * (c + 1))
-            f = f_ref[g, here]
-            part_ref[g, here] = f - flux_change_z(f, uz, z_up)
+    def fetch(i):
+        return pltpu.make_async_copy(
+            f_hbm.at[pl.ds(2 * i, 2)], f_ref.at[pl.ds(2 * i, 2)], sems.at[i]
+        )
+
+    for i in range(GROUPS // 2):
+        fetch(i).start()
+
+    def two_groups(i, carry):
+        fetch(i).wait()
+        for g in (2 * i, 2 * i + 1):
+            for c in range(BX * BY):
+                here = slice(NZ * c, NZ * (c + 1))
+                f = f_ref[g, here]
+                part_ref[g, here] = f - flux_change_z(f, uz, z_up)
         return carry
 
-    lax.fori_loop(0, GROUPS, group, 0)
+    lax.fori_loop(0, GROUPS // 2, two_groups, 0)
 
 
 def second_xy_kernel(
-    f_ref, part_ref, x_below_ref, x_above_ref, y_below_ref, y_above_ref, u_ref,
-    moved_ref,
+    f_ref, part_ref, x_below_ref, x_above_ref, y_below_ref, y_above_ref, moved_ref
 ):
-    uy = jnp.broadcast_to(u_ref[0:1], (NZ, WIDTH))
+    uy, _ = speeds_yz()
     y_up = uy > 0.0
     half = GROUPS // 2
 
@@ -333,37 +451,31 @@
     rate = jnp.broadcast_to(rate_ref[...], (LAYER, WIDTH))
     kinetic = jnp.broadcast_to(mask_ref[...], (LAYER, WIDTH)) > 0.0
     for g, collision, equilibrium in collision_terms(
-        rows, a_ref, b_ref, c_ref, project_ref, mix_ref, expand_ref, w_ref, hidden_ref
+        rows, a_ref, b_ref, c_ref, project_ref, mix_ref, expand_ref, w_ref, hidden_ref,
+        lambda i: None,
     ):
         moved = moved_ref[g]
         change = jnp.where(kinetic, COLLIDE * collision, rate * (equilibrium - moved))
         out_ref[g] = (moved + change).astype(jnp.bfloat16)
 
 
-def place_kernel(in_ref, out_ref):
-    for high in range(2):
-        for core in range(2):
-            quarter = 2 * high + (core ^ high)
-            for x in range(BX):
+def place_kernel(in_ref, out_hbm, out_ref, sems):
+    stores = []
+    for quarter in range(4):
+        high = quarter // 2
+        core = (quarter % 2) ^ high
+        for x in range(BX):
+            for y_quarter in range(4):
                 for y in range(BY):
                     c = LINE * x + NZ * y
-                    out_ref[x, BY * quarter + y] = in_ref[high, 0, core, c : c + NZ].astype(
-                        jnp.float32
-                    )
-
-
-def place(pieces):
-    pieces = pieces.reshape(2, GROUPS // 4, 2, LAYER, WIDTH)
-    return pl.pallas_call(
-        place_kernel,
-        grid=(GROUPS // 4,),
-        out_shape=jax.ShapeDtypeStruct((CX, NY, NZ, WIDTH), jnp.float32),
-        in_specs=[pl.BlockSpec((2, 1, 2, LAYER, WIDTH), lambda i: (0, i, 0, 0, 0))],
-        out_specs=pl.BlockSpec((BX, NY, NZ, WIDTH), lambda i: (i, 0, 0, 0)),
-        compiler_params=pltpu.CompilerParams(vmem_limit_bytes=8 << 20),
-        cost_estimate=pl.CostEstimate(flops=0, bytes_accessed=3 << 20, transcendentals=0),
-        name="place",
-    )(pieces)
+                    out_ref[BX * quarter + x, BY * y_quarter + y] = in_ref[
+                        high * (GROUPS // 2) + y_quarter * 2 + core, c : c + NZ
+                    ].astype(jnp.float32)
+        part = slice(BX * quarter, BX * (quarter + 1))
+        stores.append(pltpu.make_async_copy(out_ref.at[part], out_hbm.at[part], sems.at[quarter]))
+        stores[-1].start()
+    for store in stores:
+        store.wait()
 
 
 def device_of(space, high, x, core):
@@ -381,12 +493,13 @@
                     before = device_of((space - 1) % slabs, high, x, core)
                     upwind.append((me, after if high else before))
                     downwind.append((me, before if high else after))
-                    next_slab = (space + (x == 3)) % slabs
-                    x_up.append((me, device_of(next_slab, high, (x + 1) % 4, core)))
-                    quarter = (2 * high + (core ^ high) + 1) % 4
-                    y_up.append(
-                        (me, device_of(space, quarter // 2, x, (quarter % 2) ^ (quarter // 2)))
+                    quarter = 2 * high + (core ^ high)
+                    next_slab = (space + (quarter == 3)) % slabs
+                    quarter = (quarter + 1) % 4
+                    x_up.append(
+                        (me, device_of(next_slab, quarter // 2, x, (quarter % 2) ^ (quarter // 2)))
                     )
+                    y_up.append((me, device_of(space, high, (x + 1) % 4, core)))
     back = lambda pairs: [(target, source) for source, target in pairs]
     return upwind, downwind, x_up, back(x_up), y_up, back(y_up)
 
@@ -396,22 +509,24 @@
     rank_space = lax.axis_index("space")
     both = ("space", "vel")
     upwind, downwind, x_up, x_down, y_up, y_down = steps_of(lax.axis_size("space"))
-    project, mix, expand, w, u = tables()
+    project, mix, expand, w = tables()
     consts = (jnp.asarray(project), jnp.asarray(mix), jnp.asarray(expand), jnp.asarray(w))
-    maps = (map_a, map_b, map_c)
-    u = jnp.asarray(u)
     vx = (rank_vel.astype(jnp.float32) - 0.5 * (GX - 1)) * SPACING
     speed = (COURANT * jnp.abs(vx)).reshape(1)
     forward = rank_vel >= GROUPS // 2
     sign = jnp.where(forward, 1, -1).astype(jnp.int32).reshape(1)
 
-    behind = lax.dynamic_slice_in_dim(dist, jnp.where(forward, CX - 2, 0), 2, 0)
-    ahead = lax.dynamic_slice_in_dim(dist, jnp.where(forward, 0, CX - 1), 1, 0)
+    layers = (NY, NZ, WIDTH)
+    behind, ahead = call(
+        first_halo_kernel, "first_halo", ((sign, SMEM), (dist, HBM)),
+        (((2,) + layers, jnp.bfloat16, VMEM), ((1,) + layers, jnp.bfloat16, VMEM)),
+        scratch=(VMEM((3,) + layers, jnp.float32), DMA((2,))), limit=ALL_VMEM,
+    )
     behind = lax.ppermute(behind, both, upwind)
     ahead = lax.ppermute(ahead, both, downwind)
 
-    high, x_quarter, core = rank_vel // 8, rank_vel // 2 % 4, rank_vel % 2
-    y_quarter = 2 * high + (core + high) % 2
+    high, y_quarter, core = rank_vel // 8, rank_vel // 2 % 4, rank_vel % 2
+    x_quarter = 2 * high + (core + high) % 2
     rate = lax.dynamic_slice(relax_rate, (BX * x_quarter, BY * y_quarter, 0), (BX, BY, NZ))
     rate = rate.reshape(LAYER, 1)
     own = lax.dynamic_index_in_dim(kinetic_count, rank_space, 1, False)
@@ -422,36 +537,56 @@
     masks = jnp.any(listed[:, None, :] == cell[None, :, None], axis=2, keepdims=True)
     masks = masks.astype(jnp.float32)
 
-    state = jax.ShapeDtypeStruct((CX, NY, NZ, WIDTH), jnp.float32)
-    wide = jax.ShapeDtypeStruct((GROUPS, LAYER, WIDTH), jnp.float32)
-    narrow = jax.ShapeDtypeStruct((GROUPS, LAYER, WIDTH), jnp.bfloat16)
-    halo = jax.ShapeDtypeStruct((GROUPS + GROUPS // 2, LINE, WIDTH), jnp.bfloat16)
-    hidden = (pltpu.VMEM((LAYER, RANK), jnp.bfloat16),)
-
-    (part,) = call(first_yz_kernel, "first_yz", (dist, u), (state,), flops=12_000_000)
+    state = ((CX,) + layers, jnp.float32, VMEM)
+    wide = (GROUPS, LAYER, WIDTH)
+    halo = (GROUPS + GROUPS // 2, LINE, WIDTH)
+    half = jnp.bfloat16
+    hidden = VMEM((LAYER, RANK), half)
+
+    f, part = call(
+        first_yz_kernel, "first_yz", ((dist, HBM),), (state, state),
+        scratch=(DMA((CX // 2,)),), flops=12_000_000,
+    )
     (rows,) = call(
-        first_x_kernel, "first_x", (sign, speed, dist, part, behind, ahead), (narrow,), 2,
-        flops=6_000_000,
+        first_x_kernel, "first_x",
+        ((sign, SMEM), (speed, SMEM), (f, VMEM), (part, VMEM), (behind, VMEM), (ahead, VMEM)),
+        ((wide, half, HBM),), scratch=(VMEM(wide, half), DMA((GROUPS,))), flops=6_000_000, limit=X_VMEM,
     )
     gathered = lax.all_to_all(rows, "vel", split_axis=0, concat_axis=0, tiled=True)
+    held = (map_a, map_b, map_c) + consts[:3]
     f, up_x, down_x, up_y, down_y = call(
-        first_collide_kernel, "first_collide", (gathered,) + maps + consts + (rate, masks[0]),
-        (wide, halo, halo, halo, halo), scratch=hidden, flops=2_500_000_000, limit=LIMIT,
-    )
+        first_collide_kernel, "first_collide",
+        ((gathered, HBM),) + tuple((o, HBM) for o in held)
+        + ((consts[3], VMEM), (rate, VMEM), (masks[0], VMEM)),
+        ((wide, jnp.float32, HBM),) + ((halo, half, HBM),) * 4,
+        scratch=(VMEM(wide, half),) + tuple(VMEM(o.shape, o.dtype) for o in held)
+        + (hidden, VMEM(wide, jnp.float32)) + (VMEM(halo, half),) * 4 + (DMA((16,)), DMA((32,))),
+        flops=2_500_000_000, limit=ALL_VMEM,
+    )
+    y_below = lax.ppermute(up_y, both, y_up)
+    y_above = lax.ppermute(down_y, both, y_down)
     x_below = lax.ppermute(up_x, both, x_up)
     x_above = lax.ppermute(down_x, both, x_down)
-    y_below = lax.ppermute(up_y, both, y_up)
-    y_above = lax.ppermute(down_y, both, y_down)
-    (part,) = call(second_z_kernel, "second_z", (f, u), (wide,), flops=6_000_000)
+    f, part = call(
+        second_z_kernel, "second_z", ((f, HBM),), ((wide, jnp.float32, VMEM),) * 2,
+        scratch=(DMA((GROUPS // 2,)),), flops=6_000_000,
+    )
     (moved,) = call(
-        second_xy_kernel, "second_xy", (f, part, x_below, x_above, y_below, y_above, u), (wide,),
-        flops=12_000_000,
+        second_xy_kernel, "second_xy",
+        tuple((o, VMEM) for o in (f, part, x_below, x_above, y_below, y_above)),
+        ((wide, jnp.float32, VMEM),), flops=12_000_000,
     )
     (result,) = call(
-        second_collide_kernel, "second_collide", (moved,) + maps + consts + (rate, masks[1]),
-        (narrow,), scratch=hidden, flops=2_500_000_000, limit=LIMIT,
-    )
-    return place(lax.all_to_all(result, "vel", split_axis=0, concat_axis=0, tiled=True))
+        second_collide_kernel, "second_collide",
+        ((moved, VMEM),) + tuple((o, VMEM) for o in held + (consts[3], rate, masks[1])),
+        ((wide, half, VMEM),), scratch=(hidden,), flops=2_500_000_000, limit=12 << 20,
+    )
+    pieces = lax.all_to_all(result, "vel", split_axis=0, concat_axis=0, tiled=True)
+    (out,) = call(
+        place_kernel, "place", ((pieces, VMEM),), (((CX,) + layers, jnp.float32, HBM),),
+        scratch=(VMEM((CX,) + layers, jnp.float32), DMA((4,))),
+    )
+    return out
 
 
 def solution(mesh):

time: 110 us -> 95.8 us (0.87)
  local copies, waits for them, and re-layouts: 18.2 us -> 5.55 us
  Pallas kernels: 21.2 us -> 25.9 us
  starting transfers between devices: 20.2 us -> 16.8 us
  waiting for transfers between devices: 22.5 us -> 21.1 us
    unnamed x46 -> x26, local copies, waits for them, and re-layouts: 14.4 us -> 3.66 us
    ppermute x1, waiting for transfers between devices: 0.01 us -> 5.6 us  [body(): x_above = lax.ppermute(down_x, both, x_down)]
    ppermute x1, starting transfers between devices: 5.68 us -> 0.54 us  [body(): x_above = lax.ppermute(down_x, both, x_down)]
    pallas_call x7 -> x8, Pallas kernels: 21.2 us -> 25.9 us  [call(): pl.pallas_call(kernel, out_shape=tuple(shapes), in_specs=[pl.BlockSpec(me...]
    ppermute x1, waiting for transfers between devices: 4.16 us -> 0.01 us  [body(): x_below = lax.ppermute(up_x, both, x_up)]
    ppermute x1, waiting for transfers between devices: 2.88 us -> 0.01 us  [body(): y_above = lax.ppermute(down_y, both, y_down)]
    dynamic_slice x2 -> x0, local copies, waits for them, and re-layouts: 1.92 us -> none  [the longest x1 1 us: body(): behind = lax.dynamic_slice_in_dim(dist, jnp.where(forward, CX - 2, 0), 2, 0)]
    ppermute x1, starting transfers between devices: 1.01 us -> 2.67 us  [body(): y_above = lax.ppermute(down_y, both, y_down)]
  transfers between devices with their start and end apart: 7 -> 7, of which waited for: 4 -> 3; matrix products, arithmetic and copies ran while one was open for 4% -> 3% of each run, Pallas kernels for 4% -> 5%
where the time goes in v2:
time: 95.8 us; the launch traced here: 95.4 us
  Pallas kernels  25.9 us (27%)
  blocking collectives  24.4 us (25%)
  waiting for transfers between devices  21.1 us (22%)
  starting transfers between devices  16.8 us (18%)
  local copies, waits for them, and re-layouts  5.55 us (6%)
  other arithmetic  1.29 us (1%)
    pallas_call x8, Pallas kernels, call(): pl.pallas_call(kernel, out_shape=tuple(shapes), in_specs=[pl.BlockSpec(me...  25.9 us
    all_to_all x1, blocking collectives, body(): lax.all_to_all(result, 'vel', split_axis=0, concat_axis=0, tiled=True)  24.4 us
    all_to_all x1, waiting for transfers between devices, body(): lax.all_to_all(rows, 'vel', split_axis=0, concat_axis=0, tiled=True)  15.3 us
    all_to_all x1, starting transfers between devices, body(): lax.all_to_all(rows, 'vel', split_axis=0, concat_axis=0, tiled=True)  7.54 us
    ppermute x1, starting transfers between devices, body(): behind = lax.ppermute(behind, both, upwind)  5.67 us
    ppermute x1, waiting for transfers between devices, body(): x_above = lax.ppermute(down_x, both, x_down)  5.6 us
    unnamed x26, local copies, waits for them, and re-layouts  3.66 us
    ppermute x1, starting transfers between devices, body(): y_above = lax.ppermute(down_y, both, y_down)  2.67 us
  transfers between devices with their start and end apart: 7, of which 3 were waited for; matrix products, arithmetic and copies ran while one was open for 3% of the time, Pallas kernels for 5%

profile of v2, /device:TPU:1, one launch (start us, length us, event | category | flops | bytes accessed | tf_op | source)
XLA Modules:
  0.0 95.4 jit_solution(2266836884640504339)
XLA Ops:
  0.0 1.7 %first_halo.1 = (bf16[2,16,16,128]{3,2,1,0:T(8,128)(2,1)}, bf16[1,16,16,128]{3,2,1,0:T(8,128)(2,1)}) custom-call(s32[1]{0:T(128)} %bitcast.sign_ref, f32[16,16,16,128]{3,2,1,0:T(8,128)} %dist_ref.3), custom_call_target="tpu_custom_call" | custom-call | bytes 2293764 | tf_op jit(solution)/shard_map/first_halo/pallas_call | solution.py:81
  1.7 5.7 %collective-permute-start = (bf16[2,16,16,128]{3,2,1,0:T(8,128)(2,1)}, bf16[2,16,16,128]{3,2,1,0:T(8,128)(2,1)S(1)}, u32[]{:S(2)}, u32[]{:S(2)}) collective-permute-start(bf16[2,16,16,128]{3,2,1,0:T(8,128)(2,1)} %get-tuple-element.18), channel_id=1, source_target_pairs={{0,112},{1,113},{2,114},{3,115},{4,116},{5,117},{6,118},{7,119},{8... | collective-permute-start | bytes 393224 | tf_op jit(solution)/shard_map/ppermute | solution.py:525
  7.4 0.8 reshape.50.rate_ref
  8.2 0.2 dynamic-slice_reduce_fusion
  8.3 1.6 %copy-done.4 = f32[16,16,16,128]{3,2,1,0:T(8,128)S(1)} copy-done((f32[16,16,16,128]{3,2,1,0:T(8,128)S(1)}, f32[16,16,16,128]{3,2,1,0:T(8,128)}, u32[]{:S(2)}) %copy-start.4) | copy-done | bytes 2097176
  9.9 2.7 %first_yz.1 = (f32[16,16,16,128]{3,2,1,0:T(8,128)S(1)}, f32[16,16,16,128]{3,2,1,0:T(8,128)S(1)}) custom-call(f32[16,16,16,128]{3,2,1,0:T(8,128)S(1)} %copy-done.4), custom_call_target="tpu_custom_call" | custom-call | flops 12000000 | bytes 6291456 | tf_op jit(solution)/shard_map/first_yz/pallas_call | solution.py:81
  12.6 0.2 collective-permute-done.1.ahead_ref
  12.8 3.7 %first_x.1 = bf16[16,256,128]{2,1,0:T(8,128)(2,1)} custom-call(s32[1]{0:T(128)} %bitcast.sign_ref, f32[1]{0:T(128)} %bitcast.1.speed_ref, f32[16,16,16,128]{3,2,1,0:T(8,128)S(1)} %get-tuple-element.16.f_ref, f32[16,16,16,128]{3,2,1,0:T(8,128)S(1)} %get-tuple-element.17.part_ref, bf16[2,16,16,128]{3,2,1,0:T(8,128)(2,1)S(1)} %collective-permute-done.behind_ref, ...), custom_call_target="tpu_custom_call" | custom-call | flops 6000000 | bytes 5439496 | tf_op jit(solution)/shard_map/first_x/pallas_call | solution.py:81
  16.6 7.5 %all-to-all-start = ((bf16[16,256,128]{2,1,0:T(8,128)(2,1)}), bf16[16,256,128]{2,1,0:T(8,128)(2,1)}, u32[]{:S(2)}, u32[]{:S(2)}) async-start(bf16[16,256,128]{2,1,0:T(8,128)(2,1)} %first_x.1), calls=%async_computation | async-start | bytes 2097152 | tf_op jit(solution)/shard_map/all_to_all | solution.py:555
  24.2 1.2 %compare_reduce_fusion = pred[2,256]{1,0:T(4,128)(4,1)S(1)} fusion(s32[2,4096]{1,0:T(2,128)S(1)} %compare_select_fusion, s32[256]{0:T(256)S(1)} %fusion.3), kind=kLoop, calls=%fused_computation | loop fusion | flops 4193792 | bytes 34304 | tf_op jit(solution)/shard_map/reduce_or | solution.py:537
  25.4 0.8 copy.17.mask_ref
  26.2 15.3 %all-to-all-done.rows_hbm = bf16[16,256,128]{2,1,0:T(8,128)(2,1)} async-done(((bf16[16,256,128]{2,1,0:T(8,128)(2,1)}), bf16[16,256,128]{2,1,0:T(8,128)(2,1)}, u32[]{:S(2)}, u32[]{:S(2)}) %all-to-all-start) | async-done | bytes 1048608 | tf_op jit(solution)/shard_map/all_to_all | solution.py:555
  41.6 8.7 %first_collide.1 = (f32[16,256,128]{2,1,0:T(8,128)}, bf16[24,64,128]{2,1,0:T(8,128)(2,1)}, bf16[24,64,128]{2,1,0:T(8,128)(2,1)}, bf16[24,64,128]{2,1,0:T(8,128)(2,1)}, bf16[24,64,128]{2,1,0:T(8,128)(2,1)}) custom-call(bf16[16,256,128]{2,1,0:T(8,128)(2,1)} %all-to-all-done.rows_hbm, bf16[2048,768]{1,0:T(8,128)(2,1)} %a_ref.1, bf16[2048,768]{1,0:T(8,128)(2,1)} %b_ref.1, ...), custom_call_target="tpu_custom_call" | custom-call | flops 2500000000 | bytes 15280128 | tf_op jit(solution)/shard_map/first_collide/pallas_call | solution.py:81
  50.2 0.4 collective-permute-start.2
  50.6 0.5 collective-permute-start.3
  51.1 2.7 %collective-permute-start.5 = (bf16[24,64,128]{2,1,0:T(8,128)(2,1)}, bf16[24,64,128]{2,1,0:T(8,128)(2,1)S(1)}, u32[]{:S(2)}, u32[]{:S(2)}) collective-permute-start(bf16[24,64,128]{2,1,0:T(8,128)(2,1)} %get-tuple-element.26), channel_id=1, source_target_pairs={{2,0},{3,1},{4,2},{5,3},{6,4},{7,5},{0,6},{1,7},{10,8},{11,9},{12,... | collective-permute-start | bytes 1179656 | tf_op jit(solution)/shard_map/ppermute | solution.py:567
  54.0 1.6 %copy-done.7 = f32[16,256,128]{2,1,0:T(8,128)S(1)} copy-done((f32[16,256,128]{2,1,0:T(8,128)S(1)}, f32[16,256,128]{2,1,0:T(8,128)}, u32[]{:S(2)}) %copy-start.7) | copy-done | bytes 2097176
  55.6 1.7 %second_z.1 = (f32[16,256,128]{2,1,0:T(8,128)S(1)}, f32[16,256,128]{2,1,0:T(8,128)S(1)}) custom-call(f32[16,256,128]{2,1,0:T(8,128)S(1)} %copy-done.7), custom_call_target="tpu_custom_call" | custom-call | flops 6000000 | bytes 6291456 | tf_op jit(solution)/shard_map/second_z/pallas_call | solution.py:81
  57.3 5.6 %collective-permute-done.3.x_above_ref = bf16[24,64,128]{2,1,0:T(8,128)(2,1)S(1)} collective-permute-done((bf16[24,64,128]{2,1,0:T(8,128)(2,1)}, bf16[24,64,128]{2,1,0:T(8,128)(2,1)S(1)}, u32[]{:S(2)}, u32[]{:S(2)}) %collective-permute-start.3) | collective-permute-done | bytes 393248 | tf_op jit(solution)/shard_map/ppermute | solution.py:569
  62.9 2.4 %second_xy.1.moved_ref = f32[16,256,128]{2,1,0:T(8,128)S(1)} custom-call(f32[16,256,128]{2,1,0:T(8,128)S(1)} %get-tuple-element.21.f_ref, f32[16,256,128]{2,1,0:T(8,128)S(1)} %get-tuple-element.22.part_ref, bf16[24,64,128]{2,1,0:T(8,128)(2,1)S(1)} %collective-permute-done.2.x_below_ref, bf16[24,64,128]{2,1,0:T(8,128)(2,1)S(1)} %collective-permute-done.3.x_above_ref, ...), custom_call_target="tpu_custom_call" | custom-call | flops 12000000 | bytes 7864320 | tf_op jit(solution)/shard_map/second_xy/pallas_call | solution.py:81
  65.4 0.4 copy-done.2
  65.8 3.7 %second_collide.1 = bf16[16,256,128]{2,1,0:T(8,128)(2,1)S(1)} custom-call(f32[16,256,128]{2,1,0:T(8,128)S(1)} %second_xy.1.moved_ref, bf16[2048,768]{1,0:T(8,128)(2,1)S(1)} %copy-done.1, bf16[2048,768]{1,0:T(8,128)(2,1)S(1)} %copy-done.2, bf16[768,2048]{1,0:T(8,128)(2,1)S(1)} %copy-done.3, bf16[2048,128]{1,0:T(8,128)(2,1)S(1)} %copy-done.5, ...), custom_call_target="tpu_custom_call" | custom-call | flops 2500000000 | bytes 13707264 | tf_op jit(solution)/shard_map/second_collide/pallas_call | solution.py:81
  69.5 24.4 %all_to_all.10.in_ref = bf16[16,256,128]{2,1,0:T(8,128)(2,1)S(1)} all-to-all(bf16[16,256,128]{2,1,0:T(8,128)(2,1)S(1)} %second_collide.1), channel_id=1, replica_groups=mesh['space'=8,'vel'=16] {'vel'}, dimensions={0} | all-to-all | bytes 2097152 | tf_op jit(solution)/shard_map/all_to_all | solution.py:584
  93.9 1.4 %place.1 = f32[16,16,16,128]{3,2,1,0:T(8,128)} custom-call(bf16[16,256,128]{2,1,0:T(8,128)(2,1)S(1)} %all_to_all.10.in_ref), custom_call_target="tpu_custom_call" | custom-call | bytes 3145728 | tf_op jit(solution)/shard_map/place/pallas_call | solution.py:81
  (35 shorter events, 0.4 us)
Async XLA Ops:
  0.0 7.4 %copy-start = (f32[16,16,16]{2,1,0:T(8,128)S(1)}, f32[16,16,16]{2,1,0:T(8,128)}, u32[]{:S(2)}) copy-start(f32[16,16,16]{2,1,0:T(8,128)} %param.12) | copy-start | bytes 49156
  0.0 8.2 %copy-start.12 = (s32[2,8]{1,0:T(2,128)S(1)}, s32[2,8]{1,0:T(2,128)}, u32[]{:S(2)}) copy-start(s32[2,8]{1,0:T(2,128)} %param.14) | copy-start | bytes 196
  1.7 11.1 %collective-permute-start = (bf16[2,16,16,128]{3,2,1,0:T(8,128)(2,1)}, bf16[2,16,16,128]{3,2,1,0:T(8,128)(2,1)S(1)}, u32[]{:S(2)}, u32[]{:S(2)}) collective-permute-start(bf16[2,16,16,128]{3,2,1,0:T(8,128)(2,1)} %get-tuple-element.18), channel_id=1, source_target_pairs={{0,112},{1,113},{2,114},{3,115},{4,116},{5,117},{6,118},{7,119},{8... | collective-permute-start | bytes 393224 | tf_op jit(solution)/shard_map/ppermute | solution.py:525
  7.4 5.4 %collective-permute-start.1 = (bf16[1,16,16,128]{3,2,1,0:T(8,128)(2,1)}, bf16[1,16,16,128]{3,2,1,0:T(8,128)(2,1)S(1)}, u32[]{:S(2)}, u32[]{:S(2)}) collective-permute-start(bf16[1,16,16,128]{3,2,1,0:T(8,128)(2,1)} %get-tuple-element.19), channel_id=1, source_target_pairs={{0,16},{1,17},{2,18},{3,19},{4,20},{5,21},{6,22},{7,23},{8,120},{9... | collective-permute-start | bytes 196616 | tf_op jit(solution)/shard_map/ppermute | solution.py:526
  8.3 1.6 %copy-start.4 = (f32[16,16,16,128]{3,2,1,0:T(8,128)S(1)}, f32[16,16,16,128]{3,2,1,0:T(8,128)}, u32[]{:S(2)}) copy-start(f32[16,16,16,128]{3,2,1,0:T(8,128)} %dist_ref.3) | copy-start | bytes 6291460
  16.5 7.6 %copy-start.11 = (s32[2,4096]{1,0:T(2,128)S(1)}, s32[2,4096]{1,0:T(2,128)}, u32[]{:S(2)}) copy-start(s32[2,4096]{1,0:T(2,128)} %param.13) | copy-start | bytes 98308
  16.6 25.0 %all-to-all-start = ((bf16[16,256,128]{2,1,0:T(8,128)(2,1)}), bf16[16,256,128]{2,1,0:T(8,128)(2,1)}, u32[]{:S(2)}, u32[]{:S(2)}) async-start(bf16[16,256,128]{2,1,0:T(8,128)(2,1)} %first_x.1), calls=%async_computation | async-start | bytes 2097152 | tf_op jit(solution)/shard_map/all_to_all | solution.py:555
  41.6 23.8 %copy-start.6 = (bf16[128,2048]{1,0:T(8,128)(2,1)S(1)}, bf16[128,2048]{1,0:T(8,128)(2,1)}, u32[]{:S(2)}) copy-start(bf16[128,2048]{1,0:T(8,128)(2,1)} %constant.117.clone.expand_hbm.expand_ref) | copy-start | bytes 1572868
  41.6 23.8 %copy-start.8 = (f32[256,1]{1,0:T(8,128)S(1)}, f32[256,1]{1,0:T(8,128)}, u32[]{:S(2)}) copy-start(f32[256,1]{1,0:T(8,128)} %reshape.50.rate_ref) | copy-start | bytes 3076
  41.6 23.8 %copy-start.9 = (f32[128,128]{1,0:T(8,128)S(1)}, f32[128,128]{1,0:T(8,128)}, u32[]{:S(2)}) copy-start(f32[128,128]{1,0:T(8,128)} %constant.116.clone.mix_hbm.mix_ref) | copy-start | bytes 196612
  41.6 23.8 %copy-start.10 = (f32[1,2048]{1,0:T(1,128)S(1)}, f32[1,2048]{1,0:T(1,128)}, u32[]{:S(2)}) copy-start(f32[1,2048]{1,0:T(1,128)} %constant.118.clone.w_ref) | copy-start | bytes 24580
  50.2 7.0 %collective-permute-start.2 = (bf16[24,64,128]{2,1,0:T(8,128)(2,1)}, bf16[24,64,128]{2,1,0:T(8,128)(2,1)S(1)}, u32[]{:S(2)}, u32[]{:S(2)}) collective-permute-start(bf16[24,64,128]{2,1,0:T(8,128)(2,1)} %get-tuple-element.23), channel_id=1, source_target_pairs={{0,1},{1,9},{2,3},{3,11},{4,5},{5,13},{6,7},{7,15},{8,16},{9,8},{1... | collective-permute-start | bytes 1179656 | tf_op jit(solution)/shard_map/ppermute | solution.py:568
  50.6 12.3 %collective-permute-start.3 = (bf16[24,64,128]{2,1,0:T(8,128)(2,1)}, bf16[24,64,128]{2,1,0:T(8,128)(2,1)S(1)}, u32[]{:S(2)}, u32[]{:S(2)}) collective-permute-start(bf16[24,64,128]{2,1,0:T(8,128)(2,1)} %get-tuple-element.24), channel_id=1, source_target_pairs={{1,0},{9,1},{3,2},{11,3},{5,4},{13,5},{7,6},{15,7},{16,8},{8,9},{1... | collective-permute-start | bytes 1179656 | tf_op jit(solution)/shard_map/ppermute | solution.py:569
  51.1 11.8 %collective-permute-start.4 = (bf16[24,64,128]{2,1,0:T(8,128)(2,1)}, bf16[24,64,128]{2,1,0:T(8,128)(2,1)S(1)}, u32[]{:S(2)}, u32[]{:S(2)}) collective-permute-start(bf16[24,64,128]{2,1,0:T(8,128)(2,1)} %get-tuple-element.25), channel_id=1, source_target_pairs={{0,2},{1,3},{2,4},{3,5},{4,6},{5,7},{6,0},{7,1},{8,10},{9,11},{10,... | collective-permute-start | bytes 1179656 | tf_op jit(solution)/shard_map/ppermute | solution.py:566
  51.1 11.8 %collective-permute-start.5 = (bf16[24,64,128]{2,1,0:T(8,128)(2,1)}, bf16[24,64,128]{2,1,0:T(8,128)(2,1)S(1)}, u32[]{:S(2)}, u32[]{:S(2)}) collective-permute-start(bf16[24,64,128]{2,1,0:T(8,128)(2,1)} %get-tuple-element.26), channel_id=1, source_target_pairs={{2,0},{3,1},{4,2},{5,3},{6,4},{7,5},{0,6},{1,7},{10,8},{11,9},{12,... | collective-permute-start | bytes 1179656 | tf_op jit(solution)/shard_map/ppermute | solution.py:567
  54.0 1.6 %copy-start.7 = (f32[16,256,128]{2,1,0:T(8,128)S(1)}, f32[16,256,128]{2,1,0:T(8,128)}, u32[]{:S(2)}) copy-start(f32[16,256,128]{2,1,0:T(8,128)} %get-tuple-element.20.f_hbm) | copy-start | bytes 6291460
  55.6 9.8 %copy-start.3 = (bf16[768,2048]{1,0:T(8,128)(2,1)S(1)}, bf16[768,2048]{1,0:T(8,128)(2,1)}, u32[]{:S(2)}) copy-start(bf16[768,2048]{1,0:T(8,128)(2,1)} %c_ref.1) | copy-start | bytes 9437188
  62.9 2.5 %copy-start.1 = (bf16[2048,768]{1,0:T(8,128)(2,1)S(1)}, bf16[2048,768]{1,0:T(8,128)(2,1)}, u32[]{:S(2)}) copy-start(bf16[2048,768]{1,0:T(8,128)(2,1)} %a_ref.1) | copy-start | bytes 9437188
  62.9 2.8 %copy-start.2 = (bf16[2048,768]{1,0:T(8,128)(2,1)S(1)}, bf16[2048,768]{1,0:T(8,128)(2,1)}, u32[]{:S(2)}) copy-start(bf16[2048,768]{1,0:T(8,128)(2,1)} %b_ref.1) | copy-start | bytes 9437188
  62.9 2.9 %copy-start.5 = (bf16[2048,128]{1,0:T(8,128)(2,1)S(1)}, bf16[2048,128]{1,0:T(8,128)(2,1)}, u32[]{:S(2)}) copy-start(bf16[2048,128]{1,0:T(8,128)(2,1)} %constant.115.clone.project_hbm.project_ref) | copy-start | bytes 1572868

commit v3 on v2

--- a/solution.py
+++ b/solution.py
@@ -67,7 +67,6 @@
 
 
 ALL_VMEM = 62 << 20
-X_VMEM = 8 << 20
 HBM = pltpu.HBM
 VMEM = pltpu.VMEM
 SMEM = pltpu.SMEM
@@ -175,6 +174,13 @@
     s = sign_ref[0]
     ux = speed_ref[0]
     forward = s > 0
+    layers = [jnp.where(forward, k, CX - 1 - k) for k in range(CX)]
+    starts = [(x % BX) * LINE for x in layers[:BX]]
+    owners = []
+    for k in range(4):
+        quarter = jnp.where(forward, k, 3 - k)
+        high = quarter // 2
+        owners.append(high * (GROUPS // 2) + (quarter + high) % 2)
 
     def put(target):
         return pltpu.make_async_copy(rows_ref.at[target], out_ref.at[target], sems.at[target])
@@ -190,18 +196,15 @@
                 return behind_ref[jnp.where(forward, 1, 0), y].astype(jnp.float32)
             if k == CX:
                 return ahead_ref[0, y].astype(jnp.float32)
-            return f_ref[jnp.where(forward, k, CX - 1 - k), y]
+            return f_ref[layers[k], y]
 
         face_before = upwind_face(at(-2), at(-1), at(0))
         for k in range(CX):
-            x = jnp.where(forward, k, CX - 1 - k)
             face = upwind_face(at(k - 1), at(k), at(k + 1))
-            result = part_ref[x, y] - ux * (face - face_before)
+            result = part_ref[layers[k], y] - ux * (face - face_before)
             face_before = face
-            start = pl.multiple_of((x % BX) * LINE + inner, NZ)
-            high = x // (2 * BX)
-            core = (x // BX + high) % 2
-            target = high * (GROUPS // 2) + quarter * 2 + core
+            start = pl.multiple_of(starts[k % BX] + inner, NZ)
+            target = owners[k // BX] + quarter * 2
             rows_ref[target, pl.ds(start, NZ), :] = result.astype(jnp.bfloat16)
 
     def lines(quarter, carry):
@@ -220,11 +223,7 @@
         put(target).wait()
 
 
-def collision_terms(
-    rows, a_ref, b_ref, c_ref, project_ref, mix_ref, expand_ref, w_ref, hidden_ref, arrive
-):
-    arrive(0)
-    moments = jnp.dot(rows, project_ref[...], preferred_element_type=jnp.float32)
+def split_coefficients(moments, mix_ref):
     coeffs = jnp.dot(
         moments, mix_ref[...], precision=lax.Precision.HIGHEST, preferred_element_type=jnp.float32
     )
@@ -233,22 +232,18 @@
     rest = coeffs - high
     middle = rest.astype(jnp.bfloat16).astype(jnp.float32)
     split = jnp.where(lane < 8, high, jnp.where(lane < 16, middle, rest - middle))
-    split = split.astype(jnp.bfloat16)
-    for n in range(RANK // 256):
-        cols = slice(256 * n, 256 * (n + 1))
-        arrive(1 + n)
-        first = jnp.dot(rows, a_ref[:, cols], preferred_element_type=jnp.float32)
-        second = jnp.dot(rows, b_ref[:, cols], preferred_element_type=jnp.float32)
-        hidden_ref[:, cols] = (first * second).astype(jnp.bfloat16)
-    hidden = hidden_ref[...]
+    return split.astype(jnp.bfloat16)
+
+
+def outcome(hidden, split, c_ref, expand_ref, w_ref, arrive=None):
     for n in range(NV // 256):
         cols = slice(256 * n, 256 * (n + 1))
-        if n % 2 == 0:
-            arrive(4 + n // 2)
+        if arrive is not None and n % 2 == 0:
+            arrive[n // 2].wait()
+        poly = jnp.dot(split, expand_ref[:, cols], preferred_element_type=jnp.float32)
+        equilibrium = poly * w_ref[:, cols]
         collision = jnp.dot(hidden, c_ref[:, cols], preferred_element_type=jnp.float32)
         collision = collision.astype(jnp.bfloat16).astype(jnp.float32)
-        poly = jnp.dot(split, expand_ref[:, cols], preferred_element_type=jnp.float32)
-        equilibrium = poly * w_ref[:, cols]
         for half in range(2):
             part = slice(WIDTH * half, WIDTH * (half + 1))
             yield 2 * n + half, collision[:, part], equilibrium[:, part]
@@ -258,29 +253,54 @@
     rows_hbm, a_hbm, b_hbm, c_hbm, project_hbm, mix_hbm, expand_hbm, w_ref, rate_ref, mask_ref,
     f_out, x_up_out, x_down_out, y_up_out, y_down_out,
     rows_ref, a_ref, b_ref, c_ref, project_ref, mix_ref, expand_ref, hidden_ref,
-    f_ref, x_up_ref, x_down_ref, y_up_ref, y_down_ref, in_sems, out_sems,
+    first_ref, second_ref, f_ref, x_up_ref, x_down_ref, y_up_ref, y_down_ref, in_sems, out_sems,
 ):
-    pieces = [[(rows_hbm, rows_ref), (project_hbm, project_ref), (mix_hbm, mix_ref)]]
-    for n in range(RANK // 256):
-        cols = slice(256 * n, 256 * (n + 1))
-        pieces.append([(a_hbm.at[:, cols], a_ref.at[:, cols]), (b_hbm.at[:, cols], b_ref.at[:, cols])])
-    pieces.append([(expand_hbm, expand_ref)])
-    for n in range(4):
-        cols = slice(512 * n, 512 * (n + 1))
-        if n:
-            pieces.append([])
-        pieces[-1].append((c_hbm.at[:, cols], c_ref.at[:, cols]))
-    fetches, count = [], 0
-    for piece in pieces:
-        fetches.append([])
-        for source, target in piece:
-            fetches[-1].append(pltpu.make_async_copy(source, target, in_sems.at[count]))
-            fetches[-1][-1].start()
-            count += 1
-
-    def arrive(i):
-        for fetch in fetches[i]:
-            fetch.wait()
+    count = 0
+
+    def fetch(source, target, piece=None):
+        nonlocal count
+        if piece is not None:
+            source, target = source.at[piece], target.at[piece]
+        copy = pltpu.make_async_copy(source, target, in_sems.at[count])
+        copy.start()
+        count += 1
+        return copy
+
+    chunks = []
+    for k in range(4):
+        groups, depth = slice(4 * k, 4 * (k + 1)), slice(512 * k, 512 * (k + 1))
+        chunks.append(
+            [
+                fetch(rows_hbm, rows_ref, groups), fetch(a_hbm, a_ref, depth),
+                fetch(b_hbm, b_ref, depth), fetch(project_hbm, project_ref, depth),
+            ]
+        )
+    tables = [fetch(mix_hbm, mix_ref), fetch(expand_hbm, expand_ref)]
+    c_parts = [
+        fetch(c_hbm, c_ref, (slice(None), slice(512 * k, 512 * (k + 1)))) for k in range(4)
+    ]
+    moments = jnp.zeros((LAYER, WIDTH), jnp.float32)
+    for k in range(4):
+        depth = slice(512 * k, 512 * (k + 1))
+        for copy in chunks[k]:
+            copy.wait()
+        rows = jnp.concatenate([rows_ref[g] for g in range(4 * k, 4 * (k + 1))], axis=1)
+        moments += jnp.dot(rows, project_ref[depth], preferred_element_type=jnp.float32)
+        for n in range(RANK // 256):
+            cols = slice(256 * n, 256 * (n + 1))
+            first = jnp.dot(rows, a_ref[depth, cols], preferred_element_type=jnp.float32)
+            second = jnp.dot(rows, b_ref[depth, cols], preferred_element_type=jnp.float32)
+            if k:
+                first += first_ref[:, cols]
+                second += second_ref[:, cols]
+            if k < 3:
+                first_ref[:, cols] = first
+                second_ref[:, cols] = second
+            else:
+                hidden_ref[:, cols] = (first * second).astype(jnp.bfloat16)
+    for copy in tables:
+        copy.wait()
+    split = split_coefficients(moments, mix_ref)
 
     stores = []
 
@@ -292,16 +312,12 @@
         )
         stores[-1].start()
 
-    for fetch in fetches[0]:
-        fetch.wait()
-    rows = jnp.concatenate([rows_ref[g] for g in range(GROUPS)], axis=1)
     rate = jnp.broadcast_to(rate_ref[...], (LAYER, WIDTH))
     kinetic = jnp.broadcast_to(mask_ref[...], (LAYER, WIDTH)) > 0.0
     half = GROUPS // 2
     low_lane = lax.broadcasted_iota(jnp.int32, (NZ, WIDTH), 1) < WIDTH // 2
-    for g, collision, equilibrium in collision_terms(
-        rows, a_ref, b_ref, c_ref, project_ref, mix_ref, expand_ref, w_ref, hidden_ref,
-        lambda i: arrive(i) if i else None,
+    for g, collision, equilibrium in outcome(
+        hidden_ref[...], split, c_ref, expand_ref, w_ref, c_parts
     ):
         moved = rows_ref[g].astype(jnp.float32)
         change = jnp.where(kinetic, COLLIDE * collision, rate * (equilibrium - moved))
@@ -450,10 +466,14 @@
     rows = jnp.concatenate([moved_ref[g].astype(jnp.bfloat16) for g in range(GROUPS)], axis=1)
     rate = jnp.broadcast_to(rate_ref[...], (LAYER, WIDTH))
     kinetic = jnp.broadcast_to(mask_ref[...], (LAYER, WIDTH)) > 0.0
-    for g, collision, equilibrium in collision_terms(
-        rows, a_ref, b_ref, c_ref, project_ref, mix_ref, expand_ref, w_ref, hidden_ref,
-        lambda i: None,
-    ):
+    moments = jnp.dot(rows, project_ref[...], preferred_element_type=jnp.float32)
+    split = split_coefficients(moments, mix_ref)
+    for n in range(RANK // 256):
+        cols = slice(256 * n, 256 * (n + 1))
+        first = jnp.dot(rows, a_ref[:, cols], preferred_element_type=jnp.float32)
+        second = jnp.dot(rows, b_ref[:, cols], preferred_element_type=jnp.float32)
+        hidden_ref[:, cols] = (first * second).astype(jnp.bfloat16)
+    for g, collision, equilibrium in outcome(hidden_ref[...], split, c_ref, expand_ref, w_ref):
         moved = moved_ref[g]
         change = jnp.where(kinetic, COLLIDE * collision, rate * (equilibrium - moved))
         out_ref[g] = (moved + change).astype(jnp.bfloat16)
@@ -550,17 +570,18 @@
     (rows,) = call(
         first_x_kernel, "first_x",
         ((sign, SMEM), (speed, SMEM), (f, VMEM), (part, VMEM), (behind, VMEM), (ahead, VMEM)),
-        ((wide, half, HBM),), scratch=(VMEM(wide, half), DMA((GROUPS,))), flops=6_000_000, limit=X_VMEM,
+        ((wide, half, HBM),), scratch=(VMEM(wide, half), DMA((GROUPS,))), flops=6_000_000,
     )
     gathered = lax.all_to_all(rows, "vel", split_axis=0, concat_axis=0, tiled=True)
     held = (map_a, map_b, map_c) + consts[:3]
     f, up_x, down_x, up_y, down_y = call(
         first_collide_kernel, "first_collide",
-        ((gathered, HBM),) + tuple((o, HBM) for o in held)
-        + ((consts[3], VMEM), (rate, VMEM), (masks[0], VMEM)),
+        tuple((o, HBM) for o in (gathered,) + held)
+        + tuple((o, VMEM) for o in (consts[3], rate, masks[0])),
         ((wide, jnp.float32, HBM),) + ((halo, half, HBM),) * 4,
         scratch=(VMEM(wide, half),) + tuple(VMEM(o.shape, o.dtype) for o in held)
-        + (hidden, VMEM(wide, jnp.float32)) + (VMEM(halo, half),) * 4 + (DMA((16,)), DMA((32,))),
+        + (hidden, VMEM((LAYER, RANK), jnp.float32), VMEM((LAYER, RANK), jnp.float32))
+        + (VMEM(wide, jnp.float32),) + (VMEM(halo, half),) * 4 + (DMA((22,)), DMA((32,))),
         flops=2_500_000_000, limit=ALL_VMEM,
     )
     y_below = lax.ppermute(up_y, both, y_up)

time: 95.8 us -> 94.1 us (0.982)
  Pallas kernels: 25.9 us -> 24.1 us
    pallas_call x8, Pallas kernels: 25.9 us -> 24.1 us  [call(): pl.pallas_call(kernel, out_shape=tuple(shapes), in_specs=[pl.BlockSpec(me...]
where the time goes in v3:
time: 94.1 us; the launch traced here: 93.7 us
  blocking collectives  24.4 us (26%)
  Pallas kernels  24.1 us (26%)
  waiting for transfers between devices  21.1 us (22%)
  starting transfers between devices  16.8 us (18%)
  local copies, waits for them, and re-layouts  5.55 us (6%)
  other arithmetic  1.29 us (1%)
    all_to_all x1, blocking collectives, body(): lax.all_to_all(result, 'vel', split_axis=0, concat_axis=0, tiled=True)  24.4 us
    pallas_call x8, Pallas kernels, call(): pl.pallas_call(kernel, out_shape=tuple(shapes), in_specs=[pl.BlockSpec(me...  24.1 us
    all_to_all x1, waiting for transfers between devices, body(): lax.all_to_all(rows, 'vel', split_axis=0, concat_axis=0, tiled=True)  15.3 us
    all_to_all x1, starting transfers between devices, body(): lax.all_to_all(rows, 'vel', split_axis=0, concat_axis=0, tiled=True)  7.59 us
    ppermute x1, starting transfers between devices, body(): behind = lax.ppermute(behind, both, upwind)  5.67 us
    ppermute x1, waiting for transfers between devices, body(): x_above = lax.ppermute(down_x, both, x_down)  5.6 us
    unnamed x26, local copies, waits for them, and re-layouts  3.66 us
    ppermute x1, starting transfers between devices, body(): y_above = lax.ppermute(down_y, both, y_down)  2.67 us
  transfers between devices with their start and end apart: 7, of which 3 were waited for; matrix products, arithmetic and copies ran while one was open for 3% of the time, Pallas kernels for 5%

profile of v3, /device:TPU:1, one launch (start us, length us, event | category | flops | bytes accessed | tf_op | source)
XLA Modules:
  0.0 93.7 jit_solution(6889686773105512248)
XLA Ops:
  0.0 1.7 %first_halo.1 = (bf16[2,16,16,128]{3,2,1,0:T(8,128)(2,1)}, bf16[1,16,16,128]{3,2,1,0:T(8,128)(2,1)}) custom-call(s32[1]{0:T(128)} %bitcast.sign_ref, f32[16,16,16,128]{3,2,1,0:T(8,128)} %dist_ref.3), custom_call_target="tpu_custom_call" | custom-call | bytes 2293764 | tf_op jit(solution)/shard_map/first_halo/pallas_call | solution.py:80
  1.7 5.7 %collective-permute-start = (bf16[2,16,16,128]{3,2,1,0:T(8,128)(2,1)}, bf16[2,16,16,128]{3,2,1,0:T(8,128)(2,1)S(1)}, u32[]{:S(2)}, u32[]{:S(2)}) collective-permute-start(bf16[2,16,16,128]{3,2,1,0:T(8,128)(2,1)} %get-tuple-element.18), channel_id=1, source_target_pairs={{0,112},{1,113},{2,114},{3,115},{4,116},{5,117},{6,118},{7,119},{8... | collective-permute-start | bytes 393224 | tf_op jit(solution)/shard_map/ppermute | solution.py:545
  7.4 0.8 reshape.50.rate_ref
  8.2 0.2 dynamic-slice_reduce_fusion
  8.3 1.6 %copy-done.4 = f32[16,16,16,128]{3,2,1,0:T(8,128)S(1)} copy-done((f32[16,16,16,128]{3,2,1,0:T(8,128)S(1)}, f32[16,16,16,128]{3,2,1,0:T(8,128)}, u32[]{:S(2)}) %copy-start.4) | copy-done | bytes 2097176
  9.9 2.7 %first_yz.1 = (f32[16,16,16,128]{3,2,1,0:T(8,128)S(1)}, f32[16,16,16,128]{3,2,1,0:T(8,128)S(1)}) custom-call(f32[16,16,16,128]{3,2,1,0:T(8,128)S(1)} %copy-done.4), custom_call_target="tpu_custom_call" | custom-call | flops 12000000 | bytes 6291456 | tf_op jit(solution)/shard_map/first_yz/pallas_call | solution.py:80
  12.6 0.2 collective-permute-done.1.ahead_ref
  12.8 2.0 %first_x.1 = bf16[16,256,128]{2,1,0:T(8,128)(2,1)} custom-call(s32[1]{0:T(128)} %bitcast.sign_ref, f32[1]{0:T(128)} %bitcast.1.speed_ref, f32[16,16,16,128]{3,2,1,0:T(8,128)S(1)} %get-tuple-element.16.f_ref, f32[16,16,16,128]{3,2,1,0:T(8,128)S(1)} %get-tuple-element.17.part_ref, bf16[2,16,16,128]{3,2,1,0:T(8,128)(2,1)S(1)} %collective-permute-done.behind_ref, ...), custom_call_target="tpu_custom_call" | custom-call | flops 6000000 | bytes 5439496 | tf_op jit(solution)/shard_map/first_x/pallas_call | solution.py:80
  14.8 7.6 %all-to-all-start = ((bf16[16,256,128]{2,1,0:T(8,128)(2,1)}), bf16[16,256,128]{2,1,0:T(8,128)(2,1)}, u32[]{:S(2)}, u32[]{:S(2)}) async-start(bf16[16,256,128]{2,1,0:T(8,128)(2,1)} %first_x.1), calls=%async_computation | async-start | bytes 2097152 | tf_op jit(solution)/shard_map/all_to_all | solution.py:575
  22.5 1.2 %compare_reduce_fusion = pred[2,256]{1,0:T(4,128)(4,1)S(1)} fusion(s32[2,4096]{1,0:T(2,128)S(1)} %compare_select_fusion, s32[256]{0:T(256)S(1)} %fusion.3), kind=kLoop, calls=%fused_computation | loop fusion | flops 4193792 | bytes 34304 | tf_op jit(solution)/shard_map/reduce_or | solution.py:557
  23.7 0.8 copy.17.mask_ref
  24.5 15.3 %all-to-all-done.rows_hbm = bf16[16,256,128]{2,1,0:T(8,128)(2,1)} async-done(((bf16[16,256,128]{2,1,0:T(8,128)(2,1)}), bf16[16,256,128]{2,1,0:T(8,128)(2,1)}, u32[]{:S(2)}, u32[]{:S(2)}) %all-to-all-start) | async-done | bytes 1048608 | tf_op jit(solution)/shard_map/all_to_all | solution.py:575
  39.9 8.6 %first_collide.1 = (f32[16,256,128]{2,1,0:T(8,128)}, bf16[24,64,128]{2,1,0:T(8,128)(2,1)}, bf16[24,64,128]{2,1,0:T(8,128)(2,1)}, bf16[24,64,128]{2,1,0:T(8,128)(2,1)}, bf16[24,64,128]{2,1,0:T(8,128)(2,1)}) custom-call(bf16[16,256,128]{2,1,0:T(8,128)(2,1)} %all-to-all-done.rows_hbm, bf16[2048,768]{1,0:T(8,128)(2,1)} %a_ref.1, bf16[2048,768]{1,0:T(8,128)(2,1)} %b_ref.1, ...), custom_call_target="tpu_custom_call" | custom-call | flops 2500000000 | bytes 15280128 | tf_op jit(solution)/shard_map/first_collide/pallas_call | solution.py:80
  48.5 0.4 collective-permute-start.2
  48.9 0.5 collective-permute-start.3
  49.4 2.7 %collective-permute-start.5 = (bf16[24,64,128]{2,1,0:T(8,128)(2,1)}, bf16[24,64,128]{2,1,0:T(8,128)(2,1)S(1)}, u32[]{:S(2)}, u32[]{:S(2)}) collective-permute-start(bf16[24,64,128]{2,1,0:T(8,128)(2,1)} %get-tuple-element.26), channel_id=1, source_target_pairs={{2,0},{3,1},{4,2},{5,3},{6,4},{7,5},{0,6},{1,7},{10,8},{11,9},{12,... | collective-permute-start | bytes 1179656 | tf_op jit(solution)/shard_map/ppermute | solution.py:588
  52.2 1.6 %copy-done.7 = f32[16,256,128]{2,1,0:T(8,128)S(1)} copy-done((f32[16,256,128]{2,1,0:T(8,128)S(1)}, f32[16,256,128]{2,1,0:T(8,128)}, u32[]{:S(2)}) %copy-start.7) | copy-done | bytes 2097176
  53.8 1.7 %second_z.1 = (f32[16,256,128]{2,1,0:T(8,128)S(1)}, f32[16,256,128]{2,1,0:T(8,128)S(1)}) custom-call(f32[16,256,128]{2,1,0:T(8,128)S(1)} %copy-done.7), custom_call_target="tpu_custom_call" | custom-call | flops 6000000 | bytes 6291456 | tf_op jit(solution)/shard_map/second_z/pallas_call | solution.py:80
  55.6 5.6 %collective-permute-done.3.x_above_ref = bf16[24,64,128]{2,1,0:T(8,128)(2,1)S(1)} collective-permute-done((bf16[24,64,128]{2,1,0:T(8,128)(2,1)}, bf16[24,64,128]{2,1,0:T(8,128)(2,1)S(1)}, u32[]{:S(2)}, u32[]{:S(2)}) %collective-permute-start.3) | collective-permute-done | bytes 393248 | tf_op jit(solution)/shard_map/ppermute | solution.py:590
  61.2 2.4 %second_xy.1.moved_ref = f32[16,256,128]{2,1,0:T(8,128)S(1)} custom-call(f32[16,256,128]{2,1,0:T(8,128)S(1)} %get-tuple-element.21.f_ref, f32[16,256,128]{2,1,0:T(8,128)S(1)} %get-tuple-element.22.part_ref, bf16[24,64,128]{2,1,0:T(8,128)(2,1)S(1)} %collective-permute-done.2.x_below_ref, bf16[24,64,128]{2,1,0:T(8,128)(2,1)S(1)} %collective-permute-done.3.x_above_ref, ...), custom_call_target="tpu_custom_call" | custom-call | flops 12000000 | bytes 7864320 | tf_op jit(solution)/shard_map/second_xy/pallas_call | solution.py:80
  63.6 0.4 copy-done.2
  64.1 3.7 %second_collide.1 = bf16[16,256,128]{2,1,0:T(8,128)(2,1)S(1)} custom-call(f32[16,256,128]{2,1,0:T(8,128)S(1)} %second_xy.1.moved_ref, bf16[2048,768]{1,0:T(8,128)(2,1)S(1)} %copy-done.1, bf16[2048,768]{1,0:T(8,128)(2,1)S(1)} %copy-done.2, bf16[768,2048]{1,0:T(8,128)(2,1)S(1)} %copy-done.3, bf16[2048,128]{1,0:T(8,128)(2,1)S(1)} %copy-done.5, ...), custom_call_target="tpu_custom_call" | custom-call | flops 2500000000 | bytes 13707264 | tf_op jit(solution)/shard_map/second_collide/pallas_call | solution.py:80
  67.8 24.4 %all_to_all.10.in_ref = bf16[16,256,128]{2,1,0:T(8,128)(2,1)S(1)} all-to-all(bf16[16,256,128]{2,1,0:T(8,128)(2,1)S(1)} %second_collide.1), channel_id=1, replica_groups=mesh['space'=8,'vel'=16] {'vel'}, dimensions={0} | all-to-all | bytes 2097152 | tf_op jit(solution)/shard_map/all_to_all | solution.py:605
  92.2 1.4 %place.1 = f32[16,16,16,128]{3,2,1,0:T(8,128)} custom-call(bf16[16,256,128]{2,1,0:T(8,128)(2,1)S(1)} %all_to_all.10.in_ref), custom_call_target="tpu_custom_call" | custom-call | bytes 3145728 | tf_op jit(solution)/shard_map/place/pallas_call | solution.py:80
  (35 shorter events, 0.4 us)
Async XLA Ops:
  0.0 7.4 %copy-start = (f32[16,16,16]{2,1,0:T(8,128)S(1)}, f32[16,16,16]{2,1,0:T(8,128)}, u32[]{:S(2)}) copy-start(f32[16,16,16]{2,1,0:T(8,128)} %param.12) | copy-start | bytes 49156
  0.0 8.2 %copy-start.12 = (s32[2,8]{1,0:T(2,128)S(1)}, s32[2,8]{1,0:T(2,128)}, u32[]{:S(2)}) copy-start(s32[2,8]{1,0:T(2,128)} %param.14) | copy-start | bytes 196
  1.7 11.1 %collective-permute-start = (bf16[2,16,16,128]{3,2,1,0:T(8,128)(2,1)}, bf16[2,16,16,128]{3,2,1,0:T(8,128)(2,1)S(1)}, u32[]{:S(2)}, u32[]{:S(2)}) collective-permute-start(bf16[2,16,16,128]{3,2,1,0:T(8,128)(2,1)} %get-tuple-element.18), channel_id=1, source_target_pairs={{0,112},{1,113},{2,114},{3,115},{4,116},{5,117},{6,118},{7,119},{8... | collective-permute-start | bytes 393224 | tf_op jit(solution)/shard_map/ppermute | solution.py:545
  7.4 5.4 %collective-permute-start.1 = (bf16[1,16,16,128]{3,2,1,0:T(8,128)(2,1)}, bf16[1,16,16,128]{3,2,1,0:T(8,128)(2,1)S(1)}, u32[]{:S(2)}, u32[]{:S(2)}) collective-permute-start(bf16[1,16,16,128]{3,2,1,0:T(8,128)(2,1)} %get-tuple-element.19), channel_id=1, source_target_pairs={{0,16},{1,17},{2,18},{3,19},{4,20},{5,21},{6,22},{7,23},{8,120},{9... | collective-permute-start | bytes 196616 | tf_op jit(solution)/shard_map/ppermute | solution.py:546
  8.3 1.6 %copy-start.4 = (f32[16,16,16,128]{3,2,1,0:T(8,128)S(1)}, f32[16,16,16,128]{3,2,1,0:T(8,128)}, u32[]{:S(2)}) copy-start(f32[16,16,16,128]{3,2,1,0:T(8,128)} %dist_ref.3) | copy-start | bytes 6291460
  14.8 7.6 %copy-start.11 = (s32[2,4096]{1,0:T(2,128)S(1)}, s32[2,4096]{1,0:T(2,128)}, u32[]{:S(2)}) copy-start(s32[2,4096]{1,0:T(2,128)} %param.13) | copy-start | bytes 98308
  14.8 25.1 %all-to-all-start = ((bf16[16,256,128]{2,1,0:T(8,128)(2,1)}), bf16[16,256,128]{2,1,0:T(8,128)(2,1)}, u32[]{:S(2)}, u32[]{:S(2)}) async-start(bf16[16,256,128]{2,1,0:T(8,128)(2,1)} %first_x.1), calls=%async_computation | async-start | bytes 2097152 | tf_op jit(solution)/shard_map/all_to_all | solution.py:575
  39.9 23.7 %copy-start.6 = (bf16[128,2048]{1,0:T(8,128)(2,1)S(1)}, bf16[128,2048]{1,0:T(8,128)(2,1)}, u32[]{:S(2)}) copy-start(bf16[128,2048]{1,0:T(8,128)(2,1)} %constant.117.clone.expand_hbm.expand_ref) | copy-start | bytes 1572868
  39.9 23.7 %copy-start.8 = (f32[256,1]{1,0:T(8,128)S(1)}, f32[256,1]{1,0:T(8,128)}, u32[]{:S(2)}) copy-start(f32[256,1]{1,0:T(8,128)} %reshape.50.rate_ref) | copy-start | bytes 3076
  39.9 23.7 %copy-start.9 = (f32[128,128]{1,0:T(8,128)S(1)}, f32[128,128]{1,0:T(8,128)}, u32[]{:S(2)}) copy-start(f32[128,128]{1,0:T(8,128)} %constant.116.clone.mix_hbm.mix_ref) | copy-start | bytes 196612
  39.9 23.7 %copy-start.10 = (f32[1,2048]{1,0:T(1,128)S(1)}, f32[1,2048]{1,0:T(1,128)}, u32[]{:S(2)}) copy-start(f32[1,2048]{1,0:T(1,128)} %constant.118.clone.w_ref) | copy-start | bytes 24580
  48.5 7.0 %collective-permute-start.2 = (bf16[24,64,128]{2,1,0:T(8,128)(2,1)}, bf16[24,64,128]{2,1,0:T(8,128)(2,1)S(1)}, u32[]{:S(2)}, u32[]{:S(2)}) collective-permute-start(bf16[24,64,128]{2,1,0:T(8,128)(2,1)} %get-tuple-element.23), channel_id=1, source_target_pairs={{0,1},{1,9},{2,3},{3,11},{4,5},{5,13},{6,7},{7,15},{8,16},{9,8},{1... | collective-permute-start | bytes 1179656 | tf_op jit(solution)/shard_map/ppermute | solution.py:589
  48.9 12.3 %collective-permute-start.3 = (bf16[24,64,128]{2,1,0:T(8,128)(2,1)}, bf16[24,64,128]{2,1,0:T(8,128)(2,1)S(1)}, u32[]{:S(2)}, u32[]{:S(2)}) collective-permute-start(bf16[24,64,128]{2,1,0:T(8,128)(2,1)} %get-tuple-element.24), channel_id=1, source_target_pairs={{1,0},{9,1},{3,2},{11,3},{5,4},{13,5},{7,6},{15,7},{16,8},{8,9},{1... | collective-permute-start | bytes 1179656 | tf_op jit(solution)/shard_map/ppermute | solution.py:590
  49.4 11.8 %collective-permute-start.4 = (bf16[24,64,128]{2,1,0:T(8,128)(2,1)}, bf16[24,64,128]{2,1,0:T(8,128)(2,1)S(1)}, u32[]{:S(2)}, u32[]{:S(2)}) collective-permute-start(bf16[24,64,128]{2,1,0:T(8,128)(2,1)} %get-tuple-element.25), channel_id=1, source_target_pairs={{0,2},{1,3},{2,4},{3,5},{4,6},{5,7},{6,0},{7,1},{8,10},{9,11},{10,... | collective-permute-start | bytes 1179656 | tf_op jit(solution)/shard_map/ppermute | solution.py:587
  49.4 11.8 %collective-permute-start.5 = (bf16[24,64,128]{2,1,0:T(8,128)(2,1)}, bf16[24,64,128]{2,1,0:T(8,128)(2,1)S(1)}, u32[]{:S(2)}, u32[]{:S(2)}) collective-permute-start(bf16[24,64,128]{2,1,0:T(8,128)(2,1)} %get-tuple-element.26), channel_id=1, source_target_pairs={{2,0},{3,1},{4,2},{5,3},{6,4},{7,5},{0,6},{1,7},{10,8},{11,9},{12,... | collective-permute-start | bytes 1179656 | tf_op jit(solution)/shard_map/ppermute | solution.py:588
  52.2 1.6 %copy-start.7 = (f32[16,256,128]{2,1,0:T(8,128)S(1)}, f32[16,256,128]{2,1,0:T(8,128)}, u32[]{:S(2)}) copy-start(f32[16,256,128]{2,1,0:T(8,128)} %get-tuple-element.20.f_hbm) | copy-start | bytes 6291460
  53.8 9.8 %copy-start.3 = (bf16[768,2048]{1,0:T(8,128)(2,1)S(1)}, bf16[768,2048]{1,0:T(8,128)(2,1)}, u32[]{:S(2)}) copy-start(bf16[768,2048]{1,0:T(8,128)(2,1)} %c_ref.1) | copy-start | bytes 9437188
  61.2 2.5 %copy-start.1 = (bf16[2048,768]{1,0:T(8,128)(2,1)S(1)}, bf16[2048,768]{1,0:T(8,128)(2,1)}, u32[]{:S(2)}) copy-start(bf16[2048,768]{1,0:T(8,128)(2,1)} %a_ref.1) | copy-start | bytes 9437188
  61.2 2.8 %copy-start.2 = (bf16[2048,768]{1,0:T(8,128)(2,1)S(1)}, bf16[2048,768]{1,0:T(8,128)(2,1)}, u32[]{:S(2)}) copy-start(bf16[2048,768]{1,0:T(8,128)(2,1)} %b_ref.1) | copy-start | bytes 9437188
  61.2 2.9 %copy-start.5 = (bf16[2048,128]{1,0:T(8,128)(2,1)S(1)}, bf16[2048,128]{1,0:T(8,128)(2,1)}, u32[]{:S(2)}) copy-start(bf16[2048,128]{1,0:T(8,128)(2,1)} %constant.115.clone.project_hbm.project_ref) | copy-start | bytes 1572868

commit v4 on v2

--- a/solution.py
+++ b/solution.py
@@ -66,8 +66,7 @@
     return 0.5 * (jnp.maximum(jnp.minimum(a, b), 0.0) + jnp.minimum(jnp.maximum(a, b), 0.0))
 
 
-ALL_VMEM = 62 << 20
-X_VMEM = 8 << 20
+C_VMEM = 12 << 20
 HBM = pltpu.HBM
 VMEM = pltpu.VMEM
 SMEM = pltpu.SMEM
@@ -114,38 +113,20 @@
     return here + minmod_half(here - before, after - here)
 
 
-def first_halo_kernel(sign_ref, dist_ref, behind_ref, ahead_ref, layers_ref, sems):
-    forward = sign_ref[0] > 0
-    copies = [
-        pltpu.make_async_copy(
-            dist_ref.at[pl.ds(jnp.where(forward, CX - 2, 0), 2)], layers_ref.at[0:2], sems.at[0]
-        ),
-        pltpu.make_async_copy(
-            dist_ref.at[pl.ds(jnp.where(forward, 0, CX - 1), 1)], layers_ref.at[2:3], sems.at[1]
-        ),
-    ]
-    for copy in copies:
-        copy.start()
-    copies[0].wait()
-    behind_ref[...] = layers_ref[0:2].astype(jnp.bfloat16)
-    copies[1].wait()
-    ahead_ref[...] = layers_ref[2:3].astype(jnp.bfloat16)
-
-
-def first_yz_kernel(dist_ref, f_ref, part_ref, sems):
+def first_halo_kernel(vel_ref, space_ref, dist_ref, behind_ref, ahead_ref):
+    forward = vel_ref[0] >= GROUPS // 2
+    start = jnp.where(forward, CX - 2, 0)
+    for i in range(2):
+        behind_ref[i] = dist_ref[start + i].astype(jnp.bfloat16)
+    ahead_ref[0] = dist_ref[jnp.where(forward, 0, CX - 1)].astype(jnp.bfloat16)
+
+
+def first_yz_kernel(f_ref, part_ref):
     uy, uz = speeds_yz()
     y_up = uy > 0.0
     z_up = uz > 0.0
 
-    def fetch(i):
-        return pltpu.make_async_copy(
-            dist_ref.at[pl.ds(2 * i, 2)], f_ref.at[pl.ds(2 * i, 2)], sems.at[i]
-        )
-
-    for i in range(CX // 2):
-        fetch(i).start()
-
-    def layer(x):
+    def layer(x, carry):
         def at(y):
             return f_ref[x, y % NY]
 
@@ -159,25 +140,22 @@
             here = at(y)
             part_ref[x, y] = here - uy * (flux - flux_before) - flux_change_z(here, uz, z_up)
             flux_before = flux
-
-    def two_layers(i, carry):
-        fetch(i).wait()
-        layer(2 * i)
-        layer(2 * i + 1)
         return carry
 
-    lax.fori_loop(0, CX // 2, two_layers, 0)
-
-
-def first_x_kernel(
-    sign_ref, speed_ref, f_ref, part_ref, behind_ref, ahead_ref, out_ref, rows_ref, sems
-):
-    s = sign_ref[0]
-    ux = speed_ref[0]
-    forward = s > 0
-
-    def put(target):
-        return pltpu.make_async_copy(rows_ref.at[target], out_ref.at[target], sems.at[target])
+    lax.fori_loop(0, CX, layer, 0)
+
+
+def first_x_kernel(vel_ref, f_ref, part_ref, behind_ref, ahead_ref, rows_ref):
+    rank = vel_ref[0]
+    forward = rank >= GROUPS // 2
+    ux = jnp.abs(rank.astype(jnp.float32) - 0.5 * (GX - 1)) * (SPACING * COURANT)
+    layers = [jnp.where(forward, k, CX - 1 - k) for k in range(CX)]
+    starts = [(x % BX) * LINE for x in layers[:BX]]
+    owners = []
+    for k in range(4):
+        quarter = jnp.where(forward, k, 3 - k)
+        high = quarter // 2
+        owners.append(high * (GROUPS // 2) + (quarter + high) % 2)
 
     def line(quarter, y):
         inner = y * NZ
@@ -190,18 +168,15 @@
                 return behind_ref[jnp.where(forward, 1, 0), y].astype(jnp.float32)
             if k == CX:
                 return ahead_ref[0, y].astype(jnp.float32)
-            return f_ref[jnp.where(forward, k, CX - 1 - k), y]
+            return f_ref[layers[k], y]
 
         face_before = upwind_face(at(-2), at(-1), at(0))
         for k in range(CX):
-            x = jnp.where(forward, k, CX - 1 - k)
             face = upwind_face(at(k - 1), at(k), at(k + 1))
-            result = part_ref[x, y] - ux * (face - face_before)
+            result = part_ref[layers[k], y] - ux * (face - face_before)
             face_before = face
-            start = pl.multiple_of((x % BX) * LINE + inner, NZ)
-            high = x // (2 * BX)
-            core = (x // BX + high) % 2
-            target = high * (GROUPS // 2) + quarter * 2 + core
+            start = pl.multiple_of(starts[k % BX] + inner, NZ)
+            target = owners[k // BX] + quarter * 2
             rows_ref[target, pl.ds(start, NZ), :] = result.astype(jnp.bfloat16)
 
     def lines(quarter, carry):
@@ -210,20 +185,41 @@
             return inside
 
         lax.fori_loop(0, BY, one, 0)
-        for high in range(2):
-            for core in range(2):
-                put(high * (GROUPS // 2) + quarter * 2 + core).start()
         return carry
 
     lax.fori_loop(0, NY // BY, lines, 0)
-    for target in range(GROUPS):
-        put(target).wait()
-
-
-def collision_terms(
-    rows, a_ref, b_ref, c_ref, project_ref, mix_ref, expand_ref, w_ref, hidden_ref, arrive
-):
-    arrive(0)
+
+
+def cell_facts(step, vel_ref, space_ref, count_ref, cells_ref, rate_ref):
+    rank = vel_ref[0]
+    high, y_quarter, core = rank // 8, rank // 2 % 4, rank % 2
+    x_quarter = 2 * high + (core + high) % 2
+    count = count_ref[step, space_ref[0]]
+    shape = (LAYER, WIDTH)
+    slot = lax.broadcasted_iota(jnp.int32, shape, 0)
+    cell = (
+        (BX * x_quarter + (slot >> 6)) * LAYER + BY * NZ * y_quarter + (slot & (LINE - 1))
+    )
+    lane = lax.broadcasted_iota(jnp.int32, (1, WIDTH), 1)
+    found = jnp.zeros(shape, jnp.float32)
+    for i in range(CX * LAYER // WIDTH):
+        part = cells_ref[step : step + 1, WIDTH * i : WIDTH * (i + 1)]
+        part = jnp.where(lane + WIDTH * i < count, part, -1)
+        found = jnp.where(cell == part, 1.0, found)
+    kinetic = jnp.broadcast_to(jnp.max(found, axis=1, keepdims=True), shape) > 0.0
+    diagonal = lax.broadcasted_iota(jnp.int32, (NZ, NZ), 0) == lax.broadcasted_iota(
+        jnp.int32, (NZ, NZ), 1
+    )
+    columns = []
+    for x in range(BX):
+        for y in range(BY):
+            line = rate_ref[BX * x_quarter + x, pl.ds(BY * y_quarter + y, 1), :]
+            column = jnp.sum(jnp.where(diagonal, line, 0.0), axis=1, keepdims=True)
+            columns.append(jnp.broadcast_to(column, (NZ, WIDTH)))
+    return kinetic, jnp.concatenate(columns, axis=0)
+
+
+def collide(rows, a_ref, b_ref, c_ref, project_ref, mix_ref, expand_ref, w_ref, hidden_ref):
     moments = jnp.dot(rows, project_ref[...], preferred_element_type=jnp.float32)
     coeffs = jnp.dot(
         moments, mix_ref[...], precision=lax.Precision.HIGHEST, preferred_element_type=jnp.float32
@@ -236,15 +232,12 @@
     split = split.astype(jnp.bfloat16)
     for n in range(RANK // 256):
         cols = slice(256 * n, 256 * (n + 1))
-        arrive(1 + n)
         first = jnp.dot(rows, a_ref[:, cols], preferred_element_type=jnp.float32)
         second = jnp.dot(rows, b_ref[:, cols], preferred_element_type=jnp.float32)
         hidden_ref[:, cols] = (first * second).astype(jnp.bfloat16)
     hidden = hidden_ref[...]
     for n in range(NV // 256):
         cols = slice(256 * n, 256 * (n + 1))
-        if n % 2 == 0:
-            arrive(4 + n // 2)
         collision = jnp.dot(hidden, c_ref[:, cols], preferred_element_type=jnp.float32)
         collision = collision.astype(jnp.bfloat16).astype(jnp.float32)
         poly = jnp.dot(split, expand_ref[:, cols], preferred_element_type=jnp.float32)
@@ -255,53 +248,16 @@
 
 
 def first_collide_kernel(
-    rows_hbm, a_hbm, b_hbm, c_hbm, project_hbm, mix_hbm, expand_hbm, w_ref, rate_ref, mask_ref,
-    f_out, x_up_out, x_down_out, y_up_out, y_down_out,
-    rows_ref, a_ref, b_ref, c_ref, project_ref, mix_ref, expand_ref, hidden_ref,
-    f_ref, x_up_ref, x_down_ref, y_up_ref, y_down_ref, in_sems, out_sems,
+    vel_ref, space_ref, count_ref, rows_ref, a_ref, b_ref, c_ref, project_ref, mix_ref,
+    expand_ref, w_ref, cells_ref, rate_ref,
+    f_ref, x_up_ref, x_down_ref, y_up_ref, y_down_ref, hidden_ref,
 ):
-    pieces = [[(rows_hbm, rows_ref), (project_hbm, project_ref), (mix_hbm, mix_ref)]]
-    for n in range(RANK // 256):
-        cols = slice(256 * n, 256 * (n + 1))
-        pieces.append([(a_hbm.at[:, cols], a_ref.at[:, cols]), (b_hbm.at[:, cols], b_ref.at[:, cols])])
-    pieces.append([(expand_hbm, expand_ref)])
-    for n in range(4):
-        cols = slice(512 * n, 512 * (n + 1))
-        if n:
-            pieces.append([])
-        pieces[-1].append((c_hbm.at[:, cols], c_ref.at[:, cols]))
-    fetches, count = [], 0
-    for piece in pieces:
-        fetches.append([])
-        for source, target in piece:
-            fetches[-1].append(pltpu.make_async_copy(source, target, in_sems.at[count]))
-            fetches[-1][-1].start()
-            count += 1
-
-    def arrive(i):
-        for fetch in fetches[i]:
-            fetch.wait()
-
-    stores = []
-
-    def send(source, target, first, last):
-        stores.append(
-            pltpu.make_async_copy(
-                source.at[first:last], target.at[first:last], out_sems.at[len(stores)]
-            )
-        )
-        stores[-1].start()
-
-    for fetch in fetches[0]:
-        fetch.wait()
     rows = jnp.concatenate([rows_ref[g] for g in range(GROUPS)], axis=1)
-    rate = jnp.broadcast_to(rate_ref[...], (LAYER, WIDTH))
-    kinetic = jnp.broadcast_to(mask_ref[...], (LAYER, WIDTH)) > 0.0
+    kinetic, rate = cell_facts(0, vel_ref, space_ref, count_ref, cells_ref, rate_ref)
     half = GROUPS // 2
     low_lane = lax.broadcasted_iota(jnp.int32, (NZ, WIDTH), 1) < WIDTH // 2
-    for g, collision, equilibrium in collision_terms(
-        rows, a_ref, b_ref, c_ref, project_ref, mix_ref, expand_ref, w_ref, hidden_ref,
-        lambda i: arrive(i) if i else None,
+    for g, collision, equilibrium in collide(
+        rows, a_ref, b_ref, c_ref, project_ref, mix_ref, expand_ref, w_ref, hidden_ref
     ):
         moved = rows_ref[g].astype(jnp.float32)
         change = jnp.where(kinetic, COLLIDE * collision, rate * (equilibrium - moved))
@@ -328,46 +284,20 @@
                 y_down_ref[GROUPS + low, here] = jnp.where(
                     low_lane, f_ref[low, second], pltpu.roll(result[second], WIDTH // 2, 1)
                 ).astype(jnp.bfloat16)
-        if g % 4 == 3:
-            first = g - 3
-            send(f_ref, f_out, first, g + 1)
-            for source, target in (
-                (y_up_ref, y_up_out), (y_down_ref, y_down_out),
-                (x_up_ref, x_up_out), (x_down_ref, x_down_out),
-            ):
-                send(source, target, first, g + 1)
-            if g >= half:
-                send(y_up_ref, y_up_out, first + half, g + 1 + half)
-                send(y_down_ref, y_down_out, first + half, g + 1 + half)
-                send(x_up_ref, x_up_out, first + half, g + 1 + half)
-            else:
-                send(x_down_ref, x_down_out, first + GROUPS, g + 1 + GROUPS)
-    for store in stores:
-        store.wait()
-
-
-def second_z_kernel(f_hbm, f_ref, part_ref, sems):
+
+
+def second_z_kernel(f_ref, part_ref):
     _, uz = speeds_yz()
     z_up = uz > 0.0
 
-    def fetch(i):
-        return pltpu.make_async_copy(
-            f_hbm.at[pl.ds(2 * i, 2)], f_ref.at[pl.ds(2 * i, 2)], sems.at[i]
-        )
-
-    for i in range(GROUPS // 2):
-        fetch(i).start()
-
-    def two_groups(i, carry):
-        fetch(i).wait()
-        for g in (2 * i, 2 * i + 1):
-            for c in range(BX * BY):
-                here = slice(NZ * c, NZ * (c + 1))
-                f = f_ref[g, here]
-                part_ref[g, here] = f - flux_change_z(f, uz, z_up)
+    def group(g, carry):
+        for c in range(BX * BY):
+            here = slice(NZ * c, NZ * (c + 1))
+            f = f_ref[g, here]
+            part_ref[g, here] = f - flux_change_z(f, uz, z_up)
         return carry
 
-    lax.fori_loop(0, GROUPS // 2, two_groups, 0)
+    lax.fori_loop(0, GROUPS, group, 0)
 
 
 def second_xy_kernel(
@@ -444,15 +374,13 @@
 
 
 def second_collide_kernel(
-    moved_ref, a_ref, b_ref, c_ref, project_ref, mix_ref, expand_ref, w_ref, rate_ref, mask_ref,
-    out_ref, hidden_ref,
+    vel_ref, space_ref, count_ref, moved_ref, a_ref, b_ref, c_ref, project_ref, mix_ref,
+    expand_ref, w_ref, cells_ref, rate_ref, out_ref, hidden_ref,
 ):
     rows = jnp.concatenate([moved_ref[g].astype(jnp.bfloat16) for g in range(GROUPS)], axis=1)
-    rate = jnp.broadcast_to(rate_ref[...], (LAYER, WIDTH))
-    kinetic = jnp.broadcast_to(mask_ref[...], (LAYER, WIDTH)) > 0.0
-    for g, collision, equilibrium in collision_terms(
-        rows, a_ref, b_ref, c_ref, project_ref, mix_ref, expand_ref, w_ref, hidden_ref,
-        lambda i: None,
+    kinetic, rate = cell_facts(1, vel_ref, space_ref, count_ref, cells_ref, rate_ref)
+    for g, collision, equilibrium in collide(
+        rows, a_ref, b_ref, c_ref, project_ref, mix_ref, expand_ref, w_ref, hidden_ref
     ):
         moved = moved_ref[g]
         change = jnp.where(kinetic, COLLIDE * collision, rate * (equilibrium - moved))
@@ -505,37 +433,19 @@
 
 
 def body(dist, relax_rate, kinetic_cells, kinetic_count, map_a, map_b, map_c):
-    rank_vel = lax.axis_index("vel")
-    rank_space = lax.axis_index("space")
+    vel = (lax.axis_index("vel").astype(jnp.int32).reshape(1), SMEM)
+    space = (lax.axis_index("space").astype(jnp.int32).reshape(1), SMEM)
     both = ("space", "vel")
     upwind, downwind, x_up, x_down, y_up, y_down = steps_of(lax.axis_size("space"))
     project, mix, expand, w = tables()
     consts = (jnp.asarray(project), jnp.asarray(mix), jnp.asarray(expand), jnp.asarray(w))
-    vx = (rank_vel.astype(jnp.float32) - 0.5 * (GX - 1)) * SPACING
-    speed = (COURANT * jnp.abs(vx)).reshape(1)
-    forward = rank_vel >= GROUPS // 2
-    sign = jnp.where(forward, 1, -1).astype(jnp.int32).reshape(1)
-
     layers = (NY, NZ, WIDTH)
     behind, ahead = call(
-        first_halo_kernel, "first_halo", ((sign, SMEM), (dist, HBM)),
+        first_halo_kernel, "first_halo", (vel, space, (dist, VMEM)),
         (((2,) + layers, jnp.bfloat16, VMEM), ((1,) + layers, jnp.bfloat16, VMEM)),
-        scratch=(VMEM((3,) + layers, jnp.float32), DMA((2,))), limit=ALL_VMEM,
     )
     behind = lax.ppermute(behind, both, upwind)
     ahead = lax.ppermute(ahead, both, downwind)
-
-    high, y_quarter, core = rank_vel // 8, rank_vel // 2 % 4, rank_vel % 2
-    x_quarter = 2 * high + (core + high) % 2
-    rate = lax.dynamic_slice(relax_rate, (BX * x_quarter, BY * y_quarter, 0), (BX, BY, NZ))
-    rate = rate.reshape(LAYER, 1)
-    own = lax.dynamic_index_in_dim(kinetic_count, rank_space, 1, False)
-    live = jnp.arange(CX * LAYER, dtype=jnp.int32)[None, :] < own[:, None]
-    listed = jnp.where(live, kinetic_cells, -1)
-    slot = jnp.arange(LAYER, dtype=jnp.int32)
-    cell = (BX * x_quarter + slot // LINE) * LAYER + (BY * y_quarter * NZ + slot % LINE)
-    masks = jnp.any(listed[:, None, :] == cell[None, :, None], axis=2, keepdims=True)
-    masks = masks.astype(jnp.float32)
 
     state = ((CX,) + layers, jnp.float32, VMEM)
     wide = (GROUPS, LAYER, WIDTH)
@@ -543,33 +453,25 @@
     half = jnp.bfloat16
     hidden = VMEM((LAYER, RANK), half)
 
-    f, part = call(
-        first_yz_kernel, "first_yz", ((dist, HBM),), (state, state),
-        scratch=(DMA((CX // 2,)),), flops=12_000_000,
-    )
+    (part,) = call(first_yz_kernel, "first_yz", ((dist, VMEM),), (state,), flops=12_000_000)
     (rows,) = call(
-        first_x_kernel, "first_x",
-        ((sign, SMEM), (speed, SMEM), (f, VMEM), (part, VMEM), (behind, VMEM), (ahead, VMEM)),
-        ((wide, half, HBM),), scratch=(VMEM(wide, half), DMA((GROUPS,))), flops=6_000_000, limit=X_VMEM,
+        first_x_kernel, "first_x", (vel,) + tuple((o, VMEM) for o in (dist, part, behind, ahead)),
+        ((wide, half, VMEM),), flops=6_000_000,
     )
     gathered = lax.all_to_all(rows, "vel", split_axis=0, concat_axis=0, tiled=True)
-    held = (map_a, map_b, map_c) + consts[:3]
+    facts = (vel, space, (kinetic_count, SMEM))
+    held = tuple((o, VMEM) for o in (map_a, map_b, map_c) + consts + (kinetic_cells, relax_rate))
     f, up_x, down_x, up_y, down_y = call(
-        first_collide_kernel, "first_collide",
-        ((gathered, HBM),) + tuple((o, HBM) for o in held)
-        + ((consts[3], VMEM), (rate, VMEM), (masks[0], VMEM)),
-        ((wide, jnp.float32, HBM),) + ((halo, half, HBM),) * 4,
-        scratch=(VMEM(wide, half),) + tuple(VMEM(o.shape, o.dtype) for o in held)
-        + (hidden, VMEM(wide, jnp.float32)) + (VMEM(halo, half),) * 4 + (DMA((16,)), DMA((32,))),
-        flops=2_500_000_000, limit=ALL_VMEM,
+        first_collide_kernel, "first_collide", facts + ((gathered, VMEM),) + held,
+        ((wide, jnp.float32, VMEM),) + ((halo, half, VMEM),) * 4,
+        scratch=(hidden,), flops=2_500_000_000, limit=C_VMEM,
     )
     y_below = lax.ppermute(up_y, both, y_up)
     y_above = lax.ppermute(down_y, both, y_down)
     x_below = lax.ppermute(up_x, both, x_up)
     x_above = lax.ppermute(down_x, both, x_down)
-    f, part = call(
-        second_z_kernel, "second_z", ((f, HBM),), ((wide, jnp.float32, VMEM),) * 2,
-        scratch=(DMA((GROUPS // 2,)),), flops=6_000_000,
+    (part,) = call(
+        second_z_kernel, "second_z", ((f, VMEM),), ((wide, jnp.float32, VMEM),), flops=6_000_000
     )
     (moved,) = call(
         second_xy_kernel, "second_xy",
@@ -577,9 +479,8 @@
         ((wide, jnp.float32, VMEM),), flops=12_000_000,
     )
     (result,) = call(
-        second_collide_kernel, "second_collide",
-        ((moved, VMEM),) + tuple((o, VMEM) for o in held + (consts[3], rate, masks[1])),
-        ((wide, half, VMEM),), scratch=(hidden,), flops=2_500_000_000, limit=12 << 20,
+        second_collide_kernel, "second_collide", facts + ((moved, VMEM),) + held,
+        ((wide, half, VMEM),), scratch=(hidden,), flops=2_500_000_000, limit=C_VMEM,
     )
     pieces = lax.all_to_all(result, "vel", split_axis=0, concat_axis=0, tiled=True)
     (out,) = call(

time: 95.8 us -> 87.7 us (0.915)
  blocking collectives: 24.4 us -> 47.8 us
  waiting for transfers between devices: 21.1 us -> 10.2 us
  Pallas kernels: 25.9 us -> 18.1 us
  starting transfers between devices: 16.8 us -> 9.59 us
  local copies, waits for them, and re-layouts: 5.55 us -> 1.64 us
  other arithmetic: 1.29 us -> 0 us
    all_to_all x0 -> x1, blocking collectives: none -> 23.5 us  [body(): lax.all_to_all(rows, 'vel', split_axis=0, concat_axis=0, tiled=True)]
    all_to_all x1 -> x0, waiting for transfers between devices: 15.3 us -> none  [body(): lax.all_to_all(rows, 'vel', split_axis=0, concat_axis=0, tiled=True)]
    pallas_call x8, Pallas kernels: 25.9 us -> 18.1 us  [call(): pl.pallas_call(kernel, out_shape=tuple(shapes), in_specs=[pl.BlockSpec(me...]
    all_to_all x1 -> x0, starting transfers between devices: 7.54 us -> none  [body(): lax.all_to_all(rows, 'vel', split_axis=0, concat_axis=0, tiled=True)]
    ppermute x1, waiting for transfers between devices: 0.19 us -> 2.69 us  [body(): ahead = lax.ppermute(ahead, both, downwind)]
    unnamed x26 -> x22, local copies, waits for them, and re-layouts: 3.66 us -> 1.64 us
    ppermute x1, waiting for transfers between devices: 5.6 us -> 7.29 us  [body(): x_above = lax.ppermute(down_x, both, x_down)]
    reduce_or x1 -> x0, other arithmetic: 1.19 us -> none  [body(): jnp.any(listed[:, None, :] == cell[None, :, None], axis=2, keepdims=True)]
  transfers between devices with their start and end apart: 7 -> 6, of which waited for: 3 -> 3; matrix products, arithmetic and copies ran while one was open for 3% -> 0% of each run, Pallas kernels for 5% -> 5%
where the time goes in v4:
time: 87.7 us; the launch traced here: 87.5 us
  blocking collectives  47.8 us (55%)
  Pallas kernels  18.1 us (21%)
  waiting for transfers between devices  10.2 us (12%)
  starting transfers between devices  9.59 us (11%)
  local copies, waits for them, and re-layouts  1.64 us (2%)
    all_to_all x1, blocking collectives, body(): lax.all_to_all(result, 'vel', split_axis=0, concat_axis=0, tiled=True)  24.3 us
    all_to_all x1, blocking collectives, body(): lax.all_to_all(rows, 'vel', split_axis=0, concat_axis=0, tiled=True)  23.5 us
    pallas_call x8, Pallas kernels, call(): pl.pallas_call(kernel, out_shape=tuple(shapes), in_specs=[pl.BlockSpec(me...  18.1 us
    ppermute x1, waiting for transfers between devices, body(): x_above = lax.ppermute(down_x, both, x_down)  7.29 us
    ppermute x1, starting transfers between devices, body(): behind = lax.ppermute(behind, both, upwind)  5.67 us
    ppermute x1, waiting for transfers between devices, body(): ahead = lax.ppermute(ahead, both, downwind)  2.69 us
    ppermute x1, starting transfers between devices, body(): y_above = lax.ppermute(down_y, both, y_down)  2.67 us
  transfers between devices with their start and end apart: 6, of which 3 were waited for; matrix products, arithmetic and copies ran while one was open for 0% of the time, Pallas kernels for 5%

profile of v4, /device:TPU:1, one launch (start us, length us, event | category | flops | bytes accessed | tf_op | source)
XLA Modules:
  0.0 87.5 jit_solution(7460076515243849076)
XLA Ops:
  0.0 1.6 %copy-done = f32[16,16,16,128]{3,2,1,0:T(8,128)S(1)} copy-done((f32[16,16,16,128]{3,2,1,0:T(8,128)S(1)}, f32[16,16,16,128]{3,2,1,0:T(8,128)}, u32[]{:S(2)}) %copy-start) | copy-done | bytes 2097176
  1.6 5.7 %collective-permute-start = (bf16[2,16,16,128]{3,2,1,0:T(8,128)(2,1)S(1)}, bf16[2,16,16,128]{3,2,1,0:T(8,128)(2,1)S(1)}, u32[]{:S(2)}, u32[]{:S(2)}) collective-permute-start(bf16[2,16,16,128]{3,2,1,0:T(8,128)(2,1)S(1)} %get-tuple-element.12), channel_id=1, source_target_pairs={{0,112},{1,113},{2,114},{3,115},{4,116},{5,117},{6,118},{7,119},{8... | collective-permute-start | bytes 393224 | tf_op jit(solution)/shard_map/ppermute | solution.py:447
  7.3 0.0 collective-permute-start.1
  7.3 0.0 copy-start.10
  7.3 2.5 %first_yz.1.part_ref = f32[16,16,16,128]{3,2,1,0:T(8,128)S(1)} custom-call(f32[16,16,16,128]{3,2,1,0:T(8,128)S(1)} %copy-done), custom_call_target="tpu_custom_call" | custom-call | flops 12000000 | bytes 4194304 | tf_op jit(solution)/shard_map/first_yz/pallas_call | solution.py:80
  9.8 2.7 %collective-permute-done.1.ahead_ref = bf16[1,16,16,128]{3,2,1,0:T(8,128)(2,1)S(1)} collective-permute-done((bf16[1,16,16,128]{3,2,1,0:T(8,128)(2,1)S(1)}, bf16[1,16,16,128]{3,2,1,0:T(8,128)(2,1)S(1)}, u32[]{:S(2)}, u32[]{:S(2)}) %collective-permute-start.1) | collective-permute-done | bytes 65568 | tf_op jit(solution)/shard_map/ppermute | solution.py:448
  12.5 0.0 collective-permute-done.behind_ref
  12.5 1.2 %first_x.1 = bf16[16,256,128]{2,1,0:T(8,128)(2,1)S(1)} custom-call(s32[1]{0:T(128)} %bitcast.vel_ref, f32[16,16,16,128]{3,2,1,0:T(8,128)S(1)} %copy-done, f32[16,16,16,128]{3,2,1,0:T(8,128)S(1)} %first_yz.1.part_ref, bf16[2,16,16,128]{3,2,1,0:T(8,128)(2,1)S(1)} %collective-permute-done.behind_ref, bf16[1,16,16,128]{3,2,1,0:T(8,128)(2,1)S(1)} %collective-permute-done.1.ahead_ref), custom_call_target="tpu_custom_call" | custom-call | flops 6000000 | bytes 5439492 | tf_op jit(solution)/shard_map/first_x/pallas_call | solution.py:80
  13.8 0.0 copy-start.4
  13.8 0.0 copy-start.5
  13.8 0.0 copy-start.6
  13.8 0.0 copy-start.7
  13.8 23.5 %all_to_all.10.rows_ref = bf16[16,256,128]{2,1,0:T(8,128)(2,1)S(1)} all-to-all(bf16[16,256,128]{2,1,0:T(8,128)(2,1)S(1)} %first_x.1), channel_id=1, replica_groups=mesh['space'=8,'vel'=16] {'vel'}, dimensions={0} | all-to-all | bytes 2097152 | tf_op jit(solution)/shard_map/all_to_all | solution.py:461
  37.4 4.6 %first_collide.1 = (f32[16,256,128]{2,1,0:T(8,128)S(1)}, bf16[24,64,128]{2,1,0:T(8,128)(2,1)S(1)}, bf16[24,64,128]{2,1,0:T(8,128)(2,1)S(1)}, bf16[24,64,128]{2,1,0:T(8,128)(2,1)S(1)}, bf16[24,64,128]{2,1,0:T(8,128)(2,1)S(1)}) custom-call(s32[1]{0:T(128)} %bitcast.vel_ref, s32[1]{0:T(128)} %bitcast.1.space_ref, s32[2,8]{1,0:T(2,128)S(1)} %copy-done.10, ...), custom_call_target="tpu_custom_call" | custom-call | flops 2500000000 | bytes 15327304 | tf_op jit(solution)/shard_map/first_collide/pallas_call | solution.py:80
  42.0 1.0 %collective-permute-start.2 = (bf16[24,64,128]{2,1,0:T(8,128)(2,1)S(1)}, bf16[24,64,128]{2,1,0:T(8,128)(2,1)S(1)}, u32[]{:S(2)}, u32[]{:S(2)}) collective-permute-start(bf16[24,64,128]{2,1,0:T(8,128)(2,1)S(1)} %get-tuple-element.15), channel_id=1, source_target_pairs={{0,1},{1,9},{2,3},{3,11},{4,5},{5,13},{6,7},{7,15},{8,16},{9,8},{1... | collective-permute-start | bytes 1179656 | tf_op jit(solution)/shard_map/ppermute | solution.py:471
  42.9 0.3 collective-permute-start.3
  43.2 2.7 %collective-permute-start.5 = (bf16[24,64,128]{2,1,0:T(8,128)(2,1)S(1)}, bf16[24,64,128]{2,1,0:T(8,128)(2,1)S(1)}, u32[]{:S(2)}, u32[]{:S(2)}) collective-permute-start(bf16[24,64,128]{2,1,0:T(8,128)(2,1)S(1)} %get-tuple-element.18), channel_id=1, source_target_pairs={{2,0},{3,1},{4,2},{5,3},{6,4},{7,5},{0,6},{1,7},{10,8},{11,9},{12,... | collective-permute-start | bytes 1179656 | tf_op jit(solution)/shard_map/ppermute | solution.py:470
  45.9 1.6 %second_z.1.part_ref = f32[16,256,128]{2,1,0:T(8,128)S(1)} custom-call(f32[16,256,128]{2,1,0:T(8,128)S(1)} %get-tuple-element.14.f_ref), custom_call_target="tpu_custom_call" | custom-call | flops 6000000 | bytes 4194304 | tf_op jit(solution)/shard_map/second_z/pallas_call | solution.py:80
  47.4 0.2 collective-permute-done.2.x_below_ref
  47.6 7.3 %collective-permute-done.3.x_above_ref = bf16[24,64,128]{2,1,0:T(8,128)(2,1)S(1)} collective-permute-done((bf16[24,64,128]{2,1,0:T(8,128)(2,1)S(1)}, bf16[24,64,128]{2,1,0:T(8,128)(2,1)S(1)}, u32[]{:S(2)}, u32[]{:S(2)}) %collective-permute-start.3) | collective-permute-done | bytes 393248 | tf_op jit(solution)/shard_map/ppermute | solution.py:472
  54.9 2.4 %second_xy.1.moved_ref = f32[16,256,128]{2,1,0:T(8,128)S(1)} custom-call(f32[16,256,128]{2,1,0:T(8,128)S(1)} %get-tuple-element.14.f_ref, f32[16,256,128]{2,1,0:T(8,128)S(1)} %second_z.1.part_ref, bf16[24,64,128]{2,1,0:T(8,128)(2,1)S(1)} %collective-permute-done.2.x_below_ref, bf16[24,64,128]{2,1,0:T(8,128)(2,1)S(1)} %collective-permute-done.3.x_above_ref, ...), custom_call_target="tpu_custom_call" | custom-call | flops 12000000 | bytes 7864320 | tf_op jit(solution)/shard_map/second_xy/pallas_call | solution.py:80
  57.3 4.5 %second_collide.1 = bf16[16,256,128]{2,1,0:T(8,128)(2,1)S(1)} custom-call(s32[1]{0:T(128)} %bitcast.vel_ref, s32[1]{0:T(128)} %bitcast.1.space_ref, s32[2,8]{1,0:T(2,128)S(1)} %copy-done.10, f32[16,256,128]{2,1,0:T(8,128)S(1)} %second_xy.1.moved_ref, bf16[2048,768]{1,0:T(8,128)(2,1)S(1)} %copy-done.1, bf16[2048,768]{1,0:T(8,128)(2,1)S(1)} %copy-done.2, ...), custom_call_target="tpu_custom_call" | custom-call | flops 2500000000 | bytes 13754440 | tf_op jit(solution)/shard_map/second_collide/pallas_call | solution.py:80
  61.8 24.3 %all_to_all.11.in_ref = bf16[16,256,128]{2,1,0:T(8,128)(2,1)S(1)} all-to-all(bf16[16,256,128]{2,1,0:T(8,128)(2,1)S(1)} %second_collide.1), channel_id=1, replica_groups=mesh['space'=8,'vel'=16] {'vel'}, dimensions={0} | all-to-all | bytes 2097152 | tf_op jit(solution)/shard_map/all_to_all | solution.py:485
  86.1 1.4 %place.1 = f32[16,16,16,128]{3,2,1,0:T(8,128)} custom-call(bf16[16,256,128]{2,1,0:T(8,128)(2,1)S(1)} %all_to_all.11.in_ref), custom_call_target="tpu_custom_call" | custom-call | bytes 3145728 | tf_op jit(solution)/shard_map/place/pallas_call | solution.py:80
  (20 shorter events, 0.1 us)
Async XLA Ops:
  0.0 1.6 %copy-start = (f32[16,16,16,128]{3,2,1,0:T(8,128)S(1)}, f32[16,16,16,128]{3,2,1,0:T(8,128)}, u32[]{:S(2)}) copy-start(f32[16,16,16,128]{3,2,1,0:T(8,128)} %f_ref.3) | copy-start | bytes 6291460
  1.6 10.9 %collective-permute-start = (bf16[2,16,16,128]{3,2,1,0:T(8,128)(2,1)S(1)}, bf16[2,16,16,128]{3,2,1,0:T(8,128)(2,1)S(1)}, u32[]{:S(2)}, u32[]{:S(2)}) collective-permute-start(bf16[2,16,16,128]{3,2,1,0:T(8,128)(2,1)S(1)} %get-tuple-element.12), channel_id=1, source_target_pairs={{0,112},{1,113},{2,114},{3,115},{4,116},{5,117},{6,118},{7,119},{8... | collective-permute-start | bytes 393224 | tf_op jit(solution)/shard_map/ppermute | solution.py:447
  7.3 5.2 %collective-permute-start.1 = (bf16[1,16,16,128]{3,2,1,0:T(8,128)(2,1)S(1)}, bf16[1,16,16,128]{3,2,1,0:T(8,128)(2,1)S(1)}, u32[]{:S(2)}, u32[]{:S(2)}) collective-permute-start(bf16[1,16,16,128]{3,2,1,0:T(8,128)(2,1)S(1)} %get-tuple-element.13), channel_id=1, source_target_pairs={{0,16},{1,17},{2,18},{3,19},{4,20},{5,21},{6,22},{7,23},{8,120},{9... | collective-permute-start | bytes 196616 | tf_op jit(solution)/shard_map/ppermute | solution.py:448
  7.3 30.0 %copy-start.3 = (bf16[768,2048]{1,0:T(8,128)(2,1)S(1)}, bf16[768,2048]{1,0:T(8,128)(2,1)}, u32[]{:S(2)}) copy-start(bf16[768,2048]{1,0:T(8,128)(2,1)} %c_ref.3) | copy-start | bytes 9437188
  7.3 30.0 %copy-start.8 = (s32[2,4096]{1,0:T(2,128)S(1)}, s32[2,4096]{1,0:T(2,128)}, u32[]{:S(2)}) copy-start(s32[2,4096]{1,0:T(2,128)} %cells_ref.3) | copy-start | bytes 98308
  7.3 30.0 %copy-start.9 = (f32[1,2048]{1,0:T(1,128)S(1)}, f32[1,2048]{1,0:T(1,128)}, u32[]{:S(2)}) copy-start(f32[1,2048]{1,0:T(1,128)} %constant.20.clone.w_ref) | copy-start | bytes 24580
  7.3 30.0 %copy-start.10 = (s32[2,8]{1,0:T(2,128)S(1)}, s32[2,8]{1,0:T(2,128)}, u32[]{:S(2)}) copy-start(s32[2,8]{1,0:T(2,128)} %count_ref.3) | copy-start | bytes 196
  12.5 24.8 %copy-start.1 = (bf16[2048,768]{1,0:T(8,128)(2,1)S(1)}, bf16[2048,768]{1,0:T(8,128)(2,1)}, u32[]{:S(2)}) copy-start(bf16[2048,768]{1,0:T(8,128)(2,1)} %a_ref.3) | copy-start | bytes 9437188
  12.5 24.8 %copy-start.2 = (bf16[2048,768]{1,0:T(8,128)(2,1)S(1)}, bf16[2048,768]{1,0:T(8,128)(2,1)}, u32[]{:S(2)}) copy-start(bf16[2048,768]{1,0:T(8,128)(2,1)} %b_ref.3) | copy-start | bytes 9437188
  13.8 23.6 %copy-start.4 = (bf16[128,2048]{1,0:T(8,128)(2,1)S(1)}, bf16[128,2048]{1,0:T(8,128)(2,1)}, u32[]{:S(2)}) copy-start(bf16[128,2048]{1,0:T(8,128)(2,1)} %constant.19.clone.expand_ref) | copy-start | bytes 1572868
  13.8 23.6 %copy-start.5 = (bf16[2048,128]{1,0:T(8,128)(2,1)S(1)}, bf16[2048,128]{1,0:T(8,128)(2,1)}, u32[]{:S(2)}) copy-start(bf16[2048,128]{1,0:T(8,128)(2,1)} %constant.17.clone.project_ref) | copy-start | bytes 1572868
  13.8 23.6 %copy-start.6 = (f32[16,16,16]{2,1,0:T(8,128)S(1)}, f32[16,16,16]{2,1,0:T(8,128)}, u32[]{:S(2)}) copy-start(f32[16,16,16]{2,1,0:T(8,128)} %rate_ref.3) | copy-start | bytes 49156
  13.8 23.6 %copy-start.7 = (f32[128,128]{1,0:T(8,128)S(1)}, f32[128,128]{1,0:T(8,128)}, u32[]{:S(2)}) copy-start(f32[128,128]{1,0:T(8,128)} %constant.18.clone.mix_ref) | copy-start | bytes 196612
  42.0 5.7 %collective-permute-start.2 = (bf16[24,64,128]{2,1,0:T(8,128)(2,1)S(1)}, bf16[24,64,128]{2,1,0:T(8,128)(2,1)S(1)}, u32[]{:S(2)}, u32[]{:S(2)}) collective-permute-start(bf16[24,64,128]{2,1,0:T(8,128)(2,1)S(1)} %get-tuple-element.15), channel_id=1, source_target_pairs={{0,1},{1,9},{2,3},{3,11},{4,5},{5,13},{6,7},{7,15},{8,16},{9,8},{1... | collective-permute-start | bytes 1179656 | tf_op jit(solution)/shard_map/ppermute | solution.py:471
  42.9 12.0 %collective-permute-start.3 = (bf16[24,64,128]{2,1,0:T(8,128)(2,1)S(1)}, bf16[24,64,128]{2,1,0:T(8,128)(2,1)S(1)}, u32[]{:S(2)}, u32[]{:S(2)}) collective-permute-start(bf16[24,64,128]{2,1,0:T(8,128)(2,1)S(1)} %get-tuple-element.16), channel_id=1, source_target_pairs={{1,0},{9,1},{3,2},{11,3},{5,4},{13,5},{7,6},{15,7},{16,8},{8,9},{1... | collective-permute-start | bytes 1179656 | tf_op jit(solution)/shard_map/ppermute | solution.py:472
  43.2 11.8 %collective-permute-start.4 = (bf16[24,64,128]{2,1,0:T(8,128)(2,1)S(1)}, bf16[24,64,128]{2,1,0:T(8,128)(2,1)S(1)}, u32[]{:S(2)}, u32[]{:S(2)}) collective-permute-start(bf16[24,64,128]{2,1,0:T(8,128)(2,1)S(1)} %get-tuple-element.17), channel_id=1, source_target_pairs={{0,2},{1,3},{2,4},{3,5},{4,6},{5,7},{6,0},{7,1},{8,10},{9,11},{10,... | collective-permute-start | bytes 1179656 | tf_op jit(solution)/shard_map/ppermute | solution.py:469
  43.2 11.8 %collective-permute-start.5 = (bf16[24,64,128]{2,1,0:T(8,128)(2,1)S(1)}, bf16[24,64,128]{2,1,0:T(8,128)(2,1)S(1)}, u32[]{:S(2)}, u32[]{:S(2)}) collective-permute-start(bf16[24,64,128]{2,1,0:T(8,128)(2,1)S(1)} %get-tuple-element.18), channel_id=1, source_target_pairs={{2,0},{3,1},{4,2},{5,3},{6,4},{7,5},{0,6},{1,7},{10,8},{11,9},{12,... | collective-permute-start | bytes 1179656 | tf_op jit(solution)/shard_map/ppermute | solution.py:470

commit v5 on v4

--- a/solution.py
+++ b/solution.py
@@ -121,6 +121,42 @@
     ahead_ref[0] = dist_ref[jnp.where(forward, 0, CX - 1)].astype(jnp.bfloat16)
 
 
+def quarters(rank):
+    high, core = rank // 8, rank % 2
+    return 2 * high + (core + high) % 2, rank // 2 % 4
+
+
+def kinetic_cells_of(step, vel_ref, space_ref, count_ref, cells_ref):
+    x_quarter, y_quarter = quarters(vel_ref[0])
+    count = count_ref[step, space_ref[0]]
+    shape = (LAYER, WIDTH)
+    slot = lax.broadcasted_iota(jnp.int32, shape, 0)
+    cell = (
+        (BX * x_quarter + (slot >> 6)) * LAYER + BY * NZ * y_quarter + (slot & (LINE - 1))
+    )
+    lane = lax.broadcasted_iota(jnp.int32, (1, WIDTH), 1)
+    found = jnp.zeros(shape, jnp.float32)
+    for i in range(CX * LAYER // WIDTH):
+        part = cells_ref[step : step + 1, WIDTH * i : WIDTH * (i + 1)]
+        part = jnp.where(lane + WIDTH * i < count, part, -1)
+        found = jnp.where(cell == part, 1.0, found)
+    return jnp.broadcast_to(jnp.max(found, axis=1, keepdims=True), shape)
+
+
+def rates_of(vel_ref, rate_ref):
+    x_quarter, y_quarter = quarters(vel_ref[0])
+    diagonal = lax.broadcasted_iota(jnp.int32, (NZ, NZ), 0) == lax.broadcasted_iota(
+        jnp.int32, (NZ, NZ), 1
+    )
+    columns = []
+    for x in range(BX):
+        for y in range(BY):
+            line = rate_ref[BX * x_quarter + x, pl.ds(BY * y_quarter + y, 1), :]
+            column = jnp.sum(jnp.where(diagonal, line, 0.0), axis=1, keepdims=True)
+            columns.append(jnp.broadcast_to(column, (NZ, WIDTH)))
+    return jnp.concatenate(columns, axis=0)
+
+
 def first_yz_kernel(f_ref, part_ref):
     uy, uz = speeds_yz()
     y_up = uy > 0.0
@@ -188,35 +224,6 @@
         return carry
 
     lax.fori_loop(0, NY // BY, lines, 0)
-
-
-def cell_facts(step, vel_ref, space_ref, count_ref, cells_ref, rate_ref):
-    rank = vel_ref[0]
-    high, y_quarter, core = rank // 8, rank // 2 % 4, rank % 2
-    x_quarter = 2 * high + (core + high) % 2
-    count = count_ref[step, space_ref[0]]
-    shape = (LAYER, WIDTH)
-    slot = lax.broadcasted_iota(jnp.int32, shape, 0)
-    cell = (
-        (BX * x_quarter + (slot >> 6)) * LAYER + BY * NZ * y_quarter + (slot & (LINE - 1))
-    )
-    lane = lax.broadcasted_iota(jnp.int32, (1, WIDTH), 1)
-    found = jnp.zeros(shape, jnp.float32)
-    for i in range(CX * LAYER // WIDTH):
-        part = cells_ref[step : step + 1, WIDTH * i : WIDTH * (i + 1)]
-        part = jnp.where(lane + WIDTH * i < count, part, -1)
-        found = jnp.where(cell == part, 1.0, found)
-    kinetic = jnp.broadcast_to(jnp.max(found, axis=1, keepdims=True), shape) > 0.0
-    diagonal = lax.broadcasted_iota(jnp.int32, (NZ, NZ), 0) == lax.broadcasted_iota(
-        jnp.int32, (NZ, NZ), 1
-    )
-    columns = []
-    for x in range(BX):
-        for y in range(BY):
-            line = rate_ref[BX * x_quarter + x, pl.ds(BY * y_quarter + y, 1), :]
-            column = jnp.sum(jnp.where(diagonal, line, 0.0), axis=1, keepdims=True)
-            columns.append(jnp.broadcast_to(column, (NZ, WIDTH)))
-    return kinetic, jnp.concatenate(columns, axis=0)
 
 
 def collide(rows, a_ref, b_ref, c_ref, project_ref, mix_ref, expand_ref, w_ref, hidden_ref):
@@ -248,12 +255,14 @@
 
 
 def first_collide_kernel(
-    vel_ref, space_ref, count_ref, rows_ref, a_ref, b_ref, c_ref, project_ref, mix_ref,
-    expand_ref, w_ref, cells_ref, rate_ref,
-    f_ref, x_up_ref, x_down_ref, y_up_ref, y_down_ref, hidden_ref,
+    vel_ref, space_ref, count_ref, rows_ref, cells_ref, rate_ref, a_ref, b_ref, c_ref,
+    project_ref, mix_ref, expand_ref, w_ref,
+    f_ref, rates_ref, x_up_ref, x_down_ref, y_up_ref, y_down_ref, hidden_ref,
 ):
     rows = jnp.concatenate([rows_ref[g] for g in range(GROUPS)], axis=1)
-    kinetic, rate = cell_facts(0, vel_ref, space_ref, count_ref, cells_ref, rate_ref)
+    kinetic = kinetic_cells_of(0, vel_ref, space_ref, count_ref, cells_ref) > 0.0
+    rate = rates_of(vel_ref, rate_ref)
+    rates_ref[...] = rate
     half = GROUPS // 2
     low_lane = lax.broadcasted_iota(jnp.int32, (NZ, WIDTH), 1) < WIDTH // 2
     for g, collision, equilibrium in collide(
@@ -286,7 +295,8 @@
                 ).astype(jnp.bfloat16)
 
 
-def second_z_kernel(f_ref, part_ref):
+def second_z_kernel(vel_ref, space_ref, count_ref, f_ref, cells_ref, part_ref, mask_ref):
+    mask_ref[...] = kinetic_cells_of(1, vel_ref, space_ref, count_ref, cells_ref)
     _, uz = speeds_yz()
     z_up = uz > 0.0
 
@@ -301,7 +311,7 @@
 
 
 def second_xy_kernel(
-    f_ref, part_ref, x_below_ref, x_above_ref, y_below_ref, y_above_ref, moved_ref
+    f_ref, part_ref, y_below_ref, y_above_ref, x_below_ref, x_above_ref, moved_ref
 ):
     uy, _ = speeds_yz()
     y_up = uy > 0.0
@@ -374,11 +384,12 @@
 
 
 def second_collide_kernel(
-    vel_ref, space_ref, count_ref, moved_ref, a_ref, b_ref, c_ref, project_ref, mix_ref,
-    expand_ref, w_ref, cells_ref, rate_ref, out_ref, hidden_ref,
+    moved_ref, mask_ref, rates_ref, a_ref, b_ref, c_ref, project_ref, mix_ref, expand_ref, w_ref,
+    out_ref, hidden_ref,
 ):
     rows = jnp.concatenate([moved_ref[g].astype(jnp.bfloat16) for g in range(GROUPS)], axis=1)
-    kinetic, rate = cell_facts(1, vel_ref, space_ref, count_ref, cells_ref, rate_ref)
+    kinetic = mask_ref[...] > 0.0
+    rate = rates_ref[...]
     for g, collision, equilibrium in collide(
         rows, a_ref, b_ref, c_ref, project_ref, mix_ref, expand_ref, w_ref, hidden_ref
     ):
@@ -460,26 +471,29 @@
     )
     gathered = lax.all_to_all(rows, "vel", split_axis=0, concat_axis=0, tiled=True)
     facts = (vel, space, (kinetic_count, SMEM))
-    held = tuple((o, VMEM) for o in (map_a, map_b, map_c) + consts + (kinetic_cells, relax_rate))
-    f, up_x, down_x, up_y, down_y = call(
-        first_collide_kernel, "first_collide", facts + ((gathered, VMEM),) + held,
-        ((wide, jnp.float32, VMEM),) + ((halo, half, VMEM),) * 4,
+    lanes = ((LAYER, WIDTH), jnp.float32, VMEM)
+    held = tuple((o, VMEM) for o in (map_a, map_b, map_c) + consts)
+    f, rates, up_x, down_x, up_y, down_y = call(
+        first_collide_kernel, "first_collide",
+        facts + ((gathered, VMEM), (kinetic_cells, VMEM), (relax_rate, VMEM)) + held,
+        ((wide, jnp.float32, VMEM), lanes) + ((halo, half, VMEM),) * 4,
         scratch=(hidden,), flops=2_500_000_000, limit=C_VMEM,
     )
     y_below = lax.ppermute(up_y, both, y_up)
     y_above = lax.ppermute(down_y, both, y_down)
     x_below = lax.ppermute(up_x, both, x_up)
     x_above = lax.ppermute(down_x, both, x_down)
-    (part,) = call(
-        second_z_kernel, "second_z", ((f, VMEM),), ((wide, jnp.float32, VMEM),), flops=6_000_000
+    part, mask = call(
+        second_z_kernel, "second_z", facts + ((f, VMEM), (kinetic_cells, VMEM)),
+        ((wide, jnp.float32, VMEM), lanes), flops=6_000_000,
     )
     (moved,) = call(
         second_xy_kernel, "second_xy",
-        tuple((o, VMEM) for o in (f, part, x_below, x_above, y_below, y_above)),
+        tuple((o, VMEM) for o in (f, part, y_below, y_above, x_below, x_above)),
         ((wide, jnp.float32, VMEM),), flops=12_000_000,
     )
     (result,) = call(
-        second_collide_kernel, "second_collide", facts + ((moved, VMEM),) + held,
+        second_collide_kernel, "second_collide", ((moved, VMEM), (mask, VMEM), (rates, VMEM)) + held,
         ((wide, half, VMEM),), scratch=(hidden,), flops=2_500_000_000, limit=C_VMEM,
     )
     pieces = lax.all_to_all(result, "vel", split_axis=0, concat_axis=0, tiled=True)

time: 87.7 us -> 87 us (level)
  blocking collectives: 47.8 us -> 44.6 us
  waiting for transfers between devices: 10.2 us -> 12 us
    ppermute x1, waiting for transfers between devices: 0.01 us -> 3.91 us  [body(): y_below = lax.ppermute(up_y, both, y_up)]
    all_to_all x1, blocking collectives: 24.3 us -> 21.1 us  [body(): lax.all_to_all(result, 'vel', split_axis=0, concat_axis=0, tiled=True)]
    ppermute x1, waiting for transfers between devices: 7.29 us -> 5.41 us  [body(): x_above = lax.ppermute(down_x, both, x_down)]
  transfers between devices with their start and end apart: 6 -> 6, of which waited for: 3 -> 3; matrix products, arithmetic and copies ran while one was open for 0% -> 0% of each run, Pallas kernels for 5% -> 6%
where the time goes in v5:
time: 87 us; the launch traced here: 86.8 us
  blocking collectives  44.6 us (51%)
  Pallas kernels  18.3 us (21%)
  waiting for transfers between devices  12 us (14%)
  starting transfers between devices  10 us (11%)
  local copies, waits for them, and re-layouts  1.64 us (2%)
    all_to_all x1, blocking collectives, body(): lax.all_to_all(rows, 'vel', split_axis=0, concat_axis=0, tiled=True)  23.5 us
    all_to_all x1, blocking collectives, body(): lax.all_to_all(result, 'vel', split_axis=0, concat_axis=0, tiled=True)  21.1 us
    pallas_call x8, Pallas kernels, call(): pl.pallas_call(kernel, out_shape=tuple(shapes), in_specs=[pl.BlockSpec(me...  18.3 us
    ppermute x1, starting transfers between devices, body(): behind = lax.ppermute(behind, both, upwind)  5.67 us
    ppermute x1, waiting for transfers between devices, body(): x_above = lax.ppermute(down_x, both, x_down)  5.41 us
    ppermute x1, waiting for transfers between devices, body(): y_below = lax.ppermute(up_y, both, y_up)  3.91 us
    ppermute x1, waiting for transfers between devices, body(): ahead = lax.ppermute(ahead, both, downwind)  2.69 us
    ppermute x1, starting transfers between devices, body(): y_above = lax.ppermute(down_y, both, y_down)  2.66 us
  transfers between devices with their start and end apart: 6, of which 3 were waited for; matrix products, arithmetic and copies ran while one was open for 0% of the time, Pallas kernels for 6%

profile of v5, /device:TPU:1, one launch (start us, length us, event | category | flops | bytes accessed | tf_op | source)
XLA Modules:
  0.0 86.8 jit_solution(16263825498159711627)
XLA Ops:
  0.0 1.6 %copy-done = f32[16,16,16,128]{3,2,1,0:T(8,128)S(1)} copy-done((f32[16,16,16,128]{3,2,1,0:T(8,128)S(1)}, f32[16,16,16,128]{3,2,1,0:T(8,128)}, u32[]{:S(2)}) %copy-start) | copy-done | bytes 2097176
  1.6 5.7 %collective-permute-start = (bf16[2,16,16,128]{3,2,1,0:T(8,128)(2,1)S(1)}, bf16[2,16,16,128]{3,2,1,0:T(8,128)(2,1)S(1)}, u32[]{:S(2)}, u32[]{:S(2)}) collective-permute-start(bf16[2,16,16,128]{3,2,1,0:T(8,128)(2,1)S(1)} %get-tuple-element.15), channel_id=1, source_target_pairs={{0,112},{1,113},{2,114},{3,115},{4,116},{5,117},{6,118},{7,119},{8... | collective-permute-start | bytes 393224 | tf_op jit(solution)/shard_map/ppermute | solution.py:458
  7.3 0.0 collective-permute-start.1
  7.3 0.0 copy-start.10
  7.3 2.5 %first_yz.1.part_ref = f32[16,16,16,128]{3,2,1,0:T(8,128)S(1)} custom-call(f32[16,16,16,128]{3,2,1,0:T(8,128)S(1)} %copy-done), custom_call_target="tpu_custom_call" | custom-call | flops 12000000 | bytes 4194304 | tf_op jit(solution)/shard_map/first_yz/pallas_call | solution.py:80
  9.8 2.7 %collective-permute-done.1.ahead_ref = bf16[1,16,16,128]{3,2,1,0:T(8,128)(2,1)S(1)} collective-permute-done((bf16[1,16,16,128]{3,2,1,0:T(8,128)(2,1)S(1)}, bf16[1,16,16,128]{3,2,1,0:T(8,128)(2,1)S(1)}, u32[]{:S(2)}, u32[]{:S(2)}) %collective-permute-start.1) | collective-permute-done | bytes 65568 | tf_op jit(solution)/shard_map/ppermute | solution.py:459
  12.5 1.2 %first_x.1 = bf16[16,256,128]{2,1,0:T(8,128)(2,1)S(1)} custom-call(s32[1]{0:T(128)} %bitcast.vel_ref, f32[16,16,16,128]{3,2,1,0:T(8,128)S(1)} %copy-done, f32[16,16,16,128]{3,2,1,0:T(8,128)S(1)} %first_yz.1.part_ref, bf16[2,16,16,128]{3,2,1,0:T(8,128)(2,1)S(1)} %collective-permute-done.behind_ref, bf16[1,16,16,128]{3,2,1,0:T(8,128)(2,1)S(1)} %collective-permute-done.1.ahead_ref), custom_call_target="tpu_custom_call" | custom-call | flops 6000000 | bytes 5439492 | tf_op jit(solution)/shard_map/first_x/pallas_call | solution.py:80
  13.8 0.0 copy-start.4
  13.8 0.0 copy-start.5
  13.8 0.0 copy-start.6
  13.8 0.0 copy-start.7
  13.8 23.5 %all_to_all.10.rows_ref = bf16[16,256,128]{2,1,0:T(8,128)(2,1)S(1)} all-to-all(bf16[16,256,128]{2,1,0:T(8,128)(2,1)S(1)} %first_x.1), channel_id=1, replica_groups=mesh['space'=8,'vel'=16] {'vel'}, dimensions={0} | all-to-all | bytes 2097152 | tf_op jit(solution)/shard_map/all_to_all | solution.py:472
  37.4 4.6 %first_collide.1 = (f32[16,256,128]{2,1,0:T(8,128)S(1)}, f32[256,128]{1,0:T(8,128)S(1)}, bf16[24,64,128]{2,1,0:T(8,128)(2,1)S(1)}, bf16[24,64,128]{2,1,0:T(8,128...) custom-call(s32[1]{0:T(128)} %bitcast.vel_ref, s32[1]{0:T(128)} %bitcast.1.space_ref, ...), custom_call_target="tpu_custom_call" | custom-call | flops 2500000000 | bytes 15458376 | tf_op jit(solution)/shard_map/first_collide/pallas_call | solution.py:80
  42.0 0.1 collective-permute-start.2
  42.0 2.7 %collective-permute-start.3 = (bf16[24,64,128]{2,1,0:T(8,128)(2,1)S(1)}, bf16[24,64,128]{2,1,0:T(8,128)(2,1)S(1)}, u32[]{:S(2)}, u32[]{:S(2)}) collective-permute-start(bf16[24,64,128]{2,1,0:T(8,128)(2,1)S(1)} %get-tuple-element.20), channel_id=1, source_target_pairs={{2,0},{3,1},{4,2},{5,3},{6,4},{7,5},{0,6},{1,7},{10,8},{11,9},{12,... | collective-permute-start | bytes 1179656 | tf_op jit(solution)/shard_map/ppermute | solution.py:483
  44.7 0.9 %collective-permute-start.4 = (bf16[24,64,128]{2,1,0:T(8,128)(2,1)S(1)}, bf16[24,64,128]{2,1,0:T(8,128)(2,1)S(1)}, u32[]{:S(2)}, u32[]{:S(2)}) collective-permute-start(bf16[24,64,128]{2,1,0:T(8,128)(2,1)S(1)} %get-tuple-element.21), channel_id=1, source_target_pairs={{0,1},{1,9},{2,3},{3,11},{4,5},{5,13},{6,7},{7,15},{8,16},{9,8},{1... | collective-permute-start | bytes 1179656 | tf_op jit(solution)/shard_map/ppermute | solution.py:484
  45.6 0.7 collective-permute-start.5
  46.3 2.5 %second_z.1 = (f32[16,256,128]{2,1,0:T(8,128)S(1)}, f32[256,128]{1,0:T(8,128)S(1)}) custom-call(s32[1]{0:T(128)} %bitcast.vel_ref, s32[1]{0:T(128)} %bitcast.1.space_ref, s32[2,8]{1,0:T(2,128)S(1)} %copy-done.10, f32[16,256,128]{2,1,0:T(8,128)S(1)} %get-tuple-element.17.f_ref, s32[2,4096]{1,0:T(2,128)S(1)} %copy-done.8), custom_call_target="tpu_custom_call" | custom-call | flops 6000000 | bytes 4358216 | tf_op jit(solution)/shard_map/second_z/pallas_call | solution.py:80
  48.9 3.9 %collective-permute-done.2.y_below_ref = bf16[24,64,128]{2,1,0:T(8,128)(2,1)S(1)} collective-permute-done((bf16[24,64,128]{2,1,0:T(8,128)(2,1)S(1)}, bf16[24,64,128]{2,1,0:T(8,128)(2,1)S(1)}, u32[]{:S(2)}, u32[]{:S(2)}) %collective-permute-start.2) | collective-permute-done | bytes 393248 | tf_op jit(solution)/shard_map/ppermute | solution.py:482
  52.8 5.4 %collective-permute-done.5.x_above_ref = bf16[24,64,128]{2,1,0:T(8,128)(2,1)S(1)} collective-permute-done((bf16[24,64,128]{2,1,0:T(8,128)(2,1)S(1)}, bf16[24,64,128]{2,1,0:T(8,128)(2,1)S(1)}, u32[]{:S(2)}, u32[]{:S(2)}) %collective-permute-start.5) | collective-permute-done | bytes 393248 | tf_op jit(solution)/shard_map/ppermute | solution.py:485
  58.2 2.4 %second_xy.1.moved_ref = f32[16,256,128]{2,1,0:T(8,128)S(1)} custom-call(f32[16,256,128]{2,1,0:T(8,128)S(1)} %get-tuple-element.17.f_ref, f32[16,256,128]{2,1,0:T(8,128)S(1)} %get-tuple-element.18.part_ref, bf16[24,64,128]{2,1,0:T(8,128)(2,1)S(1)} %collective-permute-done.2.y_below_ref, bf16[24,64,128]{2,1,0:T(8,128)(2,1)S(1)} %collective-permute-done.3.y_above_ref, ...), custom_call_target="tpu_custom_call" | custom-call | flops 12000000 | bytes 7864320 | tf_op jit(solution)/shard_map/second_xy/pallas_call | solution.py:80
  60.6 3.7 %second_collide.1 = bf16[16,256,128]{2,1,0:T(8,128)(2,1)S(1)} custom-call(f32[16,256,128]{2,1,0:T(8,128)S(1)} %second_xy.1.moved_ref, f32[256,128]{1,0:T(8,128)S(1)} %get-tuple-element.23.mask_ref, f32[256,128]{1,0:T(8,128)S(1)} %get-tuple-element.24.rates_ref, bf16[2048,768]{1,0:T(8,128)(2,1)S(1)} %copy-done.1, bf16[2048,768]{1,0:T(8,128)(2,1)S(1)} %copy-done.2, ...), custom_call_target="tpu_custom_call" | custom-call | flops 2500000000 | bytes 13967360 | tf_op jit(solution)/shard_map/second_collide/pallas_call | solution.py:80
  64.3 21.1 %all_to_all.11.in_ref = bf16[16,256,128]{2,1,0:T(8,128)(2,1)S(1)} all-to-all(bf16[16,256,128]{2,1,0:T(8,128)(2,1)S(1)} %second_collide.1), channel_id=1, replica_groups=mesh['space'=8,'vel'=16] {'vel'}, dimensions={0} | all-to-all | bytes 2097152 | tf_op jit(solution)/shard_map/all_to_all | solution.py:499
  85.4 1.4 %place.1 = f32[16,16,16,128]{3,2,1,0:T(8,128)} custom-call(bf16[16,256,128]{2,1,0:T(8,128)(2,1)S(1)} %all_to_all.11.in_ref), custom_call_target="tpu_custom_call" | custom-call | bytes 3145728 | tf_op jit(solution)/shard_map/place/pallas_call | solution.py:80
  (20 shorter events, 0.1 us)
Async XLA Ops:
  0.0 1.6 %copy-start = (f32[16,16,16,128]{3,2,1,0:T(8,128)S(1)}, f32[16,16,16,128]{3,2,1,0:T(8,128)}, u32[]{:S(2)}) copy-start(f32[16,16,16,128]{3,2,1,0:T(8,128)} %f_ref.3) | copy-start | bytes 6291460
  1.6 10.9 %collective-permute-start = (bf16[2,16,16,128]{3,2,1,0:T(8,128)(2,1)S(1)}, bf16[2,16,16,128]{3,2,1,0:T(8,128)(2,1)S(1)}, u32[]{:S(2)}, u32[]{:S(2)}) collective-permute-start(bf16[2,16,16,128]{3,2,1,0:T(8,128)(2,1)S(1)} %get-tuple-element.15), channel_id=1, source_target_pairs={{0,112},{1,113},{2,114},{3,115},{4,116},{5,117},{6,118},{7,119},{8... | collective-permute-start | bytes 393224 | tf_op jit(solution)/shard_map/ppermute | solution.py:458
  7.3 5.2 %collective-permute-start.1 = (bf16[1,16,16,128]{3,2,1,0:T(8,128)(2,1)S(1)}, bf16[1,16,16,128]{3,2,1,0:T(8,128)(2,1)S(1)}, u32[]{:S(2)}, u32[]{:S(2)}) collective-permute-start(bf16[1,16,16,128]{3,2,1,0:T(8,128)(2,1)S(1)} %get-tuple-element.16), channel_id=1, source_target_pairs={{0,16},{1,17},{2,18},{3,19},{4,20},{5,21},{6,22},{7,23},{8,120},{9... | collective-permute-start | bytes 196616 | tf_op jit(solution)/shard_map/ppermute | solution.py:459
  7.3 30.0 %copy-start.3 = (bf16[768,2048]{1,0:T(8,128)(2,1)S(1)}, bf16[768,2048]{1,0:T(8,128)(2,1)}, u32[]{:S(2)}) copy-start(bf16[768,2048]{1,0:T(8,128)(2,1)} %c_ref.3) | copy-start | bytes 9437188
  7.3 30.0 %copy-start.8 = (s32[2,4096]{1,0:T(2,128)S(1)}, s32[2,4096]{1,0:T(2,128)}, u32[]{:S(2)}) copy-start(s32[2,4096]{1,0:T(2,128)} %cells_ref.3) | copy-start | bytes 98308
  7.3 30.0 %copy-start.9 = (f32[1,2048]{1,0:T(1,128)S(1)}, f32[1,2048]{1,0:T(1,128)}, u32[]{:S(2)}) copy-start(f32[1,2048]{1,0:T(1,128)} %constant.20.clone.w_ref) | copy-start | bytes 24580
  7.3 30.0 %copy-start.10 = (s32[2,8]{1,0:T(2,128)S(1)}, s32[2,8]{1,0:T(2,128)}, u32[]{:S(2)}) copy-start(s32[2,8]{1,0:T(2,128)} %count_ref.3) | copy-start | bytes 196
  12.5 24.8 %copy-start.1 = (bf16[2048,768]{1,0:T(8,128)(2,1)S(1)}, bf16[2048,768]{1,0:T(8,128)(2,1)}, u32[]{:S(2)}) copy-start(bf16[2048,768]{1,0:T(8,128)(2,1)} %a_ref.3) | copy-start | bytes 9437188
  12.5 24.8 %copy-start.2 = (bf16[2048,768]{1,0:T(8,128)(2,1)S(1)}, bf16[2048,768]{1,0:T(8,128)(2,1)}, u32[]{:S(2)}) copy-start(bf16[2048,768]{1,0:T(8,128)(2,1)} %b_ref.3) | copy-start | bytes 9437188
  13.8 23.6 %copy-start.4 = (bf16[128,2048]{1,0:T(8,128)(2,1)S(1)}, bf16[128,2048]{1,0:T(8,128)(2,1)}, u32[]{:S(2)}) copy-start(bf16[128,2048]{1,0:T(8,128)(2,1)} %constant.19.clone.expand_ref) | copy-start | bytes 1572868
  13.8 23.6 %copy-start.5 = (bf16[2048,128]{1,0:T(8,128)(2,1)S(1)}, bf16[2048,128]{1,0:T(8,128)(2,1)}, u32[]{:S(2)}) copy-start(bf16[2048,128]{1,0:T(8,128)(2,1)} %constant.17.clone.project_ref) | copy-start | bytes 1572868
  13.8 23.6 %copy-start.6 = (f32[128,128]{1,0:T(8,128)S(1)}, f32[128,128]{1,0:T(8,128)}, u32[]{:S(2)}) copy-start(f32[128,128]{1,0:T(8,128)} %constant.18.clone.mix_ref) | copy-start | bytes 196612
  13.8 23.6 %copy-start.7 = (f32[16,16,16]{2,1,0:T(8,128)S(1)}, f32[16,16,16]{2,1,0:T(8,128)}, u32[]{:S(2)}) copy-start(f32[16,16,16]{2,1,0:T(8,128)} %rate_ref.1) | copy-start | bytes 49156
  42.0 10.8 %collective-permute-start.2 = (bf16[24,64,128]{2,1,0:T(8,128)(2,1)S(1)}, bf16[24,64,128]{2,1,0:T(8,128)(2,1)S(1)}, u32[]{:S(2)}, u32[]{:S(2)}) collective-permute-start(bf16[24,64,128]{2,1,0:T(8,128)(2,1)S(1)} %get-tuple-element.19), channel_id=1, source_target_pairs={{0,2},{1,3},{2,4},{3,5},{4,6},{5,7},{6,0},{7,1},{8,10},{9,11},{10,... | collective-permute-start | bytes 1179656 | tf_op jit(solution)/shard_map/ppermute | solution.py:482
  42.0 10.7 %collective-permute-start.3 = (bf16[24,64,128]{2,1,0:T(8,128)(2,1)S(1)}, bf16[24,64,128]{2,1,0:T(8,128)(2,1)S(1)}, u32[]{:S(2)}, u32[]{:S(2)}) collective-permute-start(bf16[24,64,128]{2,1,0:T(8,128)(2,1)S(1)} %get-tuple-element.20), channel_id=1, source_target_pairs={{2,0},{3,1},{4,2},{5,3},{6,4},{7,5},{0,6},{1,7},{10,8},{11,9},{12,... | collective-permute-start | bytes 1179656 | tf_op jit(solution)/shard_map/ppermute | solution.py:483
  44.7 8.1 %collective-permute-start.4 = (bf16[24,64,128]{2,1,0:T(8,128)(2,1)S(1)}, bf16[24,64,128]{2,1,0:T(8,128)(2,1)S(1)}, u32[]{:S(2)}, u32[]{:S(2)}) collective-permute-start(bf16[24,64,128]{2,1,0:T(8,128)(2,1)S(1)} %get-tuple-element.21), channel_id=1, source_target_pairs={{0,1},{1,9},{2,3},{3,11},{4,5},{5,13},{6,7},{7,15},{8,16},{9,8},{1... | collective-permute-start | bytes 1179656 | tf_op jit(solution)/shard_map/ppermute | solution.py:484
  45.6 12.6 %collective-permute-start.5 = (bf16[24,64,128]{2,1,0:T(8,128)(2,1)S(1)}, bf16[24,64,128]{2,1,0:T(8,128)(2,1)S(1)}, u32[]{:S(2)}, u32[]{:S(2)}) collective-permute-start(bf16[24,64,128]{2,1,0:T(8,128)(2,1)S(1)} %get-tuple-element.22), channel_id=1, source_target_pairs={{1,0},{9,1},{3,2},{11,3},{5,4},{13,5},{7,6},{15,7},{16,8},{8,9},{1... | collective-permute-start | bytes 1179656 | tf_op jit(solution)/shard_map/ppermute | solution.py:485

commit v6 on v5

--- a/solution.py
+++ b/solution.py
@@ -121,13 +121,13 @@
     ahead_ref[0] = dist_ref[jnp.where(forward, 0, CX - 1)].astype(jnp.bfloat16)
 
 
-def quarters(rank):
-    high, core = rank // 8, rank % 2
+def quarters(rank, space):
+    high, core = (rank // 8 + space) % 2, rank % 2
     return 2 * high + (core + high) % 2, rank // 2 % 4
 
 
 def kinetic_cells_of(step, vel_ref, space_ref, count_ref, cells_ref):
-    x_quarter, y_quarter = quarters(vel_ref[0])
+    x_quarter, y_quarter = quarters(vel_ref[0], space_ref[0])
     count = count_ref[step, space_ref[0]]
     shape = (LAYER, WIDTH)
     slot = lax.broadcasted_iota(jnp.int32, shape, 0)
@@ -143,8 +143,8 @@
     return jnp.broadcast_to(jnp.max(found, axis=1, keepdims=True), shape)
 
 
-def rates_of(vel_ref, rate_ref):
-    x_quarter, y_quarter = quarters(vel_ref[0])
+def rates_of(vel_ref, space_ref, rate_ref):
+    x_quarter, y_quarter = quarters(vel_ref[0], space_ref[0])
     diagonal = lax.broadcasted_iota(jnp.int32, (NZ, NZ), 0) == lax.broadcasted_iota(
         jnp.int32, (NZ, NZ), 1
     )
@@ -181,7 +181,7 @@
     lax.fori_loop(0, CX, layer, 0)
 
 
-def first_x_kernel(vel_ref, f_ref, part_ref, behind_ref, ahead_ref, rows_ref):
+def first_x_kernel(vel_ref, space_ref, f_ref, part_ref, behind_ref, ahead_ref, rows_ref):
     rank = vel_ref[0]
     forward = rank >= GROUPS // 2
     ux = jnp.abs(rank.astype(jnp.float32) - 0.5 * (GX - 1)) * (SPACING * COURANT)
@@ -191,7 +191,7 @@
     for k in range(4):
         quarter = jnp.where(forward, k, 3 - k)
         high = quarter // 2
-        owners.append(high * (GROUPS // 2) + (quarter + high) % 2)
+        owners.append((high + space_ref[0]) % 2 * (GROUPS // 2) + (quarter + high) % 2)
 
     def line(quarter, y):
         inner = y * NZ
@@ -261,7 +261,7 @@
 ):
     rows = jnp.concatenate([rows_ref[g] for g in range(GROUPS)], axis=1)
     kinetic = kinetic_cells_of(0, vel_ref, space_ref, count_ref, cells_ref) > 0.0
-    rate = rates_of(vel_ref, rate_ref)
+    rate = rates_of(vel_ref, space_ref, rate_ref)
     rates_ref[...] = rate
     half = GROUPS // 2
     low_lane = lax.broadcasted_iota(jnp.int32, (NZ, WIDTH), 1) < WIDTH // 2
@@ -398,17 +398,18 @@
         out_ref[g] = (moved + change).astype(jnp.bfloat16)
 
 
-def place_kernel(in_ref, out_hbm, out_ref, sems):
+def place_kernel(space_ref, in_ref, out_hbm, out_ref, sems):
     stores = []
     for quarter in range(4):
         high = quarter // 2
         core = (quarter % 2) ^ high
+        first = (high + space_ref[0]) % 2 * (GROUPS // 2) + core
         for x in range(BX):
             for y_quarter in range(4):
                 for y in range(BY):
                     c = LINE * x + NZ * y
                     out_ref[BX * quarter + x, BY * y_quarter + y] = in_ref[
-                        high * (GROUPS // 2) + y_quarter * 2 + core, c : c + NZ
+                        first + y_quarter * 2, c : c + NZ
                     ].astype(jnp.float32)
         part = slice(BX * quarter, BX * (quarter + 1))
         stores.append(pltpu.make_async_copy(out_ref.at[part], out_hbm.at[part], sems.at[quarter]))
@@ -419,6 +420,11 @@
 
 def device_of(space, high, x, core):
     return (space * 2 + high) * 8 + x * 2 + core
+
+
+def holder_of(space, quarter, x):
+    high = quarter // 2
+    return device_of(space, (high + space) % 2, x, (quarter + high) % 2)
 
 
 def steps_of(slabs):
@@ -432,12 +438,10 @@
                     before = device_of((space - 1) % slabs, high, x, core)
                     upwind.append((me, after if high else before))
                     downwind.append((me, before if high else after))
-                    quarter = 2 * high + (core ^ high)
+                    turned = (high + space) % 2
+                    quarter = 2 * turned + (core + turned) % 2
                     next_slab = (space + (quarter == 3)) % slabs
-                    quarter = (quarter + 1) % 4
-                    x_up.append(
-                        (me, device_of(next_slab, quarter // 2, x, (quarter % 2) ^ (quarter // 2)))
-                    )
+                    x_up.append((me, holder_of(next_slab, (quarter + 1) % 4, x)))
                     y_up.append((me, device_of(space, high, (x + 1) % 4, core)))
     back = lambda pairs: [(target, source) for source, target in pairs]
     return upwind, downwind, x_up, back(x_up), y_up, back(y_up)
@@ -466,7 +470,7 @@
 
     (part,) = call(first_yz_kernel, "first_yz", ((dist, VMEM),), (state,), flops=12_000_000)
     (rows,) = call(
-        first_x_kernel, "first_x", (vel,) + tuple((o, VMEM) for o in (dist, part, behind, ahead)),
+        first_x_kernel, "first_x", (vel, space) + tuple((o, VMEM) for o in (dist, part, behind, ahead)),
         ((wide, half, VMEM),), flops=6_000_000,
     )
     gathered = lax.all_to_all(rows, "vel", split_axis=0, concat_axis=0, tiled=True)
@@ -498,7 +502,7 @@
     )
     pieces = lax.all_to_all(result, "vel", split_axis=0, concat_axis=0, tiled=True)
     (out,) = call(
-        place_kernel, "place", ((pieces, VMEM),), (((CX,) + layers, jnp.float32, HBM),),
+        place_kernel, "place", (space, (pieces, VMEM)), (((CX,) + layers, jnp.float32, HBM),),
         scratch=(VMEM((CX,) + layers, jnp.float32), DMA((4,))),
     )
     return out

time: 87 us -> 86.6 us (level)
  waiting for transfers between devices: 12 us -> 7.88 us
  blocking collectives: 44.6 us -> 48.3 us
    ppermute x1, waiting for transfers between devices: 5.41 us -> 1.24 us  [body(): x_above = lax.ppermute(down_x, both, x_down)]
    all_to_all x1, blocking collectives: 21.1 us -> 24.8 us  [body(): lax.all_to_all(result, 'vel', split_axis=0, concat_axis=0, tiled=True)]
where the time goes in v6:
time: 86.6 us; the launch traced here: 86.4 us
  blocking collectives  48.3 us (56%)
  Pallas kernels  18.4 us (21%)
  starting transfers between devices  10 us (12%)
  waiting for transfers between devices  7.88 us (9%)
  local copies, waits for them, and re-layouts  1.64 us (2%)
    all_to_all x1, blocking collectives, body(): lax.all_to_all(result, 'vel', split_axis=0, concat_axis=0, tiled=True)  24.8 us
    all_to_all x1, blocking collectives, body(): lax.all_to_all(rows, 'vel', split_axis=0, concat_axis=0, tiled=True)  23.5 us
    pallas_call x8, Pallas kernels, call(): pl.pallas_call(kernel, out_shape=tuple(shapes), in_specs=[pl.BlockSpec(me...  18.4 us
    ppermute x1, starting transfers between devices, body(): behind = lax.ppermute(behind, both, upwind)  5.67 us
    ppermute x1, waiting for transfers between devices, body(): y_below = lax.ppermute(up_y, both, y_up)  3.93 us
    ppermute x1, waiting for transfers between devices, body(): ahead = lax.ppermute(ahead, both, downwind)  2.7 us
    ppermute x1, starting transfers between devices, body(): y_above = lax.ppermute(down_y, both, y_down)  2.66 us
  transfers between devices with their start and end apart: 6, of which 3 were waited for; matrix products, arithmetic and copies ran while one was open for 0% of the time, Pallas kernels for 6%

profile of v6, /device:TPU:1, one launch (start us, length us, event | category | flops | bytes accessed | tf_op | source)
XLA Modules:
  0.0 86.4 jit_solution(9127754525605764937)
XLA Ops:
  0.0 1.6 %copy-done = f32[16,16,16,128]{3,2,1,0:T(8,128)S(1)} copy-done((f32[16,16,16,128]{3,2,1,0:T(8,128)S(1)}, f32[16,16,16,128]{3,2,1,0:T(8,128)}, u32[]{:S(2)}) %copy-start) | copy-done | bytes 2097176
  1.6 5.7 %collective-permute-start = (bf16[2,16,16,128]{3,2,1,0:T(8,128)(2,1)S(1)}, bf16[2,16,16,128]{3,2,1,0:T(8,128)(2,1)S(1)}, u32[]{:S(2)}, u32[]{:S(2)}) collective-permute-start(bf16[2,16,16,128]{3,2,1,0:T(8,128)(2,1)S(1)} %get-tuple-element.15), channel_id=1, source_target_pairs={{0,112},{1,113},{2,114},{3,115},{4,116},{5,117},{6,118},{7,119},{8... | collective-permute-start | bytes 393224 | tf_op jit(solution)/shard_map/ppermute | solution.py:462
  7.3 0.0 collective-permute-start.1
  7.3 2.5 %first_yz.1.part_ref = f32[16,16,16,128]{3,2,1,0:T(8,128)S(1)} custom-call(f32[16,16,16,128]{3,2,1,0:T(8,128)S(1)} %copy-done), custom_call_target="tpu_custom_call" | custom-call | flops 12000000 | bytes 4194304 | tf_op jit(solution)/shard_map/first_yz/pallas_call | solution.py:80
  9.8 2.7 %collective-permute-done.1.ahead_ref = bf16[1,16,16,128]{3,2,1,0:T(8,128)(2,1)S(1)} collective-permute-done((bf16[1,16,16,128]{3,2,1,0:T(8,128)(2,1)S(1)}, bf16[1,16,16,128]{3,2,1,0:T(8,128)(2,1)S(1)}, u32[]{:S(2)}, u32[]{:S(2)}) %collective-permute-start.1) | collective-permute-done | bytes 65568 | tf_op jit(solution)/shard_map/ppermute | solution.py:463
  12.5 1.3 %first_x.1 = bf16[16,256,128]{2,1,0:T(8,128)(2,1)S(1)} custom-call(s32[1]{0:T(128)} %bitcast.1.vel_ref, s32[1]{0:T(128)} %bitcast.space_ref, f32[16,16,16,128]{3,2,1,0:T(8,128)S(1)} %copy-done, f32[16,16,16,128]{3,2,1,0:T(8,128)S(1)} %first_yz.1.part_ref, bf16[2,16,16,128]{3,2,1,0:T(8,128)(2,1)S(1)} %collective-permute-done.behind_ref, ...), custom_call_target="tpu_custom_call" | custom-call | flops 6000000 | bytes 5439496 | tf_op jit(solution)/shard_map/first_x/pallas_call | solution.py:80
  13.8 0.0 copy-start.4
  13.8 0.0 copy-start.5
  13.8 0.0 copy-start.6
  13.8 0.0 copy-start.7
  13.8 0.0 copy-start.10
  13.8 23.5 %all_to_all.10.rows_ref = bf16[16,256,128]{2,1,0:T(8,128)(2,1)S(1)} all-to-all(bf16[16,256,128]{2,1,0:T(8,128)(2,1)S(1)} %first_x.1), channel_id=1, replica_groups=mesh['space'=8,'vel'=16] {'vel'}, dimensions={0} | all-to-all | bytes 2097152 | tf_op jit(solution)/shard_map/all_to_all | solution.py:476
  37.4 4.7 %first_collide.1 = (f32[16,256,128]{2,1,0:T(8,128)S(1)}, f32[256,128]{1,0:T(8,128)S(1)}, bf16[24,64,128]{2,1,0:T(8,128)(2,1)S(1)}, bf16[24,64,128]{2,1,0:T(8,128...) custom-call(s32[1]{0:T(128)} %bitcast.1.vel_ref, s32[1]{0:T(128)} %bitcast.space_ref, ...), custom_call_target="tpu_custom_call" | custom-call | flops 2500000000 | bytes 15458376 | tf_op jit(solution)/shard_map/first_collide/pallas_call | solution.py:80
  42.1 0.1 collective-permute-start.2
  42.1 2.7 %collective-permute-start.3 = (bf16[24,64,128]{2,1,0:T(8,128)(2,1)S(1)}, bf16[24,64,128]{2,1,0:T(8,128)(2,1)S(1)}, u32[]{:S(2)}, u32[]{:S(2)}) collective-permute-start(bf16[24,64,128]{2,1,0:T(8,128)(2,1)S(1)} %get-tuple-element.20), channel_id=1, source_target_pairs={{2,0},{3,1},{4,2},{5,3},{6,4},{7,5},{0,6},{1,7},{10,8},{11,9},{12,... | collective-permute-start | bytes 1179656 | tf_op jit(solution)/shard_map/ppermute | solution.py:487
  44.8 0.9 %collective-permute-start.4 = (bf16[24,64,128]{2,1,0:T(8,128)(2,1)S(1)}, bf16[24,64,128]{2,1,0:T(8,128)(2,1)S(1)}, u32[]{:S(2)}, u32[]{:S(2)}) collective-permute-start(bf16[24,64,128]{2,1,0:T(8,128)(2,1)S(1)} %get-tuple-element.21), channel_id=1, source_target_pairs={{0,1},{1,9},{2,3},{3,11},{4,5},{5,13},{6,7},{7,15},{8,24},{9,8},{1... | collective-permute-start | bytes 1179656 | tf_op jit(solution)/shard_map/ppermute | solution.py:488
  45.7 0.7 collective-permute-start.5
  46.4 2.5 %second_z.1 = (f32[16,256,128]{2,1,0:T(8,128)S(1)}, f32[256,128]{1,0:T(8,128)S(1)}) custom-call(s32[1]{0:T(128)} %bitcast.1.vel_ref, s32[1]{0:T(128)} %bitcast.space_ref, s32[2,8]{1,0:T(2,128)S(1)} %copy-done.10, f32[16,256,128]{2,1,0:T(8,128)S(1)} %get-tuple-element.17.f_ref, s32[2,4096]{1,0:T(2,128)S(1)} %copy-done.8), custom_call_target="tpu_custom_call" | custom-call | flops 6000000 | bytes 4358216 | tf_op jit(solution)/shard_map/second_z/pallas_call | solution.py:80
  49.0 3.9 %collective-permute-done.2.y_below_ref = bf16[24,64,128]{2,1,0:T(8,128)(2,1)S(1)} collective-permute-done((bf16[24,64,128]{2,1,0:T(8,128)(2,1)S(1)}, bf16[24,64,128]{2,1,0:T(8,128)(2,1)S(1)}, u32[]{:S(2)}, u32[]{:S(2)}) %collective-permute-start.2) | collective-permute-done | bytes 393248 | tf_op jit(solution)/shard_map/ppermute | solution.py:486
  52.9 1.2 %collective-permute-done.5.x_above_ref = bf16[24,64,128]{2,1,0:T(8,128)(2,1)S(1)} collective-permute-done((bf16[24,64,128]{2,1,0:T(8,128)(2,1)S(1)}, bf16[24,64,128]{2,1,0:T(8,128)(2,1)S(1)}, u32[]{:S(2)}, u32[]{:S(2)}) %collective-permute-start.5) | collective-permute-done | bytes 393248 | tf_op jit(solution)/shard_map/ppermute | solution.py:489
  54.1 2.4 %second_xy.1.moved_ref = f32[16,256,128]{2,1,0:T(8,128)S(1)} custom-call(f32[16,256,128]{2,1,0:T(8,128)S(1)} %get-tuple-element.17.f_ref, f32[16,256,128]{2,1,0:T(8,128)S(1)} %get-tuple-element.18.part_ref, bf16[24,64,128]{2,1,0:T(8,128)(2,1)S(1)} %collective-permute-done.2.y_below_ref, bf16[24,64,128]{2,1,0:T(8,128)(2,1)S(1)} %collective-permute-done.3.y_above_ref, ...), custom_call_target="tpu_custom_call" | custom-call | flops 12000000 | bytes 7864320 | tf_op jit(solution)/shard_map/second_xy/pallas_call | solution.py:80
  56.5 3.7 %second_collide.1 = bf16[16,256,128]{2,1,0:T(8,128)(2,1)S(1)} custom-call(f32[16,256,128]{2,1,0:T(8,128)S(1)} %second_xy.1.moved_ref, f32[256,128]{1,0:T(8,128)S(1)} %get-tuple-element.23.mask_ref, f32[256,128]{1,0:T(8,128)S(1)} %get-tuple-element.24.rates_ref, bf16[2048,768]{1,0:T(8,128)(2,1)S(1)} %copy-done.1, bf16[2048,768]{1,0:T(8,128)(2,1)S(1)} %copy-done.2, ...), custom_call_target="tpu_custom_call" | custom-call | flops 2500000000 | bytes 13967360 | tf_op jit(solution)/shard_map/second_collide/pallas_call | solution.py:80
  60.2 24.8 %all_to_all.11.in_ref = bf16[16,256,128]{2,1,0:T(8,128)(2,1)S(1)} all-to-all(bf16[16,256,128]{2,1,0:T(8,128)(2,1)S(1)} %second_collide.1), channel_id=1, replica_groups=mesh['space'=8,'vel'=16] {'vel'}, dimensions={0} | all-to-all | bytes 2097152 | tf_op jit(solution)/shard_map/all_to_all | solution.py:503
  85.0 1.4 %place.1 = f32[16,16,16,128]{3,2,1,0:T(8,128)} custom-call(s32[1]{0:T(128)} %bitcast.space_ref, bf16[16,256,128]{2,1,0:T(8,128)(2,1)S(1)} %all_to_all.11.in_ref), custom_call_target="tpu_custom_call" | custom-call | bytes 3145732 | tf_op jit(solution)/shard_map/place/pallas_call | solution.py:80
  (20 shorter events, 0.1 us)
Async XLA Ops:
  0.0 1.6 %copy-start = (f32[16,16,16,128]{3,2,1,0:T(8,128)S(1)}, f32[16,16,16,128]{3,2,1,0:T(8,128)}, u32[]{:S(2)}) copy-start(f32[16,16,16,128]{3,2,1,0:T(8,128)} %f_ref.3) | copy-start | bytes 6291460
  1.6 10.9 %collective-permute-start = (bf16[2,16,16,128]{3,2,1,0:T(8,128)(2,1)S(1)}, bf16[2,16,16,128]{3,2,1,0:T(8,128)(2,1)S(1)}, u32[]{:S(2)}, u32[]{:S(2)}) collective-permute-start(bf16[2,16,16,128]{3,2,1,0:T(8,128)(2,1)S(1)} %get-tuple-element.15), channel_id=1, source_target_pairs={{0,112},{1,113},{2,114},{3,115},{4,116},{5,117},{6,118},{7,119},{8... | collective-permute-start | bytes 393224 | tf_op jit(solution)/shard_map/ppermute | solution.py:462
  7.3 5.2 %collective-permute-start.1 = (bf16[1,16,16,128]{3,2,1,0:T(8,128)(2,1)S(1)}, bf16[1,16,16,128]{3,2,1,0:T(8,128)(2,1)S(1)}, u32[]{:S(2)}, u32[]{:S(2)}) collective-permute-start(bf16[1,16,16,128]{3,2,1,0:T(8,128)(2,1)S(1)} %get-tuple-element.16), channel_id=1, source_target_pairs={{0,16},{1,17},{2,18},{3,19},{4,20},{5,21},{6,22},{7,23},{8,120},{9... | collective-permute-start | bytes 196616 | tf_op jit(solution)/shard_map/ppermute | solution.py:463
  7.3 30.0 %copy-start.3 = (bf16[768,2048]{1,0:T(8,128)(2,1)S(1)}, bf16[768,2048]{1,0:T(8,128)(2,1)}, u32[]{:S(2)}) copy-start(bf16[768,2048]{1,0:T(8,128)(2,1)} %c_ref.3) | copy-start | bytes 9437188
  7.3 30.0 %copy-start.8 = (s32[2,4096]{1,0:T(2,128)S(1)}, s32[2,4096]{1,0:T(2,128)}, u32[]{:S(2)}) copy-start(s32[2,4096]{1,0:T(2,128)} %cells_ref.3) | copy-start | bytes 98308
  7.3 30.0 %copy-start.9 = (f32[1,2048]{1,0:T(1,128)S(1)}, f32[1,2048]{1,0:T(1,128)}, u32[]{:S(2)}) copy-start(f32[1,2048]{1,0:T(1,128)} %constant.20.clone.w_ref) | copy-start | bytes 24580
  12.5 24.8 %copy-start.1 = (bf16[2048,768]{1,0:T(8,128)(2,1)S(1)}, bf16[2048,768]{1,0:T(8,128)(2,1)}, u32[]{:S(2)}) copy-start(bf16[2048,768]{1,0:T(8,128)(2,1)} %a_ref.3) | copy-start | bytes 9437188
  12.5 24.8 %copy-start.2 = (bf16[2048,768]{1,0:T(8,128)(2,1)S(1)}, bf16[2048,768]{1,0:T(8,128)(2,1)}, u32[]{:S(2)}) copy-start(bf16[2048,768]{1,0:T(8,128)(2,1)} %b_ref.3) | copy-start | bytes 9437188
  13.8 23.6 %copy-start.4 = (bf16[128,2048]{1,0:T(8,128)(2,1)S(1)}, bf16[128,2048]{1,0:T(8,128)(2,1)}, u32[]{:S(2)}) copy-start(bf16[128,2048]{1,0:T(8,128)(2,1)} %constant.19.clone.expand_ref) | copy-start | bytes 1572868
  13.8 23.6 %copy-start.5 = (bf16[2048,128]{1,0:T(8,128)(2,1)S(1)}, bf16[2048,128]{1,0:T(8,128)(2,1)}, u32[]{:S(2)}) copy-start(bf16[2048,128]{1,0:T(8,128)(2,1)} %constant.17.clone.project_ref) | copy-start | bytes 1572868
  13.8 23.6 %copy-start.6 = (f32[128,128]{1,0:T(8,128)S(1)}, f32[128,128]{1,0:T(8,128)}, u32[]{:S(2)}) copy-start(f32[128,128]{1,0:T(8,128)} %constant.18.clone.mix_ref) | copy-start | bytes 196612
  13.8 23.6 %copy-start.7 = (f32[16,16,16]{2,1,0:T(8,128)S(1)}, f32[16,16,16]{2,1,0:T(8,128)}, u32[]{:S(2)}) copy-start(f32[16,16,16]{2,1,0:T(8,128)} %rate_ref.1) | copy-start | bytes 49156
  13.8 23.6 %copy-start.10 = (s32[2,8]{1,0:T(2,128)S(1)}, s32[2,8]{1,0:T(2,128)}, u32[]{:S(2)}) copy-start(s32[2,8]{1,0:T(2,128)} %count_ref.3) | copy-start | bytes 196
  42.1 10.8 %collective-permute-start.2 = (bf16[24,64,128]{2,1,0:T(8,128)(2,1)S(1)}, bf16[24,64,128]{2,1,0:T(8,128)(2,1)S(1)}, u32[]{:S(2)}, u32[]{:S(2)}) collective-permute-start(bf16[24,64,128]{2,1,0:T(8,128)(2,1)S(1)} %get-tuple-element.19), channel_id=1, source_target_pairs={{0,2},{1,3},{2,4},{3,5},{4,6},{5,7},{6,0},{7,1},{8,10},{9,11},{10,... | collective-permute-start | bytes 1179656 | tf_op jit(solution)/shard_map/ppermute | solution.py:486
  42.1 10.7 %collective-permute-start.3 = (bf16[24,64,128]{2,1,0:T(8,128)(2,1)S(1)}, bf16[24,64,128]{2,1,0:T(8,128)(2,1)S(1)}, u32[]{:S(2)}, u32[]{:S(2)}) collective-permute-start(bf16[24,64,128]{2,1,0:T(8,128)(2,1)S(1)} %get-tuple-element.20), channel_id=1, source_target_pairs={{2,0},{3,1},{4,2},{5,3},{6,4},{7,5},{0,6},{1,7},{10,8},{11,9},{12,... | collective-permute-start | bytes 1179656 | tf_op jit(solution)/shard_map/ppermute | solution.py:487
  44.8 8.1 %collective-permute-start.4 = (bf16[24,64,128]{2,1,0:T(8,128)(2,1)S(1)}, bf16[24,64,128]{2,1,0:T(8,128)(2,1)S(1)}, u32[]{:S(2)}, u32[]{:S(2)}) collective-permute-start(bf16[24,64,128]{2,1,0:T(8,128)(2,1)S(1)} %get-tuple-element.21), channel_id=1, source_target_pairs={{0,1},{1,9},{2,3},{3,11},{4,5},{5,13},{6,7},{7,15},{8,24},{9,8},{1... | collective-permute-start | bytes 1179656 | tf_op jit(solution)/shard_map/ppermute | solution.py:488
  45.7 8.4 %collective-permute-start.5 = (bf16[24,64,128]{2,1,0:T(8,128)(2,1)S(1)}, bf16[24,64,128]{2,1,0:T(8,128)(2,1)S(1)}, u32[]{:S(2)}, u32[]{:S(2)}) collective-permute-start(bf16[24,64,128]{2,1,0:T(8,128)(2,1)S(1)} %get-tuple-element.22), channel_id=1, source_target_pairs={{1,0},{9,1},{3,2},{11,3},{5,4},{13,5},{7,6},{15,7},{24,8},{8,9},{2... | collective-permute-start | bytes 1179656 | tf_op jit(solution)/shard_map/ppermute | solution.py:489

commit v7 on v6

--- a/solution.py
+++ b/solution.py
@@ -311,7 +311,7 @@
 
 
 def second_xy_kernel(
-    f_ref, part_ref, y_below_ref, y_above_ref, x_below_ref, x_above_ref, moved_ref
+    f_ref, part_ref, x_below_ref, y_below_ref, x_above_ref, y_above_ref, moved_ref
 ):
     uy, _ = speeds_yz()
     y_up = uy > 0.0
@@ -493,7 +493,7 @@
     )
     (moved,) = call(
         second_xy_kernel, "second_xy",
-        tuple((o, VMEM) for o in (f, part, y_below, y_above, x_below, x_above)),
+        tuple((o, VMEM) for o in (f, part, x_below, y_below, x_above, y_above)),
         ((wide, jnp.float32, VMEM),), flops=12_000_000,
     )
     (result,) = call(

time: 86.6 us -> 85.3 us (0.985)
  blocking collectives: 48.3 us -> 46.4 us
    ppermute x1, waiting for transfers between devices: 3.93 us -> 5.93 us  [body(): y_below = lax.ppermute(up_y, both, y_up)]
    all_to_all x1, blocking collectives: 24.8 us -> 22.9 us  [body(): lax.all_to_all(result, 'vel', split_axis=0, concat_axis=0, tiled=True)]
    ppermute x1, waiting for transfers between devices: 1.24 us -> 0.01 us  [body(): x_above = lax.ppermute(down_x, both, x_down)]
  transfers between devices with their start and end apart: 6 -> 6, of which waited for: 3 -> 2; matrix products, arithmetic and copies ran while one was open for 0% -> 0% of each run, Pallas kernels for 6% -> 6%
where the time goes in v7:
time: 85.3 us; the launch traced here: 85.1 us
  blocking collectives  46.4 us (54%)
  Pallas kernels  18.4 us (22%)
  starting transfers between devices  9.84 us (12%)
  waiting for transfers between devices  8.65 us (10%)
  local copies, waits for them, and re-layouts  1.64 us (2%)
    all_to_all x1, blocking collectives, body(): lax.all_to_all(rows, 'vel', split_axis=0, concat_axis=0, tiled=True)  23.5 us
    all_to_all x1, blocking collectives, body(): lax.all_to_all(result, 'vel', split_axis=0, concat_axis=0, tiled=True)  22.9 us
    pallas_call x8, Pallas kernels, call(): pl.pallas_call(kernel, out_shape=tuple(shapes), in_specs=[pl.BlockSpec(me...  18.4 us
    ppermute x1, waiting for transfers between devices, body(): y_below = lax.ppermute(up_y, both, y_up)  5.93 us
    ppermute x1, starting transfers between devices, body(): behind = lax.ppermute(behind, both, upwind)  5.67 us
    ppermute x1, starting transfers between devices, body(): y_above = lax.ppermute(down_y, both, y_down)  2.86 us
    ppermute x1, waiting for transfers between devices, body(): ahead = lax.ppermute(ahead, both, downwind)  2.7 us
  transfers between devices with their start and end apart: 6, of which 2 were waited for; matrix products, arithmetic and copies ran while one was open for 0% of the time, Pallas kernels for 6%

profile of v7, /device:TPU:1, one launch (start us, length us, event | category | flops | bytes accessed | tf_op | source)
XLA Modules:
  0.0 85.1 jit_solution(428740396580239669)
XLA Ops:
  0.0 1.6 %copy-done = f32[16,16,16,128]{3,2,1,0:T(8,128)S(1)} copy-done((f32[16,16,16,128]{3,2,1,0:T(8,128)S(1)}, f32[16,16,16,128]{3,2,1,0:T(8,128)}, u32[]{:S(2)}) %copy-start) | copy-done | bytes 2097176
  1.6 5.7 %collective-permute-start = (bf16[2,16,16,128]{3,2,1,0:T(8,128)(2,1)S(1)}, bf16[2,16,16,128]{3,2,1,0:T(8,128)(2,1)S(1)}, u32[]{:S(2)}, u32[]{:S(2)}) collective-permute-start(bf16[2,16,16,128]{3,2,1,0:T(8,128)(2,1)S(1)} %get-tuple-element.15), channel_id=1, source_target_pairs={{0,112},{1,113},{2,114},{3,115},{4,116},{5,117},{6,118},{7,119},{8... | collective-permute-start | bytes 393224 | tf_op jit(solution)/shard_map/ppermute | solution.py:462
  7.3 0.0 collective-permute-start.1
  7.3 2.5 %first_yz.1.part_ref = f32[16,16,16,128]{3,2,1,0:T(8,128)S(1)} custom-call(f32[16,16,16,128]{3,2,1,0:T(8,128)S(1)} %copy-done), custom_call_target="tpu_custom_call" | custom-call | flops 12000000 | bytes 4194304 | tf_op jit(solution)/shard_map/first_yz/pallas_call | solution.py:80
  9.8 2.7 %collective-permute-done.1.ahead_ref = bf16[1,16,16,128]{3,2,1,0:T(8,128)(2,1)S(1)} collective-permute-done((bf16[1,16,16,128]{3,2,1,0:T(8,128)(2,1)S(1)}, bf16[1,16,16,128]{3,2,1,0:T(8,128)(2,1)S(1)}, u32[]{:S(2)}, u32[]{:S(2)}) %collective-permute-start.1) | collective-permute-done | bytes 65568 | tf_op jit(solution)/shard_map/ppermute | solution.py:463
  12.5 0.0 collective-permute-done.behind_ref
  12.5 1.3 %first_x.1 = bf16[16,256,128]{2,1,0:T(8,128)(2,1)S(1)} custom-call(s32[1]{0:T(128)} %bitcast.1.vel_ref, s32[1]{0:T(128)} %bitcast.space_ref, f32[16,16,16,128]{3,2,1,0:T(8,128)S(1)} %copy-done, f32[16,16,16,128]{3,2,1,0:T(8,128)S(1)} %first_yz.1.part_ref, bf16[2,16,16,128]{3,2,1,0:T(8,128)(2,1)S(1)} %collective-permute-done.behind_ref, ...), custom_call_target="tpu_custom_call" | custom-call | flops 6000000 | bytes 5439496 | tf_op jit(solution)/shard_map/first_x/pallas_call | solution.py:80
  13.8 0.0 copy-start.4
  13.8 0.0 copy-start.5
  13.8 0.0 copy-start.6
  13.8 0.0 copy-start.7
  13.8 0.0 copy-start.10
  13.8 23.5 %all_to_all.10.rows_ref = bf16[16,256,128]{2,1,0:T(8,128)(2,1)S(1)} all-to-all(bf16[16,256,128]{2,1,0:T(8,128)(2,1)S(1)} %first_x.1), channel_id=1, replica_groups=mesh['space'=8,'vel'=16] {'vel'}, dimensions={0} | all-to-all | bytes 2097152 | tf_op jit(solution)/shard_map/all_to_all | solution.py:476
  37.4 4.7 %first_collide.1 = (f32[16,256,128]{2,1,0:T(8,128)S(1)}, f32[256,128]{1,0:T(8,128)S(1)}, bf16[24,64,128]{2,1,0:T(8,128)(2,1)S(1)}, bf16[24,64,128]{2,1,0:T(8,128...) custom-call(s32[1]{0:T(128)} %bitcast.1.vel_ref, s32[1]{0:T(128)} %bitcast.space_ref, ...), custom_call_target="tpu_custom_call" | custom-call | flops 2500000000 | bytes 15458376 | tf_op jit(solution)/shard_map/first_collide/pallas_call | solution.py:80
  42.1 1.0 %collective-permute-start.2 = (bf16[24,64,128]{2,1,0:T(8,128)(2,1)S(1)}, bf16[24,64,128]{2,1,0:T(8,128)(2,1)S(1)}, u32[]{:S(2)}, u32[]{:S(2)}) collective-permute-start(bf16[24,64,128]{2,1,0:T(8,128)(2,1)S(1)} %get-tuple-element.19), channel_id=1, source_target_pairs={{0,1},{1,9},{2,3},{3,11},{4,5},{5,13},{6,7},{7,15},{8,24},{9,8},{1... | collective-permute-start | bytes 1179656 | tf_op jit(solution)/shard_map/ppermute | solution.py:488
  43.0 0.0 collective-permute-start.3
  43.0 0.3 collective-permute-start.4
  43.4 2.9 %collective-permute-start.5 = (bf16[24,64,128]{2,1,0:T(8,128)(2,1)S(1)}, bf16[24,64,128]{2,1,0:T(8,128)(2,1)S(1)}, u32[]{:S(2)}, u32[]{:S(2)}) collective-permute-start(bf16[24,64,128]{2,1,0:T(8,128)(2,1)S(1)} %get-tuple-element.22), channel_id=1, source_target_pairs={{2,0},{3,1},{4,2},{5,3},{6,4},{7,5},{0,6},{1,7},{10,8},{11,9},{12,... | collective-permute-start | bytes 1179656 | tf_op jit(solution)/shard_map/ppermute | solution.py:487
  46.2 2.5 %second_z.1 = (f32[16,256,128]{2,1,0:T(8,128)S(1)}, f32[256,128]{1,0:T(8,128)S(1)}) custom-call(s32[1]{0:T(128)} %bitcast.1.vel_ref, s32[1]{0:T(128)} %bitcast.space_ref, s32[2,8]{1,0:T(2,128)S(1)} %copy-done.10, f32[16,256,128]{2,1,0:T(8,128)S(1)} %get-tuple-element.17.f_ref, s32[2,4096]{1,0:T(2,128)S(1)} %copy-done.8), custom_call_target="tpu_custom_call" | custom-call | flops 6000000 | bytes 4358216 | tf_op jit(solution)/shard_map/second_z/pallas_call | solution.py:80
  48.8 5.9 %collective-permute-done.3.y_below_ref = bf16[24,64,128]{2,1,0:T(8,128)(2,1)S(1)} collective-permute-done((bf16[24,64,128]{2,1,0:T(8,128)(2,1)S(1)}, bf16[24,64,128]{2,1,0:T(8,128)(2,1)S(1)}, u32[]{:S(2)}, u32[]{:S(2)}) %collective-permute-start.3) | collective-permute-done | bytes 393248 | tf_op jit(solution)/shard_map/ppermute | solution.py:486
  54.7 2.4 %second_xy.1.moved_ref = f32[16,256,128]{2,1,0:T(8,128)S(1)} custom-call(f32[16,256,128]{2,1,0:T(8,128)S(1)} %get-tuple-element.17.f_ref, f32[16,256,128]{2,1,0:T(8,128)S(1)} %get-tuple-element.18.part_ref, bf16[24,64,128]{2,1,0:T(8,128)(2,1)S(1)} %collective-permute-done.2.x_below_ref, bf16[24,64,128]{2,1,0:T(8,128)(2,1)S(1)} %collective-permute-done.3.y_below_ref, ...), custom_call_target="tpu_custom_call" | custom-call | flops 12000000 | bytes 7864320 | tf_op jit(solution)/shard_map/second_xy/pallas_call | solution.py:80
  57.1 3.7 %second_collide.1 = bf16[16,256,128]{2,1,0:T(8,128)(2,1)S(1)} custom-call(f32[16,256,128]{2,1,0:T(8,128)S(1)} %second_xy.1.moved_ref, f32[256,128]{1,0:T(8,128)S(1)} %get-tuple-element.23.mask_ref, f32[256,128]{1,0:T(8,128)S(1)} %get-tuple-element.24.rates_ref, bf16[2048,768]{1,0:T(8,128)(2,1)S(1)} %copy-done.1, bf16[2048,768]{1,0:T(8,128)(2,1)S(1)} %copy-done.2, ...), custom_call_target="tpu_custom_call" | custom-call | flops 2500000000 | bytes 13967360 | tf_op jit(solution)/shard_map/second_collide/pallas_call | solution.py:80
  60.8 22.9 %all_to_all.11.in_ref = bf16[16,256,128]{2,1,0:T(8,128)(2,1)S(1)} all-to-all(bf16[16,256,128]{2,1,0:T(8,128)(2,1)S(1)} %second_collide.1), channel_id=1, replica_groups=mesh['space'=8,'vel'=16] {'vel'}, dimensions={0} | all-to-all | bytes 2097152 | tf_op jit(solution)/shard_map/all_to_all | solution.py:503
  83.8 1.4 %place.1 = f32[16,16,16,128]{3,2,1,0:T(8,128)} custom-call(s32[1]{0:T(128)} %bitcast.space_ref, bf16[16,256,128]{2,1,0:T(8,128)(2,1)S(1)} %all_to_all.11.in_ref), custom_call_target="tpu_custom_call" | custom-call | bytes 3145732 | tf_op jit(solution)/shard_map/place/pallas_call | solution.py:80
  (20 shorter events, 0.1 us)
Async XLA Ops:
  0.0 1.6 %copy-start = (f32[16,16,16,128]{3,2,1,0:T(8,128)S(1)}, f32[16,16,16,128]{3,2,1,0:T(8,128)}, u32[]{:S(2)}) copy-start(f32[16,16,16,128]{3,2,1,0:T(8,128)} %f_ref.3) | copy-start | bytes 6291460
  1.6 10.9 %collective-permute-start = (bf16[2,16,16,128]{3,2,1,0:T(8,128)(2,1)S(1)}, bf16[2,16,16,128]{3,2,1,0:T(8,128)(2,1)S(1)}, u32[]{:S(2)}, u32[]{:S(2)}) collective-permute-start(bf16[2,16,16,128]{3,2,1,0:T(8,128)(2,1)S(1)} %get-tuple-element.15), channel_id=1, source_target_pairs={{0,112},{1,113},{2,114},{3,115},{4,116},{5,117},{6,118},{7,119},{8... | collective-permute-start | bytes 393224 | tf_op jit(solution)/shard_map/ppermute | solution.py:462
  7.3 5.2 %collective-permute-start.1 = (bf16[1,16,16,128]{3,2,1,0:T(8,128)(2,1)S(1)}, bf16[1,16,16,128]{3,2,1,0:T(8,128)(2,1)S(1)}, u32[]{:S(2)}, u32[]{:S(2)}) collective-permute-start(bf16[1,16,16,128]{3,2,1,0:T(8,128)(2,1)S(1)} %get-tuple-element.16), channel_id=1, source_target_pairs={{0,16},{1,17},{2,18},{3,19},{4,20},{5,21},{6,22},{7,23},{8,120},{9... | collective-permute-start | bytes 196616 | tf_op jit(solution)/shard_map/ppermute | solution.py:463
  7.3 30.0 %copy-start.3 = (bf16[768,2048]{1,0:T(8,128)(2,1)S(1)}, bf16[768,2048]{1,0:T(8,128)(2,1)}, u32[]{:S(2)}) copy-start(bf16[768,2048]{1,0:T(8,128)(2,1)} %c_ref.3) | copy-start | bytes 9437188
  7.3 30.0 %copy-start.8 = (s32[2,4096]{1,0:T(2,128)S(1)}, s32[2,4096]{1,0:T(2,128)}, u32[]{:S(2)}) copy-start(s32[2,4096]{1,0:T(2,128)} %cells_ref.3) | copy-start | bytes 98308
  7.3 30.0 %copy-start.9 = (f32[1,2048]{1,0:T(1,128)S(1)}, f32[1,2048]{1,0:T(1,128)}, u32[]{:S(2)}) copy-start(f32[1,2048]{1,0:T(1,128)} %constant.20.clone.w_ref) | copy-start | bytes 24580
  12.5 24.8 %copy-start.1 = (bf16[2048,768]{1,0:T(8,128)(2,1)S(1)}, bf16[2048,768]{1,0:T(8,128)(2,1)}, u32[]{:S(2)}) copy-start(bf16[2048,768]{1,0:T(8,128)(2,1)} %a_ref.3) | copy-start | bytes 9437188
  12.5 24.8 %copy-start.2 = (bf16[2048,768]{1,0:T(8,128)(2,1)S(1)}, bf16[2048,768]{1,0:T(8,128)(2,1)}, u32[]{:S(2)}) copy-start(bf16[2048,768]{1,0:T(8,128)(2,1)} %b_ref.3) | copy-start | bytes 9437188
  13.8 23.6 %copy-start.4 = (bf16[128,2048]{1,0:T(8,128)(2,1)S(1)}, bf16[128,2048]{1,0:T(8,128)(2,1)}, u32[]{:S(2)}) copy-start(bf16[128,2048]{1,0:T(8,128)(2,1)} %constant.19.clone.expand_ref) | copy-start | bytes 1572868
  13.8 23.6 %copy-start.5 = (bf16[2048,128]{1,0:T(8,128)(2,1)S(1)}, bf16[2048,128]{1,0:T(8,128)(2,1)}, u32[]{:S(2)}) copy-start(bf16[2048,128]{1,0:T(8,128)(2,1)} %constant.17.clone.project_ref) | copy-start | bytes 1572868
  13.8 23.6 %copy-start.6 = (f32[128,128]{1,0:T(8,128)S(1)}, f32[128,128]{1,0:T(8,128)}, u32[]{:S(2)}) copy-start(f32[128,128]{1,0:T(8,128)} %constant.18.clone.mix_ref) | copy-start | bytes 196612
  13.8 23.6 %copy-start.7 = (f32[16,16,16]{2,1,0:T(8,128)S(1)}, f32[16,16,16]{2,1,0:T(8,128)}, u32[]{:S(2)}) copy-start(f32[16,16,16]{2,1,0:T(8,128)} %rate_ref.1) | copy-start | bytes 49156
  13.8 23.6 %copy-start.10 = (s32[2,8]{1,0:T(2,128)S(1)}, s32[2,8]{1,0:T(2,128)}, u32[]{:S(2)}) copy-start(s32[2,8]{1,0:T(2,128)} %count_ref.3) | copy-start | bytes 196
  42.1 6.7 %collective-permute-start.2 = (bf16[24,64,128]{2,1,0:T(8,128)(2,1)S(1)}, bf16[24,64,128]{2,1,0:T(8,128)(2,1)S(1)}, u32[]{:S(2)}, u32[]{:S(2)}) collective-permute-start(bf16[24,64,128]{2,1,0:T(8,128)(2,1)S(1)} %get-tuple-element.19), channel_id=1, source_target_pairs={{0,1},{1,9},{2,3},{3,11},{4,5},{5,13},{6,7},{7,15},{8,24},{9,8},{1... | collective-permute-start | bytes 1179656 | tf_op jit(solution)/shard_map/ppermute | solution.py:488
  43.0 11.7 %collective-permute-start.3 = (bf16[24,64,128]{2,1,0:T(8,128)(2,1)S(1)}, bf16[24,64,128]{2,1,0:T(8,128)(2,1)S(1)}, u32[]{:S(2)}, u32[]{:S(2)}) collective-permute-start(bf16[24,64,128]{2,1,0:T(8,128)(2,1)S(1)} %get-tuple-element.20), channel_id=1, source_target_pairs={{0,2},{1,3},{2,4},{3,5},{4,6},{5,7},{6,0},{7,1},{8,10},{9,11},{10,... | collective-permute-start | bytes 1179656 | tf_op jit(solution)/shard_map/ppermute | solution.py:486
  43.0 11.7 %collective-permute-start.4 = (bf16[24,64,128]{2,1,0:T(8,128)(2,1)S(1)}, bf16[24,64,128]{2,1,0:T(8,128)(2,1)S(1)}, u32[]{:S(2)}, u32[]{:S(2)}) collective-permute-start(bf16[24,64,128]{2,1,0:T(8,128)(2,1)S(1)} %get-tuple-element.21), channel_id=1, source_target_pairs={{1,0},{9,1},{3,2},{11,3},{5,4},{13,5},{7,6},{15,7},{24,8},{8,9},{2... | collective-permute-start | bytes 1179656 | tf_op jit(solution)/shard_map/ppermute | solution.py:489
  43.4 11.3 %collective-permute-start.5 = (bf16[24,64,128]{2,1,0:T(8,128)(2,1)S(1)}, bf16[24,64,128]{2,1,0:T(8,128)(2,1)S(1)}, u32[]{:S(2)}, u32[]{:S(2)}) collective-permute-start(bf16[24,64,128]{2,1,0:T(8,128)(2,1)S(1)} %get-tuple-element.22), channel_id=1, source_target_pairs={{2,0},{3,1},{4,2},{5,3},{6,4},{7,5},{0,6},{1,7},{10,8},{11,9},{12,... | collective-permute-start | bytes 1179656 | tf_op jit(solution)/shard_map/ppermute | solution.py:487

commit v8 on v7

--- a/solution.py
+++ b/solution.py
@@ -257,13 +257,20 @@
 def first_collide_kernel(
     vel_ref, space_ref, count_ref, rows_ref, cells_ref, rate_ref, a_ref, b_ref, c_ref,
     project_ref, mix_ref, expand_ref, w_ref,
-    f_ref, rates_ref, x_up_ref, x_down_ref, y_up_ref, y_down_ref, hidden_ref,
+    f_ref, rates_ref, x_even_ref, x_odd_ref, y_even_ref, y_odd_ref, hidden_ref,
 ):
     rows = jnp.concatenate([rows_ref[g] for g in range(GROUPS)], axis=1)
     kinetic = kinetic_cells_of(0, vel_ref, space_ref, count_ref, cells_ref) > 0.0
     rate = rates_of(vel_ref, space_ref, rate_ref)
     rates_ref[...] = rate
     half = GROUPS // 2
+    x_quarter, y_quarter = quarters(vel_ref[0], space_ref[0])
+    x_is_even, y_is_even = x_quarter % 2 == 0, y_quarter % 2 == 0
+
+    def put(even_ref, odd_ref, is_even, where, up, down):
+        even_ref[where] = jnp.where(is_even, up, down).astype(jnp.bfloat16)
+        odd_ref[where] = jnp.where(is_even, down, up).astype(jnp.bfloat16)
+
     low_lane = lax.broadcasted_iota(jnp.int32, (NZ, WIDTH), 1) < WIDTH // 2
     for g, collision, equilibrium in collide(
         rows, a_ref, b_ref, c_ref, project_ref, mix_ref, expand_ref, w_ref, hidden_ref
@@ -272,27 +279,29 @@
         change = jnp.where(kinetic, COLLIDE * collision, rate * (equilibrium - moved))
         result = moved + change
         f_ref[g] = result
-        sent = result.astype(jnp.bfloat16)
-        x_up_ref[g] = sent[3 * LINE : 4 * LINE]
-        x_down_ref[g] = sent[0:LINE]
-        if g >= half:
-            x_up_ref[g + half] = sent[2 * LINE : 3 * LINE]
-        else:
-            x_down_ref[g + GROUPS] = sent[LINE : 2 * LINE]
+        put(x_even_ref, x_odd_ref, x_is_even, g, result[3 * LINE :], result[:LINE])
+        low = g - half
+        if low >= 0:
+            put(
+                x_even_ref, x_odd_ref, x_is_even, GROUPS + low,
+                result[2 * LINE : 3 * LINE], f_ref[low, LINE : 2 * LINE],
+            )
         for x in range(BX):
             here = slice(NZ * x, NZ * (x + 1))
-            y_down_ref[g, here] = sent[LINE * x : LINE * x + NZ]
-            y_up_ref[g, here] = sent[LINE * x + 3 * NZ : LINE * x + 4 * NZ]
-            if g >= half:
-                low = g - half
-                second = slice(LINE * x + NZ, LINE * x + 2 * NZ)
-                third = slice(LINE * x + 2 * NZ, LINE * x + 3 * NZ)
-                y_up_ref[GROUPS + low, here] = jnp.where(
-                    low_lane, pltpu.roll(f_ref[low, third], WIDTH // 2, 1), result[third]
-                ).astype(jnp.bfloat16)
-                y_down_ref[GROUPS + low, here] = jnp.where(
-                    low_lane, f_ref[low, second], pltpu.roll(result[second], WIDTH // 2, 1)
-                ).astype(jnp.bfloat16)
+            first, second, third, fourth = (
+                slice(LINE * x + NZ * y, LINE * x + NZ * (y + 1)) for y in range(BY)
+            )
+            put(y_even_ref, y_odd_ref, y_is_even, (g, here), result[fourth], result[first])
+            if low >= 0:
+                put(
+                    y_even_ref, y_odd_ref, y_is_even, (GROUPS + low, here),
+                    jnp.where(
+                        low_lane, pltpu.roll(f_ref[low, third], WIDTH // 2, 1), result[third]
+                    ),
+                    jnp.where(
+                        low_lane, f_ref[low, second], pltpu.roll(result[second], WIDTH // 2, 1)
+                    ),
+                )
 
 
 def second_z_kernel(vel_ref, space_ref, count_ref, f_ref, cells_ref, part_ref, mask_ref):
@@ -311,14 +320,19 @@
 
 
 def second_xy_kernel(
-    f_ref, part_ref, x_below_ref, y_below_ref, x_above_ref, y_above_ref, moved_ref
+    vel_ref, space_ref, f_ref, part_ref, x_odd_ref, y_even_ref, y_odd_ref, x_even_ref, moved_ref
 ):
     uy, _ = speeds_yz()
     y_up = uy > 0.0
     half = GROUPS // 2
 
-    def wide(ref, g, i):
-        return ref[g, NZ * i : NZ * (i + 1)].astype(jnp.float32)
+    x_quarter, y_quarter = quarters(vel_ref[0], space_ref[0])
+    x_is_even, y_is_even = x_quarter % 2 == 0, y_quarter % 2 == 0
+
+    def arrived(even_ref, odd_ref, is_even, g, i):
+        even = even_ref[g, NZ * i : NZ * (i + 1)].astype(jnp.float32)
+        odd = odd_ref[g, NZ * i : NZ * (i + 1)].astype(jnp.float32)
+        return jnp.where(is_even, odd, even), jnp.where(is_even, even, odd)
 
     def group(pair, upward):
         g = pair + half if upward else pair
@@ -326,17 +340,16 @@
         ux = (g.astype(jnp.float32) - 0.5 * (GX - 1)) * (SPACING * COURANT)
         ux = ux if upward else -ux
         for y in range(BY):
-            behind, ahead = (x_below_ref, x_above_ref) if upward else (x_above_ref, x_below_ref)
+            here_x = (x_even_ref, x_odd_ref, x_is_even)
+            behind, ahead = arrived(*here_x, g, y)[:: 1 if upward else -1]
+            line = [arrived(*here_x, extra, y)[0 if upward else 1], behind]
+            for k in range(BX):
+                x = k if upward else BX - 1 - k
+                line.append(f_ref[g, LINE * x + NZ * y : LINE * x + NZ * (y + 1)])
+            line.append(ahead)
 
             def at_x(k):
-                if k == -2:
-                    return wide(behind, extra, y)
-                if k == -1:
-                    return wide(behind, g, y)
-                if k == BX:
-                    return wide(ahead, g, y)
-                x = k if upward else BX - 1 - k
-                return f_ref[g, LINE * x + NZ * y : LINE * x + NZ * (y + 1)]
+                return line[k + 2]
 
             face_before = upwind_face(at_x(-2), at_x(-1), at_x(0))
             for k in range(BX):
@@ -346,19 +359,20 @@
                 moved_ref[g, here] = part_ref[g, here] - ux * (face - face_before)
                 face_before = face
         for x in range(BX):
+            here_y = (y_even_ref, y_odd_ref, y_is_even)
+            below, above = arrived(*here_y, g, x)
+            below_2, above_2 = arrived(*here_y, extra, x)
+            if upward:
+                above_2 = pltpu.roll(above_2, WIDTH // 2, 1)
+            else:
+                below_2 = pltpu.roll(below_2, WIDTH // 2, 1)
+            column = [below_2, below]
+            for y in range(BY):
+                column.append(f_ref[g, LINE * x + NZ * y : LINE * x + NZ * (y + 1)])
+            column += [above, above_2]
 
             def at_y(y):
-                if y == -2:
-                    below = wide(y_below_ref, extra, x)
-                    return below if upward else pltpu.roll(below, WIDTH // 2, 1)
-                if y == -1:
-                    return wide(y_below_ref, g, x)
-                if y == BY:
-                    return wide(y_above_ref, g, x)
-                if y == BY + 1:
-                    above = wide(y_above_ref, extra, x)
-                    return pltpu.roll(above, WIDTH // 2, 1) if upward else above
-                return f_ref[g, LINE * x + NZ * y : LINE * x + NZ * (y + 1)]
+                return column[y + 2]
 
             up, _ = edges(at_y(-2), at_y(-1), at_y(0))
             next_up, next_down = edges(at_y(-1), at_y(0), at_y(1))
@@ -428,30 +442,37 @@
 
 
 def steps_of(slabs):
-    upwind, downwind, x_up, y_up = [], [], [], []
+    upwind, downwind = [], []
+    x_even, x_odd, y_even, y_odd = [], [], [], []
     for space in range(slabs):
-        for high in range(2):
+        before, after = (space - 1) % slabs, (space + 1) % slabs
+        for quarter in range(4):
+            next_x = holder_place(space, quarter + 1, slabs)
+            last_x = holder_place(space, quarter - 1, slabs)
             for x in range(4):
-                for core in range(2):
-                    me = device_of(space, high, x, core)
-                    after = device_of((space + 1) % slabs, high, x, core)
-                    before = device_of((space - 1) % slabs, high, x, core)
-                    upwind.append((me, after if high else before))
-                    downwind.append((me, before if high else after))
-                    turned = (high + space) % 2
-                    quarter = 2 * turned + (core + turned) % 2
-                    next_slab = (space + (quarter == 3)) % slabs
-                    x_up.append((me, holder_of(next_slab, (quarter + 1) % 4, x)))
-                    y_up.append((me, device_of(space, high, (x + 1) % 4, core)))
-    back = lambda pairs: [(target, source) for source, target in pairs]
-    return upwind, downwind, x_up, back(x_up), y_up, back(y_up)
+                me = holder_of(space, quarter, x)
+                rank = me % GROUPS
+                forward = rank >= GROUPS // 2
+                upwind.append((me, (after if forward else before) * GROUPS + rank))
+                downwind.append((me, (before if forward else after) * GROUPS + rank))
+                up, down = holder_of(*next_x, x), holder_of(*last_x, x)
+                x_even.append((me, down if quarter % 2 else up))
+                x_odd.append((me, up if quarter % 2 else down))
+                up, down = (holder_of(space, quarter, (x + d) % 4) for d in (1, -1))
+                y_even.append((me, down if x % 2 else up))
+                y_odd.append((me, up if x % 2 else down))
+    return upwind, downwind, x_even, x_odd, y_even, y_odd
+
+
+def holder_place(space, quarter, slabs):
+    return (space + quarter // 4) % slabs, quarter % 4
 
 
 def body(dist, relax_rate, kinetic_cells, kinetic_count, map_a, map_b, map_c):
     vel = (lax.axis_index("vel").astype(jnp.int32).reshape(1), SMEM)
     space = (lax.axis_index("space").astype(jnp.int32).reshape(1), SMEM)
     both = ("space", "vel")
-    upwind, downwind, x_up, x_down, y_up, y_down = steps_of(lax.axis_size("space"))
+    upwind, downwind, *pairs = steps_of(lax.axis_size("space"))
     project, mix, expand, w = tables()
     consts = (jnp.asarray(project), jnp.asarray(mix), jnp.asarray(expand), jnp.asarray(w))
     layers = (NY, NZ, WIDTH)
@@ -477,23 +498,22 @@
     facts = (vel, space, (kinetic_count, SMEM))
     lanes = ((LAYER, WIDTH), jnp.float32, VMEM)
     held = tuple((o, VMEM) for o in (map_a, map_b, map_c) + consts)
-    f, rates, up_x, down_x, up_y, down_y = call(
+    f, rates, *halos = call(
         first_collide_kernel, "first_collide",
         facts + ((gathered, VMEM), (kinetic_cells, VMEM), (relax_rate, VMEM)) + held,
         ((wide, jnp.float32, VMEM), lanes) + ((halo, half, VMEM),) * 4,
         scratch=(hidden,), flops=2_500_000_000, limit=C_VMEM,
     )
-    y_below = lax.ppermute(up_y, both, y_up)
-    y_above = lax.ppermute(down_y, both, y_down)
-    x_below = lax.ppermute(up_x, both, x_up)
-    x_above = lax.ppermute(down_x, both, x_down)
+    x_even, x_odd, y_even, y_odd = (
+        lax.ppermute(o, both, p) for o, p in zip(halos, pairs, strict=True)
+    )
     part, mask = call(
         second_z_kernel, "second_z", facts + ((f, VMEM), (kinetic_cells, VMEM)),
         ((wide, jnp.float32, VMEM), lanes), flops=6_000_000,
     )
     (moved,) = call(
         second_xy_kernel, "second_xy",
-        tuple((o, VMEM) for o in (f, part, x_below, y_below, x_above, y_above)),
+        (vel, space) + tuple((o, VMEM) for o in (f, part, x_odd, y_even, y_odd, x_even)),
         ((wide, jnp.float32, VMEM),), flops=12_000_000,
     )
     (result,) = call(

time: 85.3 us -> 83.6 us (0.980)
  waiting for transfers between devices: 8.65 us -> 7.65 us
    ppermute x4, waiting for transfers between devices: 5.94 us -> 4.95 us  [body(): lax.ppermute(o, both, p)]
  transfers between devices with their start and end apart: 6 -> 6, of which waited for: 2 -> 4; matrix products, arithmetic and copies ran while one was open for 0% -> 0% of each run, Pallas kernels for 6% -> 6%
where the time goes in v8:
time: 83.6 us; the launch traced here: 83.4 us
  blocking collectives  46.2 us (55%)
  Pallas kernels  18.8 us (22%)
  starting transfers between devices  9.02 us (11%)
  waiting for transfers between devices  7.65 us (9%)
  local copies, waits for them, and re-layouts  1.64 us (2%)
    all_to_all x1, blocking collectives, body(): lax.all_to_all(rows, 'vel', split_axis=0, concat_axis=0, tiled=True)  23.5 us
    all_to_all x1, blocking collectives, body(): lax.all_to_all(result, 'vel', split_axis=0, concat_axis=0, tiled=True)  22.7 us
    pallas_call x8, Pallas kernels, call(): pl.pallas_call(kernel, out_shape=tuple(shapes), in_specs=[pl.BlockSpec(me...  18.8 us
    ppermute x1, starting transfers between devices, body(): behind = lax.ppermute(behind, both, upwind)  5.67 us
    ppermute x4, waiting for transfers between devices, body(): lax.ppermute(o, both, p)  4.95 us
    ppermute x4, starting transfers between devices, body(): lax.ppermute(o, both, p)  3.35 us
    ppermute x1, waiting for transfers between devices, body(): ahead = lax.ppermute(ahead, both, downwind)  2.7 us
  transfers between devices with their start and end apart: 6, of which 4 were waited for; matrix products, arithmetic and copies ran while one was open for 0% of the time, Pallas kernels for 6%

profile of v8, /device:TPU:1, one launch (start us, length us, event | category | flops | bytes accessed | tf_op | source)
XLA Modules:
  0.0 83.4 jit_solution(9710387402883273811)
XLA Ops:
  0.0 1.6 %copy-done = f32[16,16,16,128]{3,2,1,0:T(8,128)S(1)} copy-done((f32[16,16,16,128]{3,2,1,0:T(8,128)S(1)}, f32[16,16,16,128]{3,2,1,0:T(8,128)}, u32[]{:S(2)}) %copy-start) | copy-done | bytes 2097176
  1.6 5.7 %collective-permute-start = (bf16[2,16,16,128]{3,2,1,0:T(8,128)(2,1)S(1)}, bf16[2,16,16,128]{3,2,1,0:T(8,128)(2,1)S(1)}, u32[]{:S(2)}, u32[]{:S(2)}) collective-permute-start(bf16[2,16,16,128]{3,2,1,0:T(8,128)(2,1)S(1)} %get-tuple-element.15), channel_id=1, source_target_pairs={{0,112},{2,114},{4,116},{6,118},{1,113},{3,115},{5,117},{7,119},{9... | collective-permute-start | bytes 393224 | tf_op jit(solution)/shard_map/ppermute | solution.py:483
  7.3 2.5 %first_yz.1.part_ref = f32[16,16,16,128]{3,2,1,0:T(8,128)S(1)} custom-call(f32[16,16,16,128]{3,2,1,0:T(8,128)S(1)} %copy-done), custom_call_target="tpu_custom_call" | custom-call | flops 12000000 | bytes 4194304 | tf_op jit(solution)/shard_map/first_yz/pallas_call | solution.py:80
  9.8 2.7 %collective-permute-done.1.ahead_ref = bf16[1,16,16,128]{3,2,1,0:T(8,128)(2,1)S(1)} collective-permute-done((bf16[1,16,16,128]{3,2,1,0:T(8,128)(2,1)S(1)}, bf16[1,16,16,128]{3,2,1,0:T(8,128)(2,1)S(1)}, u32[]{:S(2)}, u32[]{:S(2)}) %collective-permute-start.1) | collective-permute-done | bytes 65568 | tf_op jit(solution)/shard_map/ppermute | solution.py:484
  12.5 1.3 %first_x.1 = bf16[16,256,128]{2,1,0:T(8,128)(2,1)S(1)} custom-call(s32[1]{0:T(128)} %bitcast.1.vel_ref, s32[1]{0:T(128)} %bitcast.space_ref, f32[16,16,16,128]{3,2,1,0:T(8,128)S(1)} %copy-done, f32[16,16,16,128]{3,2,1,0:T(8,128)S(1)} %first_yz.1.part_ref, bf16[2,16,16,128]{3,2,1,0:T(8,128)(2,1)S(1)} %collective-permute-done.behind_ref, ...), custom_call_target="tpu_custom_call" | custom-call | flops 6000000 | bytes 5439496 | tf_op jit(solution)/shard_map/first_x/pallas_call | solution.py:80
  13.8 0.0 copy-start.4
  13.8 0.0 copy-start.5
  13.8 0.0 copy-start.6
  13.8 0.0 copy-start.7
  13.8 0.0 copy-start.10
  13.8 23.5 %all_to_all.10.rows_ref = bf16[16,256,128]{2,1,0:T(8,128)(2,1)S(1)} all-to-all(bf16[16,256,128]{2,1,0:T(8,128)(2,1)S(1)} %first_x.1), channel_id=1, replica_groups=mesh['space'=8,'vel'=16] {'vel'}, dimensions={0} | all-to-all | bytes 2097152 | tf_op jit(solution)/shard_map/all_to_all | solution.py:497
  37.4 4.8 %first_collide.1 = (f32[16,256,128]{2,1,0:T(8,128)S(1)}, f32[256,128]{1,0:T(8,128)S(1)}, bf16[24,64,128]{2,1,0:T(8,128)(2,1)S(1)}, bf16[24,64,128]{2,1,0:T(8,128...) custom-call(s32[1]{0:T(128)} %bitcast.1.vel_ref, s32[1]{0:T(128)} %bitcast.space_ref, ...), custom_call_target="tpu_custom_call" | custom-call | flops 2500000000 | bytes 15458376 | tf_op jit(solution)/shard_map/first_collide/pallas_call | solution.py:80
  42.2 1.0 %collective-permute-start.2 = (bf16[24,64,128]{2,1,0:T(8,128)(2,1)S(1)}, bf16[24,64,128]{2,1,0:T(8,128)(2,1)S(1)}, u32[]{:S(2)}, u32[]{:S(2)}) collective-permute-start(bf16[24,64,128]{2,1,0:T(8,128)(2,1)S(1)} %get-tuple-element.19), channel_id=1, source_target_pairs={{0,112},{2,114},{4,116},{6,118},{1,9},{3,11},{5,13},{7,15},{9,1},{... | collective-permute-start | bytes 1179656 | tf_op jit(solution)/shard_map/ppermute | solution.py:508
  43.2 0.0 collective-permute-start.3
  43.2 1.2 %collective-permute-start.4 = (bf16[24,64,128]{2,1,0:T(8,128)(2,1)S(1)}, bf16[24,64,128]{2,1,0:T(8,128)(2,1)S(1)}, u32[]{:S(2)}, u32[]{:S(2)}) collective-permute-start(bf16[24,64,128]{2,1,0:T(8,128)(2,1)S(1)} %get-tuple-element.21), channel_id=1, source_target_pairs={{0,6},{2,4},{4,2},{6,0},{1,7},{3,5},{5,3},{7,1},{9,15},{11,13},{13... | collective-permute-start | bytes 1179656 | tf_op jit(solution)/shard_map/ppermute | solution.py:508
  44.4 1.1 %collective-permute-start.5 = (bf16[24,64,128]{2,1,0:T(8,128)(2,1)S(1)}, bf16[24,64,128]{2,1,0:T(8,128)(2,1)S(1)}, u32[]{:S(2)}, u32[]{:S(2)}) collective-permute-start(bf16[24,64,128]{2,1,0:T(8,128)(2,1)S(1)} %get-tuple-element.22), channel_id=1, source_target_pairs={{0,1},{2,3},{4,5},{6,7},{1,0},{3,2},{5,4},{7,6},{9,8},{11,10},{13,... | collective-permute-start | bytes 1179656 | tf_op jit(solution)/shard_map/ppermute | solution.py:508
  45.5 2.5 %second_z.1 = (f32[16,256,128]{2,1,0:T(8,128)S(1)}, f32[256,128]{1,0:T(8,128)S(1)}) custom-call(s32[1]{0:T(128)} %bitcast.1.vel_ref, s32[1]{0:T(128)} %bitcast.space_ref, s32[2,8]{1,0:T(2,128)S(1)} %copy-done.10, f32[16,256,128]{2,1,0:T(8,128)S(1)} %get-tuple-element.17.f_ref, s32[2,4096]{1,0:T(2,128)S(1)} %copy-done.8), custom_call_target="tpu_custom_call" | custom-call | flops 6000000 | bytes 4358216 | tf_op jit(solution)/shard_map/second_z/pallas_call | solution.py:80
  48.1 2.6 %collective-permute-done.2.x_odd_ref = bf16[24,64,128]{2,1,0:T(8,128)(2,1)S(1)} collective-permute-done((bf16[24,64,128]{2,1,0:T(8,128)(2,1)S(1)}, bf16[24,64,128]{2,1,0:T(8,128)(2,1)S(1)}, u32[]{:S(2)}, u32[]{:S(2)}) %collective-permute-start.2) | collective-permute-done | bytes 393248 | tf_op jit(solution)/shard_map/ppermute | solution.py:508
  50.7 1.1 %collective-permute-done.3.y_even_ref = bf16[24,64,128]{2,1,0:T(8,128)(2,1)S(1)} collective-permute-done((bf16[24,64,128]{2,1,0:T(8,128)(2,1)S(1)}, bf16[24,64,128]{2,1,0:T(8,128)(2,1)S(1)}, u32[]{:S(2)}, u32[]{:S(2)}) %collective-permute-start.3) | collective-permute-done | bytes 393248 | tf_op jit(solution)/shard_map/ppermute | solution.py:508
  51.8 1.2 %collective-permute-done.4.y_odd_ref = bf16[24,64,128]{2,1,0:T(8,128)(2,1)S(1)} collective-permute-done((bf16[24,64,128]{2,1,0:T(8,128)(2,1)S(1)}, bf16[24,64,128]{2,1,0:T(8,128)(2,1)S(1)}, u32[]{:S(2)}, u32[]{:S(2)}) %collective-permute-start.4) | collective-permute-done | bytes 393248 | tf_op jit(solution)/shard_map/ppermute | solution.py:508
  53.0 2.6 %second_xy.1.moved_ref = f32[16,256,128]{2,1,0:T(8,128)S(1)} custom-call(s32[1]{0:T(128)} %bitcast.1.vel_ref, s32[1]{0:T(128)} %bitcast.space_ref, f32[16,256,128]{2,1,0:T(8,128)S(1)} %get-tuple-element.17.f_ref, f32[16,256,128]{2,1,0:T(8,128)S(1)} %get-tuple-element.18.part_ref, bf16[24,64,128]{2,1,0:T(8,128)(2,1)S(1)} %collective-permute-done.2.x_odd_ref, ...), custom_call_target="tpu_custom_call" | custom-call | flops 12000000 | bytes 7864328 | tf_op jit(solution)/shard_map/second_xy/pallas_call | solution.py:80
  55.6 3.7 %second_collide.1 = bf16[16,256,128]{2,1,0:T(8,128)(2,1)S(1)} custom-call(f32[16,256,128]{2,1,0:T(8,128)S(1)} %second_xy.1.moved_ref, f32[256,128]{1,0:T(8,128)S(1)} %get-tuple-element.23.mask_ref, f32[256,128]{1,0:T(8,128)S(1)} %get-tuple-element.24.rates_ref, bf16[2048,768]{1,0:T(8,128)(2,1)S(1)} %copy-done.1, bf16[2048,768]{1,0:T(8,128)(2,1)S(1)} %copy-done.2, ...), custom_call_target="tpu_custom_call" | custom-call | flops 2500000000 | bytes 13967360 | tf_op jit(solution)/shard_map/second_collide/pallas_call | solution.py:80
  59.3 22.7 %all_to_all.11.in_ref = bf16[16,256,128]{2,1,0:T(8,128)(2,1)S(1)} all-to-all(bf16[16,256,128]{2,1,0:T(8,128)(2,1)S(1)} %second_collide.1), channel_id=1, replica_groups=mesh['space'=8,'vel'=16] {'vel'}, dimensions={0} | all-to-all | bytes 2097152 | tf_op jit(solution)/shard_map/all_to_all | solution.py:523
  82.0 1.4 %place.1 = f32[16,16,16,128]{3,2,1,0:T(8,128)} custom-call(s32[1]{0:T(128)} %bitcast.space_ref, bf16[16,256,128]{2,1,0:T(8,128)(2,1)S(1)} %all_to_all.11.in_ref), custom_call_target="tpu_custom_call" | custom-call | bytes 3145732 | tf_op jit(solution)/shard_map/place/pallas_call | solution.py:80
  (20 shorter events, 0.1 us)
Async XLA Ops:
  0.0 1.6 %copy-start = (f32[16,16,16,128]{3,2,1,0:T(8,128)S(1)}, f32[16,16,16,128]{3,2,1,0:T(8,128)}, u32[]{:S(2)}) copy-start(f32[16,16,16,128]{3,2,1,0:T(8,128)} %f_ref.3) | copy-start | bytes 6291460
  1.6 10.9 %collective-permute-start = (bf16[2,16,16,128]{3,2,1,0:T(8,128)(2,1)S(1)}, bf16[2,16,16,128]{3,2,1,0:T(8,128)(2,1)S(1)}, u32[]{:S(2)}, u32[]{:S(2)}) collective-permute-start(bf16[2,16,16,128]{3,2,1,0:T(8,128)(2,1)S(1)} %get-tuple-element.15), channel_id=1, source_target_pairs={{0,112},{2,114},{4,116},{6,118},{1,113},{3,115},{5,117},{7,119},{9... | collective-permute-start | bytes 393224 | tf_op jit(solution)/shard_map/ppermute | solution.py:483
  7.3 5.2 %collective-permute-start.1 = (bf16[1,16,16,128]{3,2,1,0:T(8,128)(2,1)S(1)}, bf16[1,16,16,128]{3,2,1,0:T(8,128)(2,1)S(1)}, u32[]{:S(2)}, u32[]{:S(2)}) collective-permute-start(bf16[1,16,16,128]{3,2,1,0:T(8,128)(2,1)S(1)} %get-tuple-element.16), channel_id=1, source_target_pairs={{0,16},{2,18},{4,20},{6,22},{1,17},{3,19},{5,21},{7,23},{9,121},{1... | collective-permute-start | bytes 196616 | tf_op jit(solution)/shard_map/ppermute | solution.py:484
  7.3 30.0 %copy-start.3 = (bf16[768,2048]{1,0:T(8,128)(2,1)S(1)}, bf16[768,2048]{1,0:T(8,128)(2,1)}, u32[]{:S(2)}) copy-start(bf16[768,2048]{1,0:T(8,128)(2,1)} %c_ref.3) | copy-start | bytes 9437188
  7.3 30.0 %copy-start.8 = (s32[2,4096]{1,0:T(2,128)S(1)}, s32[2,4096]{1,0:T(2,128)}, u32[]{:S(2)}) copy-start(s32[2,4096]{1,0:T(2,128)} %cells_ref.3) | copy-start | bytes 98308
  7.3 30.0 %copy-start.9 = (f32[1,2048]{1,0:T(1,128)S(1)}, f32[1,2048]{1,0:T(1,128)}, u32[]{:S(2)}) copy-start(f32[1,2048]{1,0:T(1,128)} %constant.20.clone.w_ref) | copy-start | bytes 24580
  12.5 24.8 %copy-start.1 = (bf16[2048,768]{1,0:T(8,128)(2,1)S(1)}, bf16[2048,768]{1,0:T(8,128)(2,1)}, u32[]{:S(2)}) copy-start(bf16[2048,768]{1,0:T(8,128)(2,1)} %a_ref.3) | copy-start | bytes 9437188
  12.5 24.8 %copy-start.2 = (bf16[2048,768]{1,0:T(8,128)(2,1)S(1)}, bf16[2048,768]{1,0:T(8,128)(2,1)}, u32[]{:S(2)}) copy-start(bf16[2048,768]{1,0:T(8,128)(2,1)} %b_ref.3) | copy-start | bytes 9437188
  13.8 23.6 %copy-start.4 = (bf16[128,2048]{1,0:T(8,128)(2,1)S(1)}, bf16[128,2048]{1,0:T(8,128)(2,1)}, u32[]{:S(2)}) copy-start(bf16[128,2048]{1,0:T(8,128)(2,1)} %constant.19.clone.expand_ref) | copy-start | bytes 1572868
  13.8 23.6 %copy-start.5 = (bf16[2048,128]{1,0:T(8,128)(2,1)S(1)}, bf16[2048,128]{1,0:T(8,128)(2,1)}, u32[]{:S(2)}) copy-start(bf16[2048,128]{1,0:T(8,128)(2,1)} %constant.17.clone.project_ref) | copy-start | bytes 1572868
  13.8 23.6 %copy-start.6 = (f32[128,128]{1,0:T(8,128)S(1)}, f32[128,128]{1,0:T(8,128)}, u32[]{:S(2)}) copy-start(f32[128,128]{1,0:T(8,128)} %constant.18.clone.mix_ref) | copy-start | bytes 196612
  13.8 23.6 %copy-start.7 = (f32[16,16,16]{2,1,0:T(8,128)S(1)}, f32[16,16,16]{2,1,0:T(8,128)}, u32[]{:S(2)}) copy-start(f32[16,16,16]{2,1,0:T(8,128)} %rate_ref.1) | copy-start | bytes 49156
  13.8 23.6 %copy-start.10 = (s32[2,8]{1,0:T(2,128)S(1)}, s32[2,8]{1,0:T(2,128)}, u32[]{:S(2)}) copy-start(s32[2,8]{1,0:T(2,128)} %count_ref.3) | copy-start | bytes 196
  42.2 8.5 %collective-permute-start.2 = (bf16[24,64,128]{2,1,0:T(8,128)(2,1)S(1)}, bf16[24,64,128]{2,1,0:T(8,128)(2,1)S(1)}, u32[]{:S(2)}, u32[]{:S(2)}) collective-permute-start(bf16[24,64,128]{2,1,0:T(8,128)(2,1)S(1)} %get-tuple-element.19), channel_id=1, source_target_pairs={{0,112},{2,114},{4,116},{6,118},{1,9},{3,11},{5,13},{7,15},{9,1},{... | collective-permute-start | bytes 1179656 | tf_op jit(solution)/shard_map/ppermute | solution.py:508
  43.2 8.6 %collective-permute-start.3 = (bf16[24,64,128]{2,1,0:T(8,128)(2,1)S(1)}, bf16[24,64,128]{2,1,0:T(8,128)(2,1)S(1)}, u32[]{:S(2)}, u32[]{:S(2)}) collective-permute-start(bf16[24,64,128]{2,1,0:T(8,128)(2,1)S(1)} %get-tuple-element.20), channel_id=1, source_target_pairs={{0,2},{2,0},{4,6},{6,4},{1,3},{3,1},{5,7},{7,5},{9,11},{11,9},{13,... | collective-permute-start | bytes 1179656 | tf_op jit(solution)/shard_map/ppermute | solution.py:508
  43.2 9.8 %collective-permute-start.4 = (bf16[24,64,128]{2,1,0:T(8,128)(2,1)S(1)}, bf16[24,64,128]{2,1,0:T(8,128)(2,1)S(1)}, u32[]{:S(2)}, u32[]{:S(2)}) collective-permute-start(bf16[24,64,128]{2,1,0:T(8,128)(2,1)S(1)} %get-tuple-element.21), channel_id=1, source_target_pairs={{0,6},{2,4},{4,2},{6,0},{1,7},{3,5},{5,3},{7,1},{9,15},{11,13},{13... | collective-permute-start | bytes 1179656 | tf_op jit(solution)/shard_map/ppermute | solution.py:508
  44.4 8.6 %collective-permute-start.5 = (bf16[24,64,128]{2,1,0:T(8,128)(2,1)S(1)}, bf16[24,64,128]{2,1,0:T(8,128)(2,1)S(1)}, u32[]{:S(2)}, u32[]{:S(2)}) collective-permute-start(bf16[24,64,128]{2,1,0:T(8,128)(2,1)S(1)} %get-tuple-element.22), channel_id=1, source_target_pairs={{0,1},{2,3},{4,5},{6,7},{1,0},{3,2},{5,4},{7,6},{9,8},{11,10},{13,... | collective-permute-start | bytes 1179656 | tf_op jit(solution)/shard_map/ppermute | solution.py:508

commit v9 on v8

--- a/solution.py
+++ b/solution.py
@@ -228,6 +228,15 @@
 
 def collide(rows, a_ref, b_ref, c_ref, project_ref, mix_ref, expand_ref, w_ref, hidden_ref):
     moments = jnp.dot(rows, project_ref[...], preferred_element_type=jnp.float32)
+    for n in range(RANK // 256):
+        cols = slice(256 * n, 256 * (n + 1))
+        first = jnp.dot(rows, a_ref[:, cols], preferred_element_type=jnp.float32)
+        second = jnp.dot(rows, b_ref[:, cols], preferred_element_type=jnp.float32)
+        hidden_ref[:, cols] = (first * second).astype(jnp.bfloat16)
+    return outcome(moments, c_ref, mix_ref, expand_ref, w_ref, hidden_ref)
+
+
+def outcome(moments, c_ref, mix_ref, expand_ref, w_ref, hidden_ref):
     coeffs = jnp.dot(
         moments, mix_ref[...], precision=lax.Precision.HIGHEST, preferred_element_type=jnp.float32
     )
@@ -237,11 +246,6 @@
     middle = rest.astype(jnp.bfloat16).astype(jnp.float32)
     split = jnp.where(lane < 8, high, jnp.where(lane < 16, middle, rest - middle))
     split = split.astype(jnp.bfloat16)
-    for n in range(RANK // 256):
-        cols = slice(256 * n, 256 * (n + 1))
-        first = jnp.dot(rows, a_ref[:, cols], preferred_element_type=jnp.float32)
-        second = jnp.dot(rows, b_ref[:, cols], preferred_element_type=jnp.float32)
-        hidden_ref[:, cols] = (first * second).astype(jnp.bfloat16)
     hidden = hidden_ref[...]
     for n in range(NV // 256):
         cols = slice(256 * n, 256 * (n + 1))
@@ -319,8 +323,10 @@
     lax.fori_loop(0, GROUPS, group, 0)
 
 
-def second_xy_kernel(
-    vel_ref, space_ref, f_ref, part_ref, x_odd_ref, y_even_ref, y_odd_ref, x_even_ref, moved_ref
+def second_kernel(
+    vel_ref, space_ref, f_ref, part_ref, x_odd_ref, y_even_ref, y_odd_ref, x_even_ref,
+    mask_ref, rates_ref, a_ref, b_ref, c_ref, project_ref, mix_ref, expand_ref, w_ref,
+    out_ref, hidden_ref, moved_ref, first_ref, second_ref,
 ):
     uy, _ = speeds_yz()
     y_up = uy > 0.0
@@ -337,8 +343,7 @@
     def group(pair, upward):
         g = pair + half if upward else pair
         extra = pair + GROUPS
-        ux = (g.astype(jnp.float32) - 0.5 * (GX - 1)) * (SPACING * COURANT)
-        ux = ux if upward else -ux
+        ux = abs(g - 0.5 * (GX - 1)) * (SPACING * COURANT)
         for y in range(BY):
             here_x = (x_even_ref, x_odd_ref, x_is_even)
             behind, ahead = arrived(*here_x, g, y)[:: 1 if upward else -1]
@@ -385,27 +390,39 @@
                 moved_ref[g, here] = moved_ref[g, here] - uy * (flux - flux_before)
                 flux_before = flux
 
-    def downwards(pair, carry):
-        group(pair, False)
-        return carry
-
-    def upwards(pair, carry):
-        group(pair, True)
-        return carry
-
-    lax.fori_loop(0, half, downwards, 0)
-    lax.fori_loop(0, half, upwards, 0)
-
-
-def second_collide_kernel(
-    moved_ref, mask_ref, rates_ref, a_ref, b_ref, c_ref, project_ref, mix_ref, expand_ref, w_ref,
-    out_ref, hidden_ref,
-):
-    rows = jnp.concatenate([moved_ref[g].astype(jnp.bfloat16) for g in range(GROUPS)], axis=1)
+    moments = jnp.zeros((LAYER, WIDTH), jnp.float32)
+    chunk = 1
+    for pair in range(0, half, chunk):
+        groups = []
+        for upward in (False, True):
+            for i in range(chunk):
+                group(pair + i, upward)
+                groups.append(pair + i + (half if upward else 0))
+        rows = jnp.concatenate([moved_ref[g].astype(jnp.bfloat16) for g in groups], axis=1)
+        spans = [
+            slice(WIDTH * g, WIDTH * (g + chunk)) for g in (pair, pair + half)
+        ]
+
+        def times(ref, cols):
+            right = jnp.concatenate([ref[span, cols] for span in spans], axis=0)
+            return jnp.dot(rows, right, preferred_element_type=jnp.float32)
+
+        moments += times(project_ref, slice(0, WIDTH))
+        for n in range(RANK // 256):
+            cols = slice(256 * n, 256 * (n + 1))
+            first, second = times(a_ref, cols), times(b_ref, cols)
+            if pair:
+                first += first_ref[:, cols]
+                second += second_ref[:, cols]
+            if pair + chunk < half:
+                first_ref[:, cols] = first
+                second_ref[:, cols] = second
+            else:
+                hidden_ref[:, cols] = (first * second).astype(jnp.bfloat16)
+    rate = rates_ref[...]
     kinetic = mask_ref[...] > 0.0
-    rate = rates_ref[...]
-    for g, collision, equilibrium in collide(
-        rows, a_ref, b_ref, c_ref, project_ref, mix_ref, expand_ref, w_ref, hidden_ref
+    for g, collision, equilibrium in outcome(
+        moments, c_ref, mix_ref, expand_ref, w_ref, hidden_ref
     ):
         moved = moved_ref[g]
         change = jnp.where(kinetic, COLLIDE * collision, rate * (equilibrium - moved))
@@ -511,14 +528,13 @@
         second_z_kernel, "second_z", facts + ((f, VMEM), (kinetic_cells, VMEM)),
         ((wide, jnp.float32, VMEM), lanes), flops=6_000_000,
     )
-    (moved,) = call(
-        second_xy_kernel, "second_xy",
-        (vel, space) + tuple((o, VMEM) for o in (f, part, x_odd, y_even, y_odd, x_even)),
-        ((wide, jnp.float32, VMEM),), flops=12_000_000,
-    )
+    sums = VMEM((LAYER, RANK), jnp.float32)
     (result,) = call(
-        second_collide_kernel, "second_collide", ((moved, VMEM), (mask, VMEM), (rates, VMEM)) + held,
-        ((wide, half, VMEM),), scratch=(hidden,), flops=2_500_000_000, limit=C_VMEM,
+        second_kernel, "second_xy_collide",
+        (vel, space)
+        + tuple((o, VMEM) for o in (f, part, x_odd, y_even, y_odd, x_even, mask, rates)) + held,
+        ((wide, half, VMEM),), scratch=(hidden, VMEM(wide, jnp.float32), sums, sums),
+        flops=2_500_000_000, limit=C_VMEM,
     )
     pieces = lax.all_to_all(result, "vel", split_axis=0, concat_axis=0, tiled=True)
     (out,) = call(

time: 83.6 us -> 82.3 us (0.984)
  Pallas kernels: 18.8 us -> 17.5 us
    pallas_call x8 -> x7, Pallas kernels: 18.8 us -> 17.5 us  [call(): pl.pallas_call(kernel, out_shape=tuple(shapes), in_specs=[pl.BlockSpec(me...]
where the time goes in v9:
time: 82.3 us; the launch traced here: 82.1 us
  blocking collectives  46.2 us (56%)
  Pallas kernels  17.5 us (21%)
  starting transfers between devices  9.01 us (11%)
  waiting for transfers between devices  7.66 us (9%)
  local copies, waits for them, and re-layouts  1.64 us (2%)
    all_to_all x1, blocking collectives, body(): lax.all_to_all(rows, 'vel', split_axis=0, concat_axis=0, tiled=True)  23.5 us
    all_to_all x1, blocking collectives, body(): lax.all_to_all(result, 'vel', split_axis=0, concat_axis=0, tiled=True)  22.7 us
    pallas_call x7, Pallas kernels, call(): pl.pallas_call(kernel, out_shape=tuple(shapes), in_specs=[pl.BlockSpec(me...  17.5 us
    ppermute x1, starting transfers between devices, body(): behind = lax.ppermute(behind, both, upwind)  5.67 us
    ppermute x4, waiting for transfers between devices, body(): lax.ppermute(o, both, p)  4.95 us
    ppermute x4, starting transfers between devices, body(): lax.ppermute(o, both, p)  3.34 us
    ppermute x1, waiting for transfers between devices, body(): ahead = lax.ppermute(ahead, both, downwind)  2.7 us
  transfers between devices with their start and end apart: 6, of which 4 were waited for; matrix products, arithmetic and copies ran while one was open for 0% of the time, Pallas kernels for 6%

profile of v9, /device:TPU:1, one launch (start us, length us, event | category | flops | bytes accessed | tf_op | source)
XLA Modules:
  0.0 82.1 jit_solution(12276748206582768998)
XLA Ops:
  0.0 1.6 %copy-done = f32[16,16,16,128]{3,2,1,0:T(8,128)S(1)} copy-done((f32[16,16,16,128]{3,2,1,0:T(8,128)S(1)}, f32[16,16,16,128]{3,2,1,0:T(8,128)}, u32[]{:S(2)}) %copy-start) | copy-done | bytes 2097176
  1.6 5.7 %collective-permute-start = (bf16[2,16,16,128]{3,2,1,0:T(8,128)(2,1)S(1)}, bf16[2,16,16,128]{3,2,1,0:T(8,128)(2,1)S(1)}, u32[]{:S(2)}, u32[]{:S(2)}) collective-permute-start(bf16[2,16,16,128]{3,2,1,0:T(8,128)(2,1)S(1)} %get-tuple-element.15), channel_id=1, source_target_pairs={{0,112},{2,114},{4,116},{6,118},{1,113},{3,115},{5,117},{7,119},{9... | collective-permute-start | bytes 393224 | tf_op jit(solution)/shard_map/ppermute | solution.py:500
  7.3 0.0 collective-permute-start.1
  7.3 2.5 %first_yz.1.part_ref = f32[16,16,16,128]{3,2,1,0:T(8,128)S(1)} custom-call(f32[16,16,16,128]{3,2,1,0:T(8,128)S(1)} %copy-done), custom_call_target="tpu_custom_call" | custom-call | flops 12000000 | bytes 4194304 | tf_op jit(solution)/shard_map/first_yz/pallas_call | solution.py:80
  9.8 2.7 %collective-permute-done.1.ahead_ref = bf16[1,16,16,128]{3,2,1,0:T(8,128)(2,1)S(1)} collective-permute-done((bf16[1,16,16,128]{3,2,1,0:T(8,128)(2,1)S(1)}, bf16[1,16,16,128]{3,2,1,0:T(8,128)(2,1)S(1)}, u32[]{:S(2)}, u32[]{:S(2)}) %collective-permute-start.1) | collective-permute-done | bytes 65568 | tf_op jit(solution)/shard_map/ppermute | solution.py:501
  12.5 0.0 collective-permute-done.behind_ref
  12.5 1.3 %first_x.1 = bf16[16,256,128]{2,1,0:T(8,128)(2,1)S(1)} custom-call(s32[1]{0:T(128)} %bitcast.1.vel_ref, s32[1]{0:T(128)} %bitcast.space_ref, f32[16,16,16,128]{3,2,1,0:T(8,128)S(1)} %copy-done, f32[16,16,16,128]{3,2,1,0:T(8,128)S(1)} %first_yz.1.part_ref, bf16[2,16,16,128]{3,2,1,0:T(8,128)(2,1)S(1)} %collective-permute-done.behind_ref, ...), custom_call_target="tpu_custom_call" | custom-call | flops 6000000 | bytes 5439496 | tf_op jit(solution)/shard_map/first_x/pallas_call | solution.py:80
  13.8 0.0 copy-start.4
  13.8 0.0 copy-start.5
  13.8 0.0 copy-start.6
  13.8 0.0 copy-start.7
  13.8 0.0 copy-start.10
  13.8 23.5 %all_to_all.10.rows_ref = bf16[16,256,128]{2,1,0:T(8,128)(2,1)S(1)} all-to-all(bf16[16,256,128]{2,1,0:T(8,128)(2,1)S(1)} %first_x.1), channel_id=1, replica_groups=mesh['space'=8,'vel'=16] {'vel'}, dimensions={0} | all-to-all | bytes 2097152 | tf_op jit(solution)/shard_map/all_to_all | solution.py:514
  37.4 4.6 %first_collide.1 = (f32[16,256,128]{2,1,0:T(8,128)S(1)}, f32[256,128]{1,0:T(8,128)S(1)}, bf16[24,64,128]{2,1,0:T(8,128)(2,1)S(1)}, bf16[24,64,128]{2,1,0:T(8,128...) custom-call(s32[1]{0:T(128)} %bitcast.1.vel_ref, s32[1]{0:T(128)} %bitcast.space_ref, ...), custom_call_target="tpu_custom_call" | custom-call | flops 2500000000 | bytes 15458376 | tf_op jit(solution)/shard_map/first_collide/pallas_call | solution.py:80
  42.0 1.0 %collective-permute-start.2 = (bf16[24,64,128]{2,1,0:T(8,128)(2,1)S(1)}, bf16[24,64,128]{2,1,0:T(8,128)(2,1)S(1)}, u32[]{:S(2)}, u32[]{:S(2)}) collective-permute-start(bf16[24,64,128]{2,1,0:T(8,128)(2,1)S(1)} %get-tuple-element.19), channel_id=1, source_target_pairs={{0,112},{2,114},{4,116},{6,118},{1,9},{3,11},{5,13},{7,15},{9,1},{... | collective-permute-start | bytes 1179656 | tf_op jit(solution)/shard_map/ppermute | solution.py:525
  43.0 1.2 %collective-permute-start.4 = (bf16[24,64,128]{2,1,0:T(8,128)(2,1)S(1)}, bf16[24,64,128]{2,1,0:T(8,128)(2,1)S(1)}, u32[]{:S(2)}, u32[]{:S(2)}) collective-permute-start(bf16[24,64,128]{2,1,0:T(8,128)(2,1)S(1)} %get-tuple-element.21), channel_id=1, source_target_pairs={{0,6},{2,4},{4,2},{6,0},{1,7},{3,5},{5,3},{7,1},{9,15},{11,13},{13... | collective-permute-start | bytes 1179656 | tf_op jit(solution)/shard_map/ppermute | solution.py:525
  44.2 1.1 %collective-permute-start.5 = (bf16[24,64,128]{2,1,0:T(8,128)(2,1)S(1)}, bf16[24,64,128]{2,1,0:T(8,128)(2,1)S(1)}, u32[]{:S(2)}, u32[]{:S(2)}) collective-permute-start(bf16[24,64,128]{2,1,0:T(8,128)(2,1)S(1)} %get-tuple-element.22), channel_id=1, source_target_pairs={{0,1},{2,3},{4,5},{6,7},{1,0},{3,2},{5,4},{7,6},{9,8},{11,10},{13,... | collective-permute-start | bytes 1179656 | tf_op jit(solution)/shard_map/ppermute | solution.py:525
  45.4 2.5 %second_z.1 = (f32[16,256,128]{2,1,0:T(8,128)S(1)}, f32[256,128]{1,0:T(8,128)S(1)}) custom-call(s32[1]{0:T(128)} %bitcast.1.vel_ref, s32[1]{0:T(128)} %bitcast.space_ref, s32[2,8]{1,0:T(2,128)S(1)} %copy-done.10, f32[16,256,128]{2,1,0:T(8,128)S(1)} %get-tuple-element.17.f_ref, s32[2,4096]{1,0:T(2,128)S(1)} %copy-done.8), custom_call_target="tpu_custom_call" | custom-call | flops 6000000 | bytes 4358216 | tf_op jit(solution)/shard_map/second_z/pallas_call | solution.py:80
  47.9 2.6 %collective-permute-done.2.x_odd_ref = bf16[24,64,128]{2,1,0:T(8,128)(2,1)S(1)} collective-permute-done((bf16[24,64,128]{2,1,0:T(8,128)(2,1)S(1)}, bf16[24,64,128]{2,1,0:T(8,128)(2,1)S(1)}, u32[]{:S(2)}, u32[]{:S(2)}) %collective-permute-start.2) | collective-permute-done | bytes 393248 | tf_op jit(solution)/shard_map/ppermute | solution.py:525
  50.5 1.1 %collective-permute-done.3.y_even_ref = bf16[24,64,128]{2,1,0:T(8,128)(2,1)S(1)} collective-permute-done((bf16[24,64,128]{2,1,0:T(8,128)(2,1)S(1)}, bf16[24,64,128]{2,1,0:T(8,128)(2,1)S(1)}, u32[]{:S(2)}, u32[]{:S(2)}) %collective-permute-start.3) | collective-permute-done | bytes 393248 | tf_op jit(solution)/shard_map/ppermute | solution.py:525
  51.6 1.2 %collective-permute-done.4.y_odd_ref = bf16[24,64,128]{2,1,0:T(8,128)(2,1)S(1)} collective-permute-done((bf16[24,64,128]{2,1,0:T(8,128)(2,1)S(1)}, bf16[24,64,128]{2,1,0:T(8,128)(2,1)S(1)}, u32[]{:S(2)}, u32[]{:S(2)}) %collective-permute-start.4) | collective-permute-done | bytes 393248 | tf_op jit(solution)/shard_map/ppermute | solution.py:525
  52.8 5.2 %second_xy_collide.1 = bf16[16,256,128]{2,1,0:T(8,128)(2,1)S(1)} custom-call(s32[1]{0:T(128)} %bitcast.1.vel_ref, s32[1]{0:T(128)} %bitcast.space_ref, f32[16,256,128]{2,1,0:T(8,128)S(1)} %get-tuple-element.17.f_ref, f32[16,256,128]{2,1,0:T(8,128)S(1)} %get-tuple-element.18.part_ref, bf16[24,64,128]{2,1,0:T(8,128)(2,1)S(1)} %collective-permute-done.2.x_odd_ref, ...), custom_call_target="tpu_custom_call" | custom-call | flops 2500000000 | bytes 17637384 | tf_op jit(solution)/shard_map/second_xy_collide/pallas_call | solution.py:80
  58.1 22.7 %all_to_all.11.in_ref = bf16[16,256,128]{2,1,0:T(8,128)(2,1)S(1)} all-to-all(bf16[16,256,128]{2,1,0:T(8,128)(2,1)S(1)} %second_xy_collide.1), channel_id=1, replica_groups=mesh['space'=8,'vel'=16] {'vel'}, dimensions={0} | all-to-all | bytes 2097152 | tf_op jit(solution)/shard_map/all_to_all | solution.py:539
  80.8 1.4 %place.1 = f32[16,16,16,128]{3,2,1,0:T(8,128)} custom-call(s32[1]{0:T(128)} %bitcast.space_ref, bf16[16,256,128]{2,1,0:T(8,128)(2,1)S(1)} %all_to_all.11.in_ref), custom_call_target="tpu_custom_call" | custom-call | bytes 3145732 | tf_op jit(solution)/shard_map/place/pallas_call | solution.py:80
  (19 shorter events, 0.1 us)
Async XLA Ops:
  0.0 1.6 %copy-start = (f32[16,16,16,128]{3,2,1,0:T(8,128)S(1)}, f32[16,16,16,128]{3,2,1,0:T(8,128)}, u32[]{:S(2)}) copy-start(f32[16,16,16,128]{3,2,1,0:T(8,128)} %f_ref.3) | copy-start | bytes 6291460
  1.6 10.9 %collective-permute-start = (bf16[2,16,16,128]{3,2,1,0:T(8,128)(2,1)S(1)}, bf16[2,16,16,128]{3,2,1,0:T(8,128)(2,1)S(1)}, u32[]{:S(2)}, u32[]{:S(2)}) collective-permute-start(bf16[2,16,16,128]{3,2,1,0:T(8,128)(2,1)S(1)} %get-tuple-element.15), channel_id=1, source_target_pairs={{0,112},{2,114},{4,116},{6,118},{1,113},{3,115},{5,117},{7,119},{9... | collective-permute-start | bytes 393224 | tf_op jit(solution)/shard_map/ppermute | solution.py:500
  7.3 5.2 %collective-permute-start.1 = (bf16[1,16,16,128]{3,2,1,0:T(8,128)(2,1)S(1)}, bf16[1,16,16,128]{3,2,1,0:T(8,128)(2,1)S(1)}, u32[]{:S(2)}, u32[]{:S(2)}) collective-permute-start(bf16[1,16,16,128]{3,2,1,0:T(8,128)(2,1)S(1)} %get-tuple-element.16), channel_id=1, source_target_pairs={{0,16},{2,18},{4,20},{6,22},{1,17},{3,19},{5,21},{7,23},{9,121},{1... | collective-permute-start | bytes 196616 | tf_op jit(solution)/shard_map/ppermute | solution.py:501
  7.3 30.0 %copy-start.3 = (bf16[768,2048]{1,0:T(8,128)(2,1)S(1)}, bf16[768,2048]{1,0:T(8,128)(2,1)}, u32[]{:S(2)}) copy-start(bf16[768,2048]{1,0:T(8,128)(2,1)} %c_ref.3) | copy-start | bytes 9437188
  7.3 30.0 %copy-start.8 = (s32[2,4096]{1,0:T(2,128)S(1)}, s32[2,4096]{1,0:T(2,128)}, u32[]{:S(2)}) copy-start(s32[2,4096]{1,0:T(2,128)} %cells_ref.3) | copy-start | bytes 98308
  7.3 30.0 %copy-start.9 = (f32[1,2048]{1,0:T(1,128)S(1)}, f32[1,2048]{1,0:T(1,128)}, u32[]{:S(2)}) copy-start(f32[1,2048]{1,0:T(1,128)} %constant.20.clone.w_ref) | copy-start | bytes 24580
  12.5 24.8 %copy-start.1 = (bf16[2048,768]{1,0:T(8,128)(2,1)S(1)}, bf16[2048,768]{1,0:T(8,128)(2,1)}, u32[]{:S(2)}) copy-start(bf16[2048,768]{1,0:T(8,128)(2,1)} %a_ref.3) | copy-start | bytes 9437188
  12.5 24.8 %copy-start.2 = (bf16[2048,768]{1,0:T(8,128)(2,1)S(1)}, bf16[2048,768]{1,0:T(8,128)(2,1)}, u32[]{:S(2)}) copy-start(bf16[2048,768]{1,0:T(8,128)(2,1)} %b_ref.3) | copy-start | bytes 9437188
  13.8 23.6 %copy-start.4 = (bf16[128,2048]{1,0:T(8,128)(2,1)S(1)}, bf16[128,2048]{1,0:T(8,128)(2,1)}, u32[]{:S(2)}) copy-start(bf16[128,2048]{1,0:T(8,128)(2,1)} %constant.19.clone.expand_ref) | copy-start | bytes 1572868
  13.8 23.6 %copy-start.5 = (bf16[2048,128]{1,0:T(8,128)(2,1)S(1)}, bf16[2048,128]{1,0:T(8,128)(2,1)}, u32[]{:S(2)}) copy-start(bf16[2048,128]{1,0:T(8,128)(2,1)} %constant.17.clone.project_ref) | copy-start | bytes 1572868
  13.8 23.6 %copy-start.6 = (f32[128,128]{1,0:T(8,128)S(1)}, f32[128,128]{1,0:T(8,128)}, u32[]{:S(2)}) copy-start(f32[128,128]{1,0:T(8,128)} %constant.18.clone.mix_ref) | copy-start | bytes 196612
  13.8 23.6 %copy-start.7 = (f32[16,16,16]{2,1,0:T(8,128)S(1)}, f32[16,16,16]{2,1,0:T(8,128)}, u32[]{:S(2)}) copy-start(f32[16,16,16]{2,1,0:T(8,128)} %rate_ref.1) | copy-start | bytes 49156
  13.8 23.6 %copy-start.10 = (s32[2,8]{1,0:T(2,128)S(1)}, s32[2,8]{1,0:T(2,128)}, u32[]{:S(2)}) copy-start(s32[2,8]{1,0:T(2,128)} %count_ref.3) | copy-start | bytes 196
  42.0 8.5 %collective-permute-start.2 = (bf16[24,64,128]{2,1,0:T(8,128)(2,1)S(1)}, bf16[24,64,128]{2,1,0:T(8,128)(2,1)S(1)}, u32[]{:S(2)}, u32[]{:S(2)}) collective-permute-start(bf16[24,64,128]{2,1,0:T(8,128)(2,1)S(1)} %get-tuple-element.19), channel_id=1, source_target_pairs={{0,112},{2,114},{4,116},{6,118},{1,9},{3,11},{5,13},{7,15},{9,1},{... | collective-permute-start | bytes 1179656 | tf_op jit(solution)/shard_map/ppermute | solution.py:525
  43.0 8.6 %collective-permute-start.3 = (bf16[24,64,128]{2,1,0:T(8,128)(2,1)S(1)}, bf16[24,64,128]{2,1,0:T(8,128)(2,1)S(1)}, u32[]{:S(2)}, u32[]{:S(2)}) collective-permute-start(bf16[24,64,128]{2,1,0:T(8,128)(2,1)S(1)} %get-tuple-element.20), channel_id=1, source_target_pairs={{0,2},{2,0},{4,6},{6,4},{1,3},{3,1},{5,7},{7,5},{9,11},{11,9},{13,... | collective-permute-start | bytes 1179656 | tf_op jit(solution)/shard_map/ppermute | solution.py:525
  43.0 9.8 %collective-permute-start.4 = (bf16[24,64,128]{2,1,0:T(8,128)(2,1)S(1)}, bf16[24,64,128]{2,1,0:T(8,128)(2,1)S(1)}, u32[]{:S(2)}, u32[]{:S(2)}) collective-permute-start(bf16[24,64,128]{2,1,0:T(8,128)(2,1)S(1)} %get-tuple-element.21), channel_id=1, source_target_pairs={{0,6},{2,4},{4,2},{6,0},{1,7},{3,5},{5,3},{7,1},{9,15},{11,13},{13... | collective-permute-start | bytes 1179656 | tf_op jit(solution)/shard_map/ppermute | solution.py:525
  44.2 8.6 %collective-permute-start.5 = (bf16[24,64,128]{2,1,0:T(8,128)(2,1)S(1)}, bf16[24,64,128]{2,1,0:T(8,128)(2,1)S(1)}, u32[]{:S(2)}, u32[]{:S(2)}) collective-permute-start(bf16[24,64,128]{2,1,0:T(8,128)(2,1)S(1)} %get-tuple-element.22), channel_id=1, source_target_pairs={{0,1},{2,3},{4,5},{6,7},{1,0},{3,2},{5,4},{7,6},{9,8},{11,10},{13,... | collective-permute-start | bytes 1179656 | tf_op jit(solution)/shard_map/ppermute | solution.py:525

commit v10 on v9

--- a/solution.py
+++ b/solution.py
@@ -313,14 +313,33 @@
     _, uz = speeds_yz()
     z_up = uz > 0.0
 
-    def group(g, carry):
-        for c in range(BX * BY):
-            here = slice(NZ * c, NZ * (c + 1))
-            f = f_ref[g, here]
-            part_ref[g, here] = f - flux_change_z(f, uz, z_up)
+    half = GROUPS // 2
+
+    def group(g, upward):
+        ux = jnp.abs(g.astype(jnp.float32) - 0.5 * (GX - 1)) * (SPACING * COURANT)
+        for y in range(BY):
+            places = []
+            for k in range(BX):
+                x = k if upward else BX - 1 - k
+                places.append(slice(LINE * x + NZ * y, LINE * x + NZ * (y + 1)))
+            line = [f_ref[g, here] for here in places]
+            face_1 = ux * upwind_face(line[0], line[1], line[2])
+            face_2 = ux * upwind_face(line[1], line[2], line[3])
+            inner = [None, face_1, face_2 - face_1, -face_2]
+            for here, f, change in zip(places, line, inner, strict=True):
+                part = f - flux_change_z(f, uz, z_up)
+                part_ref[g, here] = part if change is None else part - change
+
+    def downwards(g, carry):
+        group(g, False)
         return carry
 
-    lax.fori_loop(0, GROUPS, group, 0)
+    def upwards(g, carry):
+        group(g, True)
+        return carry
+
+    lax.fori_loop(0, half, downwards, 0)
+    lax.fori_loop(half, GROUPS, upwards, 0)
 
 
 def second_kernel(
@@ -343,6 +362,7 @@
     def group(pair, upward):
         g = pair + half if upward else pair
         extra = pair + GROUPS
+        partial = {}
         ux = abs(g - 0.5 * (GX - 1)) * (SPACING * COURANT)
         for y in range(BY):
             here_x = (x_even_ref, x_odd_ref, x_is_even)
@@ -356,13 +376,16 @@
             def at_x(k):
                 return line[k + 2]
 
-            face_before = upwind_face(at_x(-2), at_x(-1), at_x(0))
+            face_0 = upwind_face(at_x(-1), at_x(0), at_x(1))
+            outer = [
+                face_0 - upwind_face(at_x(-2), at_x(-1), at_x(0)), -face_0, None,
+                upwind_face(at_x(2), at_x(3), at_x(4)),
+            ]
             for k in range(BX):
                 x = k if upward else BX - 1 - k
-                face = upwind_face(at_x(k - 1), at_x(k), at_x(k + 1))
                 here = slice(LINE * x + NZ * y, LINE * x + NZ * (y + 1))
-                moved_ref[g, here] = part_ref[g, here] - ux * (face - face_before)
-                face_before = face
+                part = part_ref[g, here]
+                partial[x, y] = part if outer[k] is None else part - ux * outer[k]
         for x in range(BX):
             here_y = (y_even_ref, y_odd_ref, y_is_even)
             below, above = arrived(*here_y, g, x)
@@ -387,7 +410,7 @@
                 next_up, next_down = edges(at_y(y), at_y(y + 1), at_y(y + 2))
                 flux = jnp.where(y_up, up, next_down)
                 here = slice(LINE * x + NZ * y, LINE * x + NZ * (y + 1))
-                moved_ref[g, here] = moved_ref[g, here] - uy * (flux - flux_before)
+                moved_ref[g, here] = partial[x, y] - uy * (flux - flux_before)
                 flux_before = flux
 
     moments = jnp.zeros((LAYER, WIDTH), jnp.float32)

time: 82.3 us -> 82 us (level)
  transfers between devices with their start and end apart: 6 -> 6, of which waited for: 4 -> 4; matrix products, arithmetic and copies ran while one was open for 0% -> 0% of each run, Pallas kernels for 6% -> 7%
where the time goes in v10:
time: 82 us; the launch traced here: 81.8 us
  blocking collectives  46.2 us (56%)
  Pallas kernels  17.5 us (21%)
  starting transfers between devices  9.01 us (11%)
  waiting for transfers between devices  7.26 us (9%)
  local copies, waits for them, and re-layouts  1.64 us (2%)
    all_to_all x1, blocking collectives, body(): lax.all_to_all(rows, 'vel', split_axis=0, concat_axis=0, tiled=True)  23.5 us
    all_to_all x1, blocking collectives, body(): lax.all_to_all(result, 'vel', split_axis=0, concat_axis=0, tiled=True)  22.7 us
    pallas_call x7, Pallas kernels, call(): pl.pallas_call(kernel, out_shape=tuple(shapes), in_specs=[pl.BlockSpec(me...  17.5 us
    ppermute x1, starting transfers between devices, body(): behind = lax.ppermute(behind, both, upwind)  5.67 us
    ppermute x4, waiting for transfers between devices, body(): lax.ppermute(o, both, p)  4.56 us
    ppermute x4, starting transfers between devices, body(): lax.ppermute(o, both, p)  3.34 us
    ppermute x1, waiting for transfers between devices, body(): ahead = lax.ppermute(ahead, both, downwind)  2.7 us
    unnamed x22, local copies, waits for them, and re-layouts  1.64 us
  transfers between devices with their start and end apart: 6, of which 4 were waited for; matrix products, arithmetic and copies ran while one was open for 0% of the time, Pallas kernels for 7%

profile of v10, /device:TPU:1, one launch (start us, length us, event | category | flops | bytes accessed | tf_op | source)
XLA Modules:
  0.0 81.8 jit_solution(5178601386959706356)
XLA Ops:
  0.0 1.6 %copy-done = f32[16,16,16,128]{3,2,1,0:T(8,128)S(1)} copy-done((f32[16,16,16,128]{3,2,1,0:T(8,128)S(1)}, f32[16,16,16,128]{3,2,1,0:T(8,128)}, u32[]{:S(2)}) %copy-start) | copy-done | bytes 2097176
  1.6 5.7 %collective-permute-start = (bf16[2,16,16,128]{3,2,1,0:T(8,128)(2,1)S(1)}, bf16[2,16,16,128]{3,2,1,0:T(8,128)(2,1)S(1)}, u32[]{:S(2)}, u32[]{:S(2)}) collective-permute-start(bf16[2,16,16,128]{3,2,1,0:T(8,128)(2,1)S(1)} %get-tuple-element.15), channel_id=1, source_target_pairs={{0,112},{2,114},{4,116},{6,118},{1,113},{3,115},{5,117},{7,119},{9... | collective-permute-start | bytes 393224 | tf_op jit(solution)/shard_map/ppermute | solution.py:523
  7.3 2.5 %first_yz.1.part_ref = f32[16,16,16,128]{3,2,1,0:T(8,128)S(1)} custom-call(f32[16,16,16,128]{3,2,1,0:T(8,128)S(1)} %copy-done), custom_call_target="tpu_custom_call" | custom-call | flops 12000000 | bytes 4194304 | tf_op jit(solution)/shard_map/first_yz/pallas_call | solution.py:80
  9.8 2.7 %collective-permute-done.1.ahead_ref = bf16[1,16,16,128]{3,2,1,0:T(8,128)(2,1)S(1)} collective-permute-done((bf16[1,16,16,128]{3,2,1,0:T(8,128)(2,1)S(1)}, bf16[1,16,16,128]{3,2,1,0:T(8,128)(2,1)S(1)}, u32[]{:S(2)}, u32[]{:S(2)}) %collective-permute-start.1) | collective-permute-done | bytes 65568 | tf_op jit(solution)/shard_map/ppermute | solution.py:524
  12.5 0.0 collective-permute-done.behind_ref
  12.5 1.3 %first_x.1 = bf16[16,256,128]{2,1,0:T(8,128)(2,1)S(1)} custom-call(s32[1]{0:T(128)} %bitcast.1.vel_ref, s32[1]{0:T(128)} %bitcast.space_ref, f32[16,16,16,128]{3,2,1,0:T(8,128)S(1)} %copy-done, f32[16,16,16,128]{3,2,1,0:T(8,128)S(1)} %first_yz.1.part_ref, bf16[2,16,16,128]{3,2,1,0:T(8,128)(2,1)S(1)} %collective-permute-done.behind_ref, ...), custom_call_target="tpu_custom_call" | custom-call | flops 6000000 | bytes 5439496 | tf_op jit(solution)/shard_map/first_x/pallas_call | solution.py:80
  13.8 0.0 copy-start.4
  13.8 0.0 copy-start.5
  13.8 0.0 copy-start.6
  13.8 0.0 copy-start.7
  13.8 0.0 copy-start.10
  13.8 23.5 %all_to_all.10.rows_ref = bf16[16,256,128]{2,1,0:T(8,128)(2,1)S(1)} all-to-all(bf16[16,256,128]{2,1,0:T(8,128)(2,1)S(1)} %first_x.1), channel_id=1, replica_groups=mesh['space'=8,'vel'=16] {'vel'}, dimensions={0} | all-to-all | bytes 2097152 | tf_op jit(solution)/shard_map/all_to_all | solution.py:537
  37.4 4.6 %first_collide.1 = (f32[16,256,128]{2,1,0:T(8,128)S(1)}, f32[256,128]{1,0:T(8,128)S(1)}, bf16[24,64,128]{2,1,0:T(8,128)(2,1)S(1)}, bf16[24,64,128]{2,1,0:T(8,128...) custom-call(s32[1]{0:T(128)} %bitcast.1.vel_ref, s32[1]{0:T(128)} %bitcast.space_ref, ...), custom_call_target="tpu_custom_call" | custom-call | flops 2500000000 | bytes 15458376 | tf_op jit(solution)/shard_map/first_collide/pallas_call | solution.py:80
  42.0 1.0 %collective-permute-start.2 = (bf16[24,64,128]{2,1,0:T(8,128)(2,1)S(1)}, bf16[24,64,128]{2,1,0:T(8,128)(2,1)S(1)}, u32[]{:S(2)}, u32[]{:S(2)}) collective-permute-start(bf16[24,64,128]{2,1,0:T(8,128)(2,1)S(1)} %get-tuple-element.19), channel_id=1, source_target_pairs={{0,112},{2,114},{4,116},{6,118},{1,9},{3,11},{5,13},{7,15},{9,1},{... | collective-permute-start | bytes 1179656 | tf_op jit(solution)/shard_map/ppermute | solution.py:548
  43.0 0.0 collective-permute-start.3
  43.0 1.2 %collective-permute-start.4 = (bf16[24,64,128]{2,1,0:T(8,128)(2,1)S(1)}, bf16[24,64,128]{2,1,0:T(8,128)(2,1)S(1)}, u32[]{:S(2)}, u32[]{:S(2)}) collective-permute-start(bf16[24,64,128]{2,1,0:T(8,128)(2,1)S(1)} %get-tuple-element.21), channel_id=1, source_target_pairs={{0,6},{2,4},{4,2},{6,0},{1,7},{3,5},{5,3},{7,1},{9,15},{11,13},{13... | collective-permute-start | bytes 1179656 | tf_op jit(solution)/shard_map/ppermute | solution.py:548
  44.2 1.1 %collective-permute-start.5 = (bf16[24,64,128]{2,1,0:T(8,128)(2,1)S(1)}, bf16[24,64,128]{2,1,0:T(8,128)(2,1)S(1)}, u32[]{:S(2)}, u32[]{:S(2)}) collective-permute-start(bf16[24,64,128]{2,1,0:T(8,128)(2,1)S(1)} %get-tuple-element.22), channel_id=1, source_target_pairs={{0,1},{2,3},{4,5},{6,7},{1,0},{3,2},{5,4},{7,6},{9,8},{11,10},{13,... | collective-permute-start | bytes 1179656 | tf_op jit(solution)/shard_map/ppermute | solution.py:548
  45.4 2.9 %second_z.1 = (f32[16,256,128]{2,1,0:T(8,128)S(1)}, f32[256,128]{1,0:T(8,128)S(1)}) custom-call(s32[1]{0:T(128)} %bitcast.1.vel_ref, s32[1]{0:T(128)} %bitcast.space_ref, s32[2,8]{1,0:T(2,128)S(1)} %copy-done.10, f32[16,256,128]{2,1,0:T(8,128)S(1)} %get-tuple-element.17.f_ref, s32[2,4096]{1,0:T(2,128)S(1)} %copy-done.8), custom_call_target="tpu_custom_call" | custom-call | flops 6000000 | bytes 4358216 | tf_op jit(solution)/shard_map/second_z/pallas_call | solution.py:80
  48.3 2.2 %collective-permute-done.2.x_odd_ref = bf16[24,64,128]{2,1,0:T(8,128)(2,1)S(1)} collective-permute-done((bf16[24,64,128]{2,1,0:T(8,128)(2,1)S(1)}, bf16[24,64,128]{2,1,0:T(8,128)(2,1)S(1)}, u32[]{:S(2)}, u32[]{:S(2)}) %collective-permute-start.2) | collective-permute-done | bytes 393248 | tf_op jit(solution)/shard_map/ppermute | solution.py:548
  50.5 1.1 %collective-permute-done.3.y_even_ref = bf16[24,64,128]{2,1,0:T(8,128)(2,1)S(1)} collective-permute-done((bf16[24,64,128]{2,1,0:T(8,128)(2,1)S(1)}, bf16[24,64,128]{2,1,0:T(8,128)(2,1)S(1)}, u32[]{:S(2)}, u32[]{:S(2)}) %collective-permute-start.3) | collective-permute-done | bytes 393248 | tf_op jit(solution)/shard_map/ppermute | solution.py:548
  51.6 1.2 %collective-permute-done.4.y_odd_ref = bf16[24,64,128]{2,1,0:T(8,128)(2,1)S(1)} collective-permute-done((bf16[24,64,128]{2,1,0:T(8,128)(2,1)S(1)}, bf16[24,64,128]{2,1,0:T(8,128)(2,1)S(1)}, u32[]{:S(2)}, u32[]{:S(2)}) %collective-permute-start.4) | collective-permute-done | bytes 393248 | tf_op jit(solution)/shard_map/ppermute | solution.py:548
  52.8 4.9 %second_xy_collide.1 = bf16[16,256,128]{2,1,0:T(8,128)(2,1)S(1)} custom-call(s32[1]{0:T(128)} %bitcast.1.vel_ref, s32[1]{0:T(128)} %bitcast.space_ref, f32[16,256,128]{2,1,0:T(8,128)S(1)} %get-tuple-element.17.f_ref, f32[16,256,128]{2,1,0:T(8,128)S(1)} %get-tuple-element.18.part_ref, bf16[24,64,128]{2,1,0:T(8,128)(2,1)S(1)} %collective-permute-done.2.x_odd_ref, ...), custom_call_target="tpu_custom_call" | custom-call | flops 2500000000 | bytes 17637384 | tf_op jit(solution)/shard_map/second_xy_collide/pallas_call | solution.py:80
  57.7 22.7 %all_to_all.11.in_ref = bf16[16,256,128]{2,1,0:T(8,128)(2,1)S(1)} all-to-all(bf16[16,256,128]{2,1,0:T(8,128)(2,1)S(1)} %second_xy_collide.1), channel_id=1, replica_groups=mesh['space'=8,'vel'=16] {'vel'}, dimensions={0} | all-to-all | bytes 2097152 | tf_op jit(solution)/shard_map/all_to_all | solution.py:562
  80.4 1.4 %place.1 = f32[16,16,16,128]{3,2,1,0:T(8,128)} custom-call(s32[1]{0:T(128)} %bitcast.space_ref, bf16[16,256,128]{2,1,0:T(8,128)(2,1)S(1)} %all_to_all.11.in_ref), custom_call_target="tpu_custom_call" | custom-call | bytes 3145732 | tf_op jit(solution)/shard_map/place/pallas_call | solution.py:80
  (19 shorter events, 0.1 us)
Async XLA Ops:
  0.0 1.6 %copy-start = (f32[16,16,16,128]{3,2,1,0:T(8,128)S(1)}, f32[16,16,16,128]{3,2,1,0:T(8,128)}, u32[]{:S(2)}) copy-start(f32[16,16,16,128]{3,2,1,0:T(8,128)} %f_ref.3) | copy-start | bytes 6291460
  1.6 10.9 %collective-permute-start = (bf16[2,16,16,128]{3,2,1,0:T(8,128)(2,1)S(1)}, bf16[2,16,16,128]{3,2,1,0:T(8,128)(2,1)S(1)}, u32[]{:S(2)}, u32[]{:S(2)}) collective-permute-start(bf16[2,16,16,128]{3,2,1,0:T(8,128)(2,1)S(1)} %get-tuple-element.15), channel_id=1, source_target_pairs={{0,112},{2,114},{4,116},{6,118},{1,113},{3,115},{5,117},{7,119},{9... | collective-permute-start | bytes 393224 | tf_op jit(solution)/shard_map/ppermute | solution.py:523
  7.3 5.2 %collective-permute-start.1 = (bf16[1,16,16,128]{3,2,1,0:T(8,128)(2,1)S(1)}, bf16[1,16,16,128]{3,2,1,0:T(8,128)(2,1)S(1)}, u32[]{:S(2)}, u32[]{:S(2)}) collective-permute-start(bf16[1,16,16,128]{3,2,1,0:T(8,128)(2,1)S(1)} %get-tuple-element.16), channel_id=1, source_target_pairs={{0,16},{2,18},{4,20},{6,22},{1,17},{3,19},{5,21},{7,23},{9,121},{1... | collective-permute-start | bytes 196616 | tf_op jit(solution)/shard_map/ppermute | solution.py:524
  7.3 30.0 %copy-start.3 = (bf16[768,2048]{1,0:T(8,128)(2,1)S(1)}, bf16[768,2048]{1,0:T(8,128)(2,1)}, u32[]{:S(2)}) copy-start(bf16[768,2048]{1,0:T(8,128)(2,1)} %c_ref.3) | copy-start | bytes 9437188
  7.3 30.0 %copy-start.8 = (s32[2,4096]{1,0:T(2,128)S(1)}, s32[2,4096]{1,0:T(2,128)}, u32[]{:S(2)}) copy-start(s32[2,4096]{1,0:T(2,128)} %cells_ref.3) | copy-start | bytes 98308
  7.3 30.0 %copy-start.9 = (f32[1,2048]{1,0:T(1,128)S(1)}, f32[1,2048]{1,0:T(1,128)}, u32[]{:S(2)}) copy-start(f32[1,2048]{1,0:T(1,128)} %constant.20.clone.w_ref) | copy-start | bytes 24580
  12.5 24.8 %copy-start.1 = (bf16[2048,768]{1,0:T(8,128)(2,1)S(1)}, bf16[2048,768]{1,0:T(8,128)(2,1)}, u32[]{:S(2)}) copy-start(bf16[2048,768]{1,0:T(8,128)(2,1)} %a_ref.3) | copy-start | bytes 9437188
  12.5 24.8 %copy-start.2 = (bf16[2048,768]{1,0:T(8,128)(2,1)S(1)}, bf16[2048,768]{1,0:T(8,128)(2,1)}, u32[]{:S(2)}) copy-start(bf16[2048,768]{1,0:T(8,128)(2,1)} %b_ref.3) | copy-start | bytes 9437188
  13.8 23.6 %copy-start.4 = (bf16[128,2048]{1,0:T(8,128)(2,1)S(1)}, bf16[128,2048]{1,0:T(8,128)(2,1)}, u32[]{:S(2)}) copy-start(bf16[128,2048]{1,0:T(8,128)(2,1)} %constant.19.clone.expand_ref) | copy-start | bytes 1572868
  13.8 23.6 %copy-start.5 = (bf16[2048,128]{1,0:T(8,128)(2,1)S(1)}, bf16[2048,128]{1,0:T(8,128)(2,1)}, u32[]{:S(2)}) copy-start(bf16[2048,128]{1,0:T(8,128)(2,1)} %constant.17.clone.project_ref) | copy-start | bytes 1572868
  13.8 23.6 %copy-start.6 = (f32[128,128]{1,0:T(8,128)S(1)}, f32[128,128]{1,0:T(8,128)}, u32[]{:S(2)}) copy-start(f32[128,128]{1,0:T(8,128)} %constant.18.clone.mix_ref) | copy-start | bytes 196612
  13.8 23.6 %copy-start.7 = (f32[16,16,16]{2,1,0:T(8,128)S(1)}, f32[16,16,16]{2,1,0:T(8,128)}, u32[]{:S(2)}) copy-start(f32[16,16,16]{2,1,0:T(8,128)} %rate_ref.1) | copy-start | bytes 49156
  13.8 23.6 %copy-start.10 = (s32[2,8]{1,0:T(2,128)S(1)}, s32[2,8]{1,0:T(2,128)}, u32[]{:S(2)}) copy-start(s32[2,8]{1,0:T(2,128)} %count_ref.3) | copy-start | bytes 196
  42.0 8.5 %collective-permute-start.2 = (bf16[24,64,128]{2,1,0:T(8,128)(2,1)S(1)}, bf16[24,64,128]{2,1,0:T(8,128)(2,1)S(1)}, u32[]{:S(2)}, u32[]{:S(2)}) collective-permute-start(bf16[24,64,128]{2,1,0:T(8,128)(2,1)S(1)} %get-tuple-element.19), channel_id=1, source_target_pairs={{0,112},{2,114},{4,116},{6,118},{1,9},{3,11},{5,13},{7,15},{9,1},{... | collective-permute-start | bytes 1179656 | tf_op jit(solution)/shard_map/ppermute | solution.py:548
  43.0 8.6 %collective-permute-start.3 = (bf16[24,64,128]{2,1,0:T(8,128)(2,1)S(1)}, bf16[24,64,128]{2,1,0:T(8,128)(2,1)S(1)}, u32[]{:S(2)}, u32[]{:S(2)}) collective-permute-start(bf16[24,64,128]{2,1,0:T(8,128)(2,1)S(1)} %get-tuple-element.20), channel_id=1, source_target_pairs={{0,2},{2,0},{4,6},{6,4},{1,3},{3,1},{5,7},{7,5},{9,11},{11,9},{13,... | collective-permute-start | bytes 1179656 | tf_op jit(solution)/shard_map/ppermute | solution.py:548
  43.0 9.8 %collective-permute-start.4 = (bf16[24,64,128]{2,1,0:T(8,128)(2,1)S(1)}, bf16[24,64,128]{2,1,0:T(8,128)(2,1)S(1)}, u32[]{:S(2)}, u32[]{:S(2)}) collective-permute-start(bf16[24,64,128]{2,1,0:T(8,128)(2,1)S(1)} %get-tuple-element.21), channel_id=1, source_target_pairs={{0,6},{2,4},{4,2},{6,0},{1,7},{3,5},{5,3},{7,1},{9,15},{11,13},{13... | collective-permute-start | bytes 1179656 | tf_op jit(solution)/shard_map/ppermute | solution.py:548
  44.2 8.6 %collective-permute-start.5 = (bf16[24,64,128]{2,1,0:T(8,128)(2,1)S(1)}, bf16[24,64,128]{2,1,0:T(8,128)(2,1)S(1)}, u32[]{:S(2)}, u32[]{:S(2)}) collective-permute-start(bf16[24,64,128]{2,1,0:T(8,128)(2,1)S(1)} %get-tuple-element.22), channel_id=1, source_target_pairs={{0,1},{2,3},{4,5},{6,7},{1,0},{3,2},{5,4},{7,6},{9,8},{11,10},{13,... | collective-permute-start | bytes 1179656 | tf_op jit(solution)/shard_map/ppermute | solution.py:548

commit v11 on v10

--- a/solution.py
+++ b/solution.py
@@ -264,6 +264,9 @@
     f_ref, rates_ref, x_even_ref, x_odd_ref, y_even_ref, y_odd_ref, hidden_ref,
 ):
     rows = jnp.concatenate([rows_ref[g] for g in range(GROUPS)], axis=1)
+    terms = collide(
+        rows, a_ref, b_ref, c_ref, project_ref, mix_ref, expand_ref, w_ref, hidden_ref
+    )
     kinetic = kinetic_cells_of(0, vel_ref, space_ref, count_ref, cells_ref) > 0.0
     rate = rates_of(vel_ref, space_ref, rate_ref)
     rates_ref[...] = rate
@@ -276,9 +279,7 @@
         odd_ref[where] = jnp.where(is_even, down, up).astype(jnp.bfloat16)
 
     low_lane = lax.broadcasted_iota(jnp.int32, (NZ, WIDTH), 1) < WIDTH // 2
-    for g, collision, equilibrium in collide(
-        rows, a_ref, b_ref, c_ref, project_ref, mix_ref, expand_ref, w_ref, hidden_ref
-    ):
+    for g, collision, equilibrium in terms:
         moved = rows_ref[g].astype(jnp.float32)
         change = jnp.where(kinetic, COLLIDE * collision, rate * (equilibrium - moved))
         result = moved + change

time: 82 us -> 82 us (level)
  no operation moved by 1% of the time
where the time goes in v11:
time: 82 us; the launch traced here: 81.8 us
  blocking collectives  46.2 us (56%)
  Pallas kernels  17.5 us (21%)
  starting transfers between devices  9.01 us (11%)
  waiting for transfers between devices  7.26 us (9%)
  local copies, waits for them, and re-layouts  1.64 us (2%)
    all_to_all x1, blocking collectives, body(): lax.all_to_all(rows, 'vel', split_axis=0, concat_axis=0, tiled=True)  23.5 us
    all_to_all x1, blocking collectives, body(): lax.all_to_all(result, 'vel', split_axis=0, concat_axis=0, tiled=True)  22.7 us
    pallas_call x7, Pallas kernels, call(): pl.pallas_call(kernel, out_shape=tuple(shapes), in_specs=[pl.BlockSpec(me...  17.5 us
    ppermute x1, starting transfers between devices, body(): behind = lax.ppermute(behind, both, upwind)  5.67 us
    ppermute x4, waiting for transfers between devices, body(): lax.ppermute(o, both, p)  4.56 us
    ppermute x4, starting transfers between devices, body(): lax.ppermute(o, both, p)  3.34 us
    ppermute x1, waiting for transfers between devices, body(): ahead = lax.ppermute(ahead, both, downwind)  2.7 us
    unnamed x22, local copies, waits for them, and re-layouts  1.64 us
  transfers between devices with their start and end apart: 6, of which 4 were waited for; matrix products, arithmetic and copies ran while one was open for 0% of the time, Pallas kernels for 7%

profile of v11, /device:TPU:1, one launch (start us, length us, event | category | flops | bytes accessed | tf_op | source)
XLA Modules:
  0.0 81.8 jit_solution(5178601386959706356)
XLA Ops:
  0.0 1.6 %copy-done = f32[16,16,16,128]{3,2,1,0:T(8,128)S(1)} copy-done((f32[16,16,16,128]{3,2,1,0:T(8,128)S(1)}, f32[16,16,16,128]{3,2,1,0:T(8,128)}, u32[]{:S(2)}) %copy-start) | copy-done | bytes 2097176
  1.6 5.7 %collective-permute-start = (bf16[2,16,16,128]{3,2,1,0:T(8,128)(2,1)S(1)}, bf16[2,16,16,128]{3,2,1,0:T(8,128)(2,1)S(1)}, u32[]{:S(2)}, u32[]{:S(2)}) collective-permute-start(bf16[2,16,16,128]{3,2,1,0:T(8,128)(2,1)S(1)} %get-tuple-element.15), channel_id=1, source_target_pairs={{0,112},{2,114},{4,116},{6,118},{1,113},{3,115},{5,117},{7,119},{9... | collective-permute-start | bytes 393224 | tf_op jit(solution)/shard_map/ppermute | solution.py:524
  7.3 2.5 %first_yz.1.part_ref = f32[16,16,16,128]{3,2,1,0:T(8,128)S(1)} custom-call(f32[16,16,16,128]{3,2,1,0:T(8,128)S(1)} %copy-done), custom_call_target="tpu_custom_call" | custom-call | flops 12000000 | bytes 4194304 | tf_op jit(solution)/shard_map/first_yz/pallas_call | solution.py:80
  9.8 2.7 %collective-permute-done.1.ahead_ref = bf16[1,16,16,128]{3,2,1,0:T(8,128)(2,1)S(1)} collective-permute-done((bf16[1,16,16,128]{3,2,1,0:T(8,128)(2,1)S(1)}, bf16[1,16,16,128]{3,2,1,0:T(8,128)(2,1)S(1)}, u32[]{:S(2)}, u32[]{:S(2)}) %collective-permute-start.1) | collective-permute-done | bytes 65568 | tf_op jit(solution)/shard_map/ppermute | solution.py:525
  12.5 0.0 collective-permute-done.behind_ref
  12.5 1.3 %first_x.1 = bf16[16,256,128]{2,1,0:T(8,128)(2,1)S(1)} custom-call(s32[1]{0:T(128)} %bitcast.1.vel_ref, s32[1]{0:T(128)} %bitcast.space_ref, f32[16,16,16,128]{3,2,1,0:T(8,128)S(1)} %copy-done, f32[16,16,16,128]{3,2,1,0:T(8,128)S(1)} %first_yz.1.part_ref, bf16[2,16,16,128]{3,2,1,0:T(8,128)(2,1)S(1)} %collective-permute-done.behind_ref, ...), custom_call_target="tpu_custom_call" | custom-call | flops 6000000 | bytes 5439496 | tf_op jit(solution)/shard_map/first_x/pallas_call | solution.py:80
  13.8 0.0 copy-start.4
  13.8 0.0 copy-start.5
  13.8 0.0 copy-start.6
  13.8 0.0 copy-start.7
  13.8 0.0 copy-start.10
  13.8 23.5 %all_to_all.10.rows_ref = bf16[16,256,128]{2,1,0:T(8,128)(2,1)S(1)} all-to-all(bf16[16,256,128]{2,1,0:T(8,128)(2,1)S(1)} %first_x.1), channel_id=1, replica_groups=mesh['space'=8,'vel'=16] {'vel'}, dimensions={0} | all-to-all | bytes 2097152 | tf_op jit(solution)/shard_map/all_to_all | solution.py:538
  37.4 4.6 %first_collide.1 = (f32[16,256,128]{2,1,0:T(8,128)S(1)}, f32[256,128]{1,0:T(8,128)S(1)}, bf16[24,64,128]{2,1,0:T(8,128)(2,1)S(1)}, bf16[24,64,128]{2,1,0:T(8,128...) custom-call(s32[1]{0:T(128)} %bitcast.1.vel_ref, s32[1]{0:T(128)} %bitcast.space_ref, ...), custom_call_target="tpu_custom_call" | custom-call | flops 2500000000 | bytes 15458376 | tf_op jit(solution)/shard_map/first_collide/pallas_call | solution.py:80
  42.0 1.0 %collective-permute-start.2 = (bf16[24,64,128]{2,1,0:T(8,128)(2,1)S(1)}, bf16[24,64,128]{2,1,0:T(8,128)(2,1)S(1)}, u32[]{:S(2)}, u32[]{:S(2)}) collective-permute-start(bf16[24,64,128]{2,1,0:T(8,128)(2,1)S(1)} %get-tuple-element.19), channel_id=1, source_target_pairs={{0,112},{2,114},{4,116},{6,118},{1,9},{3,11},{5,13},{7,15},{9,1},{... | collective-permute-start | bytes 1179656 | tf_op jit(solution)/shard_map/ppermute | solution.py:549
  43.0 0.0 collective-permute-start.3
  43.0 1.2 %collective-permute-start.4 = (bf16[24,64,128]{2,1,0:T(8,128)(2,1)S(1)}, bf16[24,64,128]{2,1,0:T(8,128)(2,1)S(1)}, u32[]{:S(2)}, u32[]{:S(2)}) collective-permute-start(bf16[24,64,128]{2,1,0:T(8,128)(2,1)S(1)} %get-tuple-element.21), channel_id=1, source_target_pairs={{0,6},{2,4},{4,2},{6,0},{1,7},{3,5},{5,3},{7,1},{9,15},{11,13},{13... | collective-permute-start | bytes 1179656 | tf_op jit(solution)/shard_map/ppermute | solution.py:549
  44.2 1.1 %collective-permute-start.5 = (bf16[24,64,128]{2,1,0:T(8,128)(2,1)S(1)}, bf16[24,64,128]{2,1,0:T(8,128)(2,1)S(1)}, u32[]{:S(2)}, u32[]{:S(2)}) collective-permute-start(bf16[24,64,128]{2,1,0:T(8,128)(2,1)S(1)} %get-tuple-element.22), channel_id=1, source_target_pairs={{0,1},{2,3},{4,5},{6,7},{1,0},{3,2},{5,4},{7,6},{9,8},{11,10},{13,... | collective-permute-start | bytes 1179656 | tf_op jit(solution)/shard_map/ppermute | solution.py:549
  45.4 2.9 %second_z.1 = (f32[16,256,128]{2,1,0:T(8,128)S(1)}, f32[256,128]{1,0:T(8,128)S(1)}) custom-call(s32[1]{0:T(128)} %bitcast.1.vel_ref, s32[1]{0:T(128)} %bitcast.space_ref, s32[2,8]{1,0:T(2,128)S(1)} %copy-done.10, f32[16,256,128]{2,1,0:T(8,128)S(1)} %get-tuple-element.17.f_ref, s32[2,4096]{1,0:T(2,128)S(1)} %copy-done.8), custom_call_target="tpu_custom_call" | custom-call | flops 6000000 | bytes 4358216 | tf_op jit(solution)/shard_map/second_z/pallas_call | solution.py:80
  48.3 2.2 %collective-permute-done.2.x_odd_ref = bf16[24,64,128]{2,1,0:T(8,128)(2,1)S(1)} collective-permute-done((bf16[24,64,128]{2,1,0:T(8,128)(2,1)S(1)}, bf16[24,64,128]{2,1,0:T(8,128)(2,1)S(1)}, u32[]{:S(2)}, u32[]{:S(2)}) %collective-permute-start.2) | collective-permute-done | bytes 393248 | tf_op jit(solution)/shard_map/ppermute | solution.py:549
  50.5 1.1 %collective-permute-done.3.y_even_ref = bf16[24,64,128]{2,1,0:T(8,128)(2,1)S(1)} collective-permute-done((bf16[24,64,128]{2,1,0:T(8,128)(2,1)S(1)}, bf16[24,64,128]{2,1,0:T(8,128)(2,1)S(1)}, u32[]{:S(2)}, u32[]{:S(2)}) %collective-permute-start.3) | collective-permute-done | bytes 393248 | tf_op jit(solution)/shard_map/ppermute | solution.py:549
  51.6 1.2 %collective-permute-done.4.y_odd_ref = bf16[24,64,128]{2,1,0:T(8,128)(2,1)S(1)} collective-permute-done((bf16[24,64,128]{2,1,0:T(8,128)(2,1)S(1)}, bf16[24,64,128]{2,1,0:T(8,128)(2,1)S(1)}, u32[]{:S(2)}, u32[]{:S(2)}) %collective-permute-start.4) | collective-permute-done | bytes 393248 | tf_op jit(solution)/shard_map/ppermute | solution.py:549
  52.8 4.9 %second_xy_collide.1 = bf16[16,256,128]{2,1,0:T(8,128)(2,1)S(1)} custom-call(s32[1]{0:T(128)} %bitcast.1.vel_ref, s32[1]{0:T(128)} %bitcast.space_ref, f32[16,256,128]{2,1,0:T(8,128)S(1)} %get-tuple-element.17.f_ref, f32[16,256,128]{2,1,0:T(8,128)S(1)} %get-tuple-element.18.part_ref, bf16[24,64,128]{2,1,0:T(8,128)(2,1)S(1)} %collective-permute-done.2.x_odd_ref, ...), custom_call_target="tpu_custom_call" | custom-call | flops 2500000000 | bytes 17637384 | tf_op jit(solution)/shard_map/second_xy_collide/pallas_call | solution.py:80
  57.7 22.7 %all_to_all.11.in_ref = bf16[16,256,128]{2,1,0:T(8,128)(2,1)S(1)} all-to-all(bf16[16,256,128]{2,1,0:T(8,128)(2,1)S(1)} %second_xy_collide.1), channel_id=1, replica_groups=mesh['space'=8,'vel'=16] {'vel'}, dimensions={0} | all-to-all | bytes 2097152 | tf_op jit(solution)/shard_map/all_to_all | solution.py:563
  80.4 1.4 %place.1 = f32[16,16,16,128]{3,2,1,0:T(8,128)} custom-call(s32[1]{0:T(128)} %bitcast.space_ref, bf16[16,256,128]{2,1,0:T(8,128)(2,1)S(1)} %all_to_all.11.in_ref), custom_call_target="tpu_custom_call" | custom-call | bytes 3145732 | tf_op jit(solution)/shard_map/place/pallas_call | solution.py:80
  (19 shorter events, 0.1 us)
Async XLA Ops:
  0.0 1.6 %copy-start = (f32[16,16,16,128]{3,2,1,0:T(8,128)S(1)}, f32[16,16,16,128]{3,2,1,0:T(8,128)}, u32[]{:S(2)}) copy-start(f32[16,16,16,128]{3,2,1,0:T(8,128)} %f_ref.3) | copy-start | bytes 6291460
  1.6 10.9 %collective-permute-start = (bf16[2,16,16,128]{3,2,1,0:T(8,128)(2,1)S(1)}, bf16[2,16,16,128]{3,2,1,0:T(8,128)(2,1)S(1)}, u32[]{:S(2)}, u32[]{:S(2)}) collective-permute-start(bf16[2,16,16,128]{3,2,1,0:T(8,128)(2,1)S(1)} %get-tuple-element.15), channel_id=1, source_target_pairs={{0,112},{2,114},{4,116},{6,118},{1,113},{3,115},{5,117},{7,119},{9... | collective-permute-start | bytes 393224 | tf_op jit(solution)/shard_map/ppermute | solution.py:524
  7.3 5.2 %collective-permute-start.1 = (bf16[1,16,16,128]{3,2,1,0:T(8,128)(2,1)S(1)}, bf16[1,16,16,128]{3,2,1,0:T(8,128)(2,1)S(1)}, u32[]{:S(2)}, u32[]{:S(2)}) collective-permute-start(bf16[1,16,16,128]{3,2,1,0:T(8,128)(2,1)S(1)} %get-tuple-element.16), channel_id=1, source_target_pairs={{0,16},{2,18},{4,20},{6,22},{1,17},{3,19},{5,21},{7,23},{9,121},{1... | collective-permute-start | bytes 196616 | tf_op jit(solution)/shard_map/ppermute | solution.py:525
  7.3 30.0 %copy-start.3 = (bf16[768,2048]{1,0:T(8,128)(2,1)S(1)}, bf16[768,2048]{1,0:T(8,128)(2,1)}, u32[]{:S(2)}) copy-start(bf16[768,2048]{1,0:T(8,128)(2,1)} %c_ref.3) | copy-start | bytes 9437188
  7.3 30.0 %copy-start.8 = (s32[2,4096]{1,0:T(2,128)S(1)}, s32[2,4096]{1,0:T(2,128)}, u32[]{:S(2)}) copy-start(s32[2,4096]{1,0:T(2,128)} %cells_ref.3) | copy-start | bytes 98308
  7.3 30.0 %copy-start.9 = (f32[1,2048]{1,0:T(1,128)S(1)}, f32[1,2048]{1,0:T(1,128)}, u32[]{:S(2)}) copy-start(f32[1,2048]{1,0:T(1,128)} %constant.20.clone.w_ref) | copy-start | bytes 24580
  12.5 24.8 %copy-start.1 = (bf16[2048,768]{1,0:T(8,128)(2,1)S(1)}, bf16[2048,768]{1,0:T(8,128)(2,1)}, u32[]{:S(2)}) copy-start(bf16[2048,768]{1,0:T(8,128)(2,1)} %a_ref.3) | copy-start | bytes 9437188
  12.5 24.8 %copy-start.2 = (bf16[2048,768]{1,0:T(8,128)(2,1)S(1)}, bf16[2048,768]{1,0:T(8,128)(2,1)}, u32[]{:S(2)}) copy-start(bf16[2048,768]{1,0:T(8,128)(2,1)} %b_ref.3) | copy-start | bytes 9437188
  13.8 23.6 %copy-start.4 = (bf16[128,2048]{1,0:T(8,128)(2,1)S(1)}, bf16[128,2048]{1,0:T(8,128)(2,1)}, u32[]{:S(2)}) copy-start(bf16[128,2048]{1,0:T(8,128)(2,1)} %constant.19.clone.expand_ref) | copy-start | bytes 1572868
  13.8 23.6 %copy-start.5 = (bf16[2048,128]{1,0:T(8,128)(2,1)S(1)}, bf16[2048,128]{1,0:T(8,128)(2,1)}, u32[]{:S(2)}) copy-start(bf16[2048,128]{1,0:T(8,128)(2,1)} %constant.17.clone.project_ref) | copy-start | bytes 1572868
  13.8 23.6 %copy-start.6 = (f32[128,128]{1,0:T(8,128)S(1)}, f32[128,128]{1,0:T(8,128)}, u32[]{:S(2)}) copy-start(f32[128,128]{1,0:T(8,128)} %constant.18.clone.mix_ref) | copy-start | bytes 196612
  13.8 23.6 %copy-start.7 = (f32[16,16,16]{2,1,0:T(8,128)S(1)}, f32[16,16,16]{2,1,0:T(8,128)}, u32[]{:S(2)}) copy-start(f32[16,16,16]{2,1,0:T(8,128)} %rate_ref.1) | copy-start | bytes 49156
  13.8 23.6 %copy-start.10 = (s32[2,8]{1,0:T(2,128)S(1)}, s32[2,8]{1,0:T(2,128)}, u32[]{:S(2)}) copy-start(s32[2,8]{1,0:T(2,128)} %count_ref.3) | copy-start | bytes 196
  42.0 8.5 %collective-permute-start.2 = (bf16[24,64,128]{2,1,0:T(8,128)(2,1)S(1)}, bf16[24,64,128]{2,1,0:T(8,128)(2,1)S(1)}, u32[]{:S(2)}, u32[]{:S(2)}) collective-permute-start(bf16[24,64,128]{2,1,0:T(8,128)(2,1)S(1)} %get-tuple-element.19), channel_id=1, source_target_pairs={{0,112},{2,114},{4,116},{6,118},{1,9},{3,11},{5,13},{7,15},{9,1},{... | collective-permute-start | bytes 1179656 | tf_op jit(solution)/shard_map/ppermute | solution.py:549
  43.0 8.6 %collective-permute-start.3 = (bf16[24,64,128]{2,1,0:T(8,128)(2,1)S(1)}, bf16[24,64,128]{2,1,0:T(8,128)(2,1)S(1)}, u32[]{:S(2)}, u32[]{:S(2)}) collective-permute-start(bf16[24,64,128]{2,1,0:T(8,128)(2,1)S(1)} %get-tuple-element.20), channel_id=1, source_target_pairs={{0,2},{2,0},{4,6},{6,4},{1,3},{3,1},{5,7},{7,5},{9,11},{11,9},{13,... | collective-permute-start | bytes 1179656 | tf_op jit(solution)/shard_map/ppermute | solution.py:549
  43.0 9.8 %collective-permute-start.4 = (bf16[24,64,128]{2,1,0:T(8,128)(2,1)S(1)}, bf16[24,64,128]{2,1,0:T(8,128)(2,1)S(1)}, u32[]{:S(2)}, u32[]{:S(2)}) collective-permute-start(bf16[24,64,128]{2,1,0:T(8,128)(2,1)S(1)} %get-tuple-element.21), channel_id=1, source_target_pairs={{0,6},{2,4},{4,2},{6,0},{1,7},{3,5},{5,3},{7,1},{9,15},{11,13},{13... | collective-permute-start | bytes 1179656 | tf_op jit(solution)/shard_map/ppermute | solution.py:549
  44.2 8.6 %collective-permute-start.5 = (bf16[24,64,128]{2,1,0:T(8,128)(2,1)S(1)}, bf16[24,64,128]{2,1,0:T(8,128)(2,1)S(1)}, u32[]{:S(2)}, u32[]{:S(2)}) collective-permute-start(bf16[24,64,128]{2,1,0:T(8,128)(2,1)S(1)} %get-tuple-element.22), channel_id=1, source_target_pairs={{0,1},{2,3},{4,5},{6,7},{1,0},{3,2},{5,4},{7,6},{9,8},{11,10},{13,... | collective-permute-start | bytes 1179656 | tf_op jit(solution)/shard_map/ppermute | solution.py:549
